TPU v7x, 128 devices: a whole 4x4x4 slice. The times are simulated.
128 devices in a mesh: view: 4 (over z_hi, core), rows: 32 (over y, x, z_lo).
Axes of the slice: x: 4, y: 4, z: 4 (z_hi: 2, z_lo: 2; z = z_hi * 2 + z_lo), core: 2. Of those that a mesh axis runs over, the one named last changes fastest.
Arguments:
- features: bfloat16 [12, 12, 256, 256, 128], P('view', None, 'rows'), may hold values from -6 to 6
- analysis_kernel: bfloat16 [5, 5, 128, 128], replicated, may hold values from -0.109375 to 0.109375
- norm_floor: float32 [128], replicated, may hold values from 0.3 to 3
- norm_mixing: float32 [128, 128], replicated, may hold values from 0 to 0.015625
- epipolar_kernel: bfloat16 [3, 3, 3, 128, 128], replicated, may hold values from -0.109375 to 0.109375
- epipolar_bias: float32 [128], replicated, may hold values from -3 to 3
Outputs:
- analysis: bfloat16 [12, 12, 128, 128, 128], P(None, None, ('rows', 'view'))
All inputs are finite; a program needn't handle non-finite values.
Results may differ from a plain program's by a relative error of at most 0.007.
Values may be sent and summed in bfloat16 or wider, within the bound.
No kernel may reach another device: no remote copies, remote signals or barrier semaphores. Data moves between devices by JAX's collectives and lax.ppermute only.
A program may use at most 128 MiB of HBM per device.

v0:
```python
import jax
import jax.numpy as jnp
from jax import lax
from jax.sharding import PartitionSpec as P


def passed_along(value, axis, steps):
    count = lax.axis_size(axis)
    leading, last = (max(0, -steps), min(count, count - steps))
    return lax.ppermute(value, axis, [(source, source + steps) for source in range(leading, last)])


def strided(view_block, kernel, pad_rows):
    return lax.conv_general_dilated(
        view_block,
        kernel,
        (2, 2),
        (pad_rows, (2, 2)),
        dimension_numbers=("NHWC", "HWIO", "NHWC"),
        preferred_element_type=jnp.float32,
    )


def divisive(response, norm_floor, norm_mixing):
    energy = jnp.einsum(
        "...c,cd->...d", response * response, norm_mixing, precision=lax.Precision.HIGHEST
    )
    return (response * lax.rsqrt(norm_floor + energy)).astype(jnp.bfloat16)


def epipolar(row_bands, kernel, bias):
    result = lax.conv_general_dilated(
        row_bands,
        kernel,
        (1, 1, 1),
        ((1, 1), (1, 1), (1, 1)),
        dimension_numbers=("DHNWC", "DHWIO", "DHNWC"),
        preferred_element_type=jnp.float32,
    )
    return (result + bias).astype(jnp.bfloat16)


def shards(features, analysis_kernel, norm_floor, norm_mixing, epipolar_kernel, epipolar_bias):
    stacked = features.reshape((-1,) + features.shape[2:])
    from_above = passed_along(stacked[:, -2:], "rows", 1)
    from_below = passed_along(stacked[:, :1], "rows", -1)
    padded = jnp.concatenate([from_above, stacked, from_below], axis=1)
    responses = strided(padded, analysis_kernel, (0, 0))
    coded_views = divisive(responses, norm_floor, norm_mixing).reshape(
        features.shape[:2] + responses.shape[1:]
    )
    row_bands = lax.all_to_all(coded_views, "view", split_axis=2, concat_axis=0, tiled=True)
    return epipolar(row_bands, epipolar_kernel, epipolar_bias)


def solution(mesh):
    in_specs = (P("view", None, "rows", None, None), P(), P(), P(), P(), P())
    out_specs = P(None, None, ("rows", "view"), None, None)
    return jax.shard_map(shards, mesh=mesh, in_specs=in_specs, out_specs=out_specs, check_vma=False)
```

profile of v0, /device:TPU:121, one launch (start us, length us, event | category | flops | bytes accessed | tf_op | source)
XLA Modules:
  0.0 372.7 jit_solution(15254264940836465597)
XLA Ops:
  0.0 0.0 copy-start
  0.0 2.7 slice.10
  2.7 3.0 collective-permute-start
  5.7 1.9 slice.11
  7.6 2.3 collective-permute-start.1
  10.0 18.2 %copy.33 = bf16[36,8,256,128]{3,0,2,1:T(8,128)(2,1)S(1)} copy(bf16[36,8,256,128]{3,2,1,0:T(8,128)(2,1)} %bitcast.27) | data formatting | bytes 37748736 | tf_op jit(solution)/shard_map/reshape | solution.py:44
  28.1 131.7 %collective-permute-done.1 = bf16[36,1,256,128]{3,2,1,0:T(8,128)(2,1)S(1)} collective-permute-done((bf16[36,1,256,128]{3,2,1,0:T(8,128)(2,1)S(1)}, bf16[36,1,256,128]{3,2,1,0:T(8,128)(2,1)S(1)}, u32[]{:S(2)}, u32[]{:S(2)}) %collective-permute-start.1) | collective-permute-done | bytes 2359328 | tf_op jit(solution)/shard_map/ppermute | solution.py:10
  159.8 3.0 copy.34
  162.9 0.0 collective-permute-done
  162.9 7.8 %copy.32 = bf16[36,2,256,128]{3,0,2,1:T(8,128)(2,1)} copy(bf16[36,2,256,128]{3,2,1,0:T(8,128)(2,1)} %collective-permute-done) | data formatting | bytes 9437184 | tf_op jit(solution)/shard_map/ppermute | solution.py:10
  170.7 0.0 copy-start.1
  170.7 0.0 copy-start.2
  170.7 42.2 %fusion.27 = (f32[36,4,128,128]{3,0,2,1:T(8,128)}, f32[36,4,128,128]{3,0,2,1:T(8,128)}) fusion(bf16[5,5,128,128]{3,2,1,0:T(8,128)(2,1)} %param.7, bf16[36,1,256,128]{3,0,2,1:T(8,128)(2,1)} %copy.34, bf16[36,8,256,128]{3,0,2,1:T(8,128)(2,1)S(1)} %copy.33, bf16[36,2,256,128]{3,0,2,1:T(8,128)(2,1)} %copy.32), kind=kOutput, calls=%fused_computation.26 | convolution fusion | flops 15108931584 | bytes 45645824 | tf_op jit(solution)/shard_map/conv_general_dilated | solution.py:14
  212.9 0.0 copy-done.1
  212.9 0.0 copy-done.2
  212.9 25.4 %fusion.7 = bf16[36,4,128,128]{3,2,1,0:T(8,128)(2,1)S(1)} fusion(f32[36,4,128,128]{3,0,2,1:T(8,128)} %get-tuple-element.6, f32[128]{0:T(128)S(1)} %copy-done.2, f32[36,4,128,128]{3,0,2,1:T(8,128)} %get-tuple-element.5, f32[128,128]{1,0:T(8,128)S(1)} %copy-done.1), kind=kOutput, calls=%fused_computation.10 | convolution fusion | flops 3630956544 | bytes 23659008 | tf_op jit(solution)/shard_map/...c,cd->...d/dot_general | solution.py:25
  238.3 1.8 copy.37
  240.2 56.6 %all_to_all.18 = bf16[3,12,4,128,128]{4,3,1,0,2:T(8,128)(2,1)S(1)} all-to-all(bf16[3,12,4,128,128]{4,3,1,0,2:T(8,128)(2,1)S(1)} %copy.37), channel_id=1, replica_groups=mesh['view'=4,'rows'=32] {'view'}, dimensions={2} | all-to-all | bytes 9437184 | tf_op jit(solution)/shard_map/all_to_all | solution.py:52
  296.8 5.1 %pad = bf16[12,12,1,136,128]{4,3,1,0,2:T(8,128)(2,1)} pad(bf16[12,12,1,128,128]{4,3,1,0,2:T(8,128)(2,1)S(1)} %bitcast.29, bf16[]{:T(256)} %constant.1), padding=0_0x0_0x0_0x1_7x0_0 | pad | bytes 9732098 | tf_op jit(solution)/shard_map/all_to_all | solution.py:52
  301.9 9.4 %reshape.14 = bf16[12,12,1,8,17,128]{5,4,3,1,0,2:T(8,128)(2,1)} reshape(bf16[12,12,1,136,128]{4,3,1,0,2:T(8,128)(2,1)} %pad) | data formatting | bytes 10027008 | tf_op jit(solution)/shard_map/conv_general_dilated | solution.py:32
  311.3 0.0 copy-start.3
  311.3 0.0 copy-start.4
  311.3 4.0 %copy.39 = bf16[12,12,1,8,17,128]{5,3,4,1,0,2:T(8,128)(2,1)S(1)} copy(bf16[12,12,1,8,17,128]{5,4,3,1,0,2:T(8,128)(2,1)} %reshape.14) | data formatting | bytes 10027008 | tf_op jit(solution)/shard_map/conv_general_dilated | solution.py:32
  315.4 0.2 slice.12
  315.5 0.0 copy-done
  315.5 0.0 copy-done.3
  315.6 0.0 copy-done.4
  315.6 35.8 %add_convert_fusion = bf16[12,12,8,17,128]{4,2,3,1,0:T(8,128)(2,1)S(1)} fusion(f32[128]{0:T(128)S(1)} %copy-done.3, pred[8,17]{0,1:T(8,128)(4,1)S(1)} %copy-done.4, bf16[3,3,3,128,128]{4,3,2,1,0:T(8,128)(2,1)S(1)} %copy-done, bf16[12,12,1,7,2,128]{5,3,4,1,0,2:T(8,128)(2,1)S(1)} %slice.12, bf16[12,12,1,8,17,128]{5,3,4,1,0,2:T(8,128)(2,1)S(1)} %copy.39), kind=kOutput, calls=%fused_computation.8 | convolution fusion | flops 15479291904 | bytes 11428488 | tf_op jit(solution)/shard_map/conv_general_dilated | solution.py:32
  351.4 5.1 %copy.40 = bf16[12,12,8,17,128]{4,3,2,1,0:T(8,128)(2,1)} copy(bf16[12,12,8,17,128]{4,2,3,1,0:T(8,128)(2,1)S(1)} %add_convert_fusion) | data formatting | bytes 10027008 | tf_op jit(solution)/shard_map/convert_element_type | solution.py:40
  356.5 9.6 %reshape.18 = bf16[12,12,1,136,128]{4,3,1,0,2:T(8,128)(2,1)} reshape(bf16[12,12,8,17,128]{4,3,2,1,0:T(8,128)(2,1)} %copy.40) | data formatting | bytes 10027008 | tf_op jit(solution)/shard_map/convert_element_type | solution.py:40
  366.1 6.4 %slice_bitcast_fusion = bf16[12,12,1,128,128]{4,3,2,1,0:T(8,128)(2,1)} fusion(bf16[12,12,1,136,128]{4,3,1,0,2:T(8,128)(2,1)} %reshape.18), kind=kLoop, calls=%fused_computation.19 | loop fusion | bytes 9437184 | tf_op jit(solution)/shard_map/convert_element_type | solution.py:40
Async XLA Ops:
  0.0 315.5 %copy-start = (bf16[3,3,3,128,128]{4,3,2,1,0:T(8,128)(2,1)S(1)}, bf16[3,3,3,128,128]{4,3,2,1,0:T(8,128)(2,1)}, u32[]{:S(2)}) copy-start(bf16[3,3,3,128,128]{4,3,2,1,0:T(8,128)(2,1)} %param.10) | copy-start | bytes 2654212
  2.7 160.2 %collective-permute-start = (bf16[36,2,256,128]{3,2,1,0:T(8,128)(2,1)S(1)}, bf16[36,2,256,128]{3,2,1,0:T(8,128)(2,1)}, u32[]{:S(2)}, u32[]{:S(2)}) collective-permute-start(bf16[36,2,256,128]{3,2,1,0:T(8,128)(2,1)S(1)} %slice.10), channel_id=1, source_target_pairs={{0,1},{1,2},{2,3},{3,4},{4,5},{5,6},{6,7},{7,8},{8,9},{9,10},{10,1... | collective-permute-start | bytes 14155784 | tf_op jit(solution)/shard_map/ppermute | solution.py:10
  7.6 152.2 %collective-permute-start.1 = (bf16[36,1,256,128]{3,2,1,0:T(8,128)(2,1)S(1)}, bf16[36,1,256,128]{3,2,1,0:T(8,128)(2,1)S(1)}, u32[]{:S(2)}, u32[]{:S(2)}) collective-permute-start(bf16[36,1,256,128]{3,2,1,0:T(8,128)(2,1)S(1)} %slice.11), channel_id=1, source_target_pairs={{1,0},{2,1},{3,2},{4,3},{5,4},{6,5},{7,6},{8,7},{9,8},{10,9},{11,1... | collective-permute-start | bytes 7077896 | tf_op jit(solution)/shard_map/ppermute | solution.py:10
  170.7 42.2 %copy-start.1 = (f32[128,128]{1,0:T(8,128)S(1)}, f32[128,128]{1,0:T(8,128)}, u32[]{:S(2)}) copy-start(f32[128,128]{1,0:T(8,128)} %param.9) | copy-start | bytes 196612
  170.7 42.2 %copy-start.2 = (f32[128]{0:T(128)S(1)}, f32[128]{0:T(128)}, u32[]{:S(2)}) copy-start(f32[128]{0:T(128)} %param.8) | copy-start | bytes 1540
  311.3 4.2 %copy-start.3 = (f32[128]{0:T(128)S(1)}, f32[128]{0:T(128)}, u32[]{:S(2)}) copy-start(f32[128]{0:T(128)} %param.11) | copy-start | bytes 1540
  311.3 4.2 %copy-start.4 = (pred[8,17]{0,1:T(8,128)(4,1)S(1)}, pred[8,17]{0,1:T(8,128)(4,1)}, u32[]{:S(2)}) copy-start(pred[8,17]{0,1:T(8,128)(4,1)} %constant.5) | copy-start | bytes 412
where the time goes:
time: 379 us; the launch traced here: 373 us
  waiting for transfers between devices  132 us (35%)
  matrix products  103 us (27%)
  local copies, waits for them, and re-layouts  75.2 us (20%)
  blocking collectives  56.6 us (15%)
  starting transfers between devices  5.28 us (1%)
    ppermute x2, waiting for transfers between devices, passed_along(): lax.ppermute(value, axis, [(source, source + steps) for source in range(l...  132 us
    all_to_all x1, blocking collectives, shards(): lax.all_to_all(coded_views, 'view', split_axis=2, concat_axis=0, tiled=True)  56.6 us
    conv_general_dilated x1, matrix products, strided(): lax.conv_general_dilated(view_block, kernel, (2, 2), (pad_rows, (2, 2)),...  42.2 us
    conv_general_dilated x1, matrix products, epipolar(): lax.conv_general_dilated(row_bands, kernel, (1, 1, 1), ((1, 1), (1, 1), (...  35.8 us
    dot_general x1, matrix products, divisive(): jnp.einsum('...c,cd->...d', response * response, norm_mixing, precision=l...  25.4 us
    convert_element_type x3, local copies, waits for them, and re-layouts, epipolar(): return (result + bias).astype(jnp.bfloat16)  21.1 us
    reshape x1, local copies, waits for them, and re-layouts, shards(): stacked = features.reshape((-1,) + features.shape[2:])  18.2 us
    conv_general_dilated x3, local copies, waits for them, and re-layouts, epipolar(): lax.conv_general_dilated(row_bands, kernel, (1, 1, 1), ((1, 1), (1, 1), (...  13.6 us
  transfers between devices with their start and end apart: 2, of which 1 were waited for; matrix products, arithmetic and copies ran while one was open for 6% of the time, Pallas kernels for 0%

commit v1 on v0

v1 whole, which is shorter than its diff:
```python
import functools
import jax, jax.numpy as jnp
from jax import lax
from jax.experimental import pallas as pl
from jax.experimental.pallas import tpu as pltpu
from jax.sharding import PartitionSpec as P

bf16, f32 = jnp.bfloat16, jnp.float32

def shifted_sum(before, here, after, cols):
    rows = before.shape[0]
    place = lax.broadcasted_iota(jnp.int32, before.shape, 0) % cols
    down = jnp.where(place == 0, 0.0, pltpu.roll(before, 1, 0))
    up = jnp.where(place == cols - 1, 0.0, pltpu.roll(after, rows - 1, 0))
    return down + here + up

def conv_kernel(view_ref, x_ref, wm_ref, we_ref, own_ref, oth_ref, h1_ref, h2_ref, wide, ev, od):
    g, rows, wid, c = x_ref.shape[0], x_ref.shape[2], x_ref.shape[3], x_ref.shape[4]
    n = wid // 2
    m = g * n
    for v in range(g):
      for i in range(rows):
        wide[...] = x_ref[v, 0, i].astype(f32)
        ev[v, i] = wide[pl.ds(0, n, 2), :].astype(bf16)
        od[v, i] = wide[pl.ds(1, n, 2), :].astype(bf16)
    first = view_ref[0] < 2
    def block(ref, i):
        return ref[:, i].reshape(m, c)
    def main(lo, hi, a):
        lhs = jnp.concatenate([block(ref, i) for i in range(lo, hi) for ref in (ev, od)], axis=1)
        return jnp.dot(lhs, wm_ref[a * 2 * c:(a + hi - lo) * 2 * c, :], preferred_element_type=f32)
    def extra(lo, hi, a):
        lhs = jnp.concatenate([block(ev, i) for i in range(lo, hi)], axis=1)
        return jnp.dot(lhs, we_ref[a * c:(a + hi - lo) * c, :], preferred_element_type=f32)
    def row(mn, ex):
        return shifted_sum(mn[:, :c], mn[:, c:], ex, n).astype(bf16).reshape(g, n, c)
    pair = extra(0, 3, 4)
    up = row(main(0, 1, 4), pair[:, :c])
    r0 = row(main(0, 3, 2), pair[:, c:])
    pair = extra(4, 8, 0)
    r3 = row(main(4, 8, 0), pair[:, :c])
    dn = row(main(6, 8, 0), pair[:, c:])
    h1_ref[:, 0] = jnp.where(first, dn, up)
    h2_ref[:, 0] = jnp.where(first, up, dn)
    pair = extra(0, 7, 0)
    r1 = row(main(0, 5, 0), pair[:, :c])
    r2 = row(main(2, 7, 0), pair[:, c:])
    own_ref[0, :, 0] = jnp.where(first, r0, r2)
    own_ref[1, :, 0] = jnp.where(first, r1, r3)
    oth_ref[0, :, 0] = jnp.where(first, r2, r0)
    oth_ref[1, :, 0] = jnp.where(first, r3, r1)

def conv_weights(k):
    c = k.shape[2]
    main = jnp.stack([jnp.concatenate([k[:, 0], k[:, 2]], -1), jnp.concatenate([k[:, 1], k[:, 3]], -1)], 1)
    z = jnp.zeros((2,) + k.shape[2:], k.dtype)
    last = jnp.concatenate([jnp.concatenate([k[:, 4], z], 0), jnp.concatenate([z, k[:, 4]], 0)], -1)
    return main.reshape(-1, 2 * c), last.reshape(-1, 2 * c)

def conv_chunk(view, features, wm, we, lo, cv):
    U, V, H, W, C = features.shape
    n = W // 2
    spec = lambda lead: pl.BlockSpec(lead + (U, 1, n, C), lambda t, s: (0,) * len(lead) + (0, t, 0, 0))
    shp = lambda lead: jax.ShapeDtypeStruct(lead + (U, cv, n, C), bf16)
    full = lambda a: pl.BlockSpec(a.shape, lambda t, s: (0,) * a.ndim)
    return pl.pallas_call(
        conv_kernel,
        grid_spec=pltpu.PrefetchScalarGridSpec(
            num_scalar_prefetch=1, grid=(cv,),
            in_specs=[pl.BlockSpec((U, 1, H, W, C), lambda t, s: (0, lo + t, 0, 0, 0)), full(wm), full(we)],
            out_specs=[spec((2,)), spec((2,)), spec(()), spec(())],
            scratch_shapes=[pltpu.VMEM((W, C), f32), pltpu.VMEM((U, H, n, C), bf16), pltpu.VMEM((U, H, n, C), bf16)],
        ),
        out_shape=[shp((2,)), shp((2,)), shp(()), shp(())],
        compiler_params=pltpu.CompilerParams(vmem_limit_bytes=48 * 2**20),
        cost_estimate=pl.CostEstimate(flops=2 * cv * U * 4 * n * 25 * C * C, bytes_accessed=cv * U * (H * W + 6 * n) * C * 2, transcendentals=0),
        name="conv",
    )(view, features, wm, we)
def norm_kernel(place_ref, own_ref, oth_ref, h1_ref, h2_ref, floor_ref, mix_ref, mine_ref, give_ref):
    first = place_ref[0] < 2
    upper = place_ref[0] % 2 == 0
    g, n, c = h1_ref.shape[0], h1_ref.shape[2], h1_ref.shape[3]
    mix = mix_ref[...].astype(bf16)
    for j, (raw_ref, part_ref) in enumerate(((own_ref, h1_ref), (oth_ref, h2_ref))):
        part = part_ref[:, 0].reshape(g * n, c).astype(f32)
        coded = []
        for r in range(2):
            x = raw_ref[r, :, 0].reshape(g * n, c).astype(f32)
            x = x + jnp.where(first == (r == 0), part, 0.0)
            energy = jnp.dot((x * x).astype(bf16), mix, preferred_element_type=f32)
            coded.append((x * lax.rsqrt(floor_ref[...] + energy)).astype(bf16).reshape(g, n, c))
        mine_ref[j, :, 0] = jnp.where(upper, coded[0], coded[1])
        give_ref[j, :, 0] = jnp.where(upper, coded[1], coded[0])

def norm_chunk(place, own, oth, h1, h2, floor, mix):
    _, U, cv, n, C = own.shape
    spec = lambda lead: pl.BlockSpec(lead + (U, 1, n, C), lambda t, s: (0,) * len(lead) + (0, t, 0, 0))
    full = lambda a: pl.BlockSpec(a.shape, lambda t, s: (0,) * a.ndim)
    return pl.pallas_call(
        norm_kernel,
        grid_spec=pltpu.PrefetchScalarGridSpec(
            num_scalar_prefetch=1, grid=(cv,),
            in_specs=[spec((2,)), spec((2,)), spec(()), spec(()), full(floor), full(mix)],
            out_specs=[spec((2,)), spec((2,))],
        ),
        out_shape=[jax.ShapeDtypeStruct((2, U, cv, n, C), bf16)] * 2,
        compiler_params=pltpu.CompilerParams(vmem_limit_bytes=40 * 2**20),
        cost_estimate=pl.CostEstimate(flops=8 * cv * U * n * C * C, bytes_accessed=cv * U * 10 * n * C * 2, transcendentals=4 * cv * U * n * C),
        name="norm",
    )(place, own, oth, h1, h2, floor, mix)

def epi_kernel(pieces, v0, v1, has_prev, place_ref, *refs):
    k = len(pieces)
    srcs = refs[:2 * k]
    wm_ref, we_ref, bias_ref = refs[2 * k:2 * k + 3]
    rest = refs[2 * k + 3 + has_prev:]
    out_ref, cod, obuf, sem_in, sem_out = rest
    U = srcs[0].shape[1]
    n, c = cod.shape[2], cod.shape[3]
    V = out_ref.shape[1]
    total = out_ref.shape[0]
    nv = v1 - v0
    copies = []
    for p, (s0, s1, d0) in enumerate(pieces):
        for j, flip in enumerate((0, 2, 1, 3)):
            src = srcs[2 * p + j // 2]
            blk = place_ref[1 + j]
            cp = pltpu.make_async_copy(src.at[j % 2, :, s0:s1], cod.at[pl.ds(1 + U * blk, U), d0:d0 + s1 - s0], sem_in.at[4 * p + j])
            cp.start()
            copies.append(cp)
    edge = jnp.zeros((nv + 2, n, c), bf16)
    cod[0] = edge
    cod[total + 1] = edge
    if v0 == 0:
        cod[:, 0] = jnp.zeros((total + 2, n, c), bf16)
    if v1 == V:
        cod[:, nv + 1] = jnp.zeros((total + 2, n, c), bf16)
    for cp in copies:
        cp.wait()
    m = nv * n
    steps = total // 2
    def out_copy(t, slot):
        return pltpu.make_async_copy(obuf.at[slot], out_ref.at[pl.ds(2 * t, 2), v0:v1, 0], sem_out.at[slot])
    def step(t, carry):
        slot = lax.rem(t, 2)
        @pl.when(t >= 2)
        def _():
            out_copy(t - 2, slot).wait()
        def block(i, j):
            return cod[2 * t + i, j:j + nv].reshape(m, c)
        blocks = [[block(i, j) for j in range(3)] for i in range(4)]
        ex = jnp.dot(jnp.concatenate(sum(blocks, []), axis=1), we_ref[...], preferred_element_type=f32)
        for h in range(2):
            mn = jnp.dot(jnp.concatenate(sum(blocks[h:h + 3], []), axis=1), wm_ref[...], preferred_element_type=f32)
            res = shifted_sum(mn[:, :c], mn[:, c:], ex[:, h * c:(h + 1) * c], n) + bias_ref[...]
            obuf[slot, h] = res.astype(bf16).reshape(nv, n, c)
        out_copy(t, slot).start()
        return carry
    lax.fori_loop(0, steps, step, 0)
    for t in (steps - 2, steps - 1):
        out_copy(t, t % 2).wait()

def epi_weights(k):
    c = k.shape[3]
    main = jnp.concatenate([k[:, :, 0], k[:, :, 1]], -1).reshape(-1, 2 * c)
    z = jnp.zeros((1,) + k.shape[1:2] + k.shape[3:], k.dtype)
    last = jnp.concatenate([jnp.concatenate([k[:, :, 2], z], 0), jnp.concatenate([z, k[:, :, 2]], 0)], -1)
    return main, last.reshape(-1, 2 * c)

def epi_chunk(place, sources, spans, v0, v1, prev, wm, we, bias, total, V):
    used, pieces = [], []
    for (mine, flipped), (lo, hi) in zip(sources, spans):
        a, b = max(lo, v0 - 1), min(hi, v1 + 1)
        if a < b:
            used += [mine, flipped]
            pieces.append((a - lo, b - lo, a - (v0 - 1)))
    _, U, _, n, C = used[0].shape
    anyspec = pl.BlockSpec(memory_space=pl.ANY)
    full = lambda a: pl.BlockSpec(a.shape, lambda t, s: (0,) * a.ndim)
    nv = v1 - v0
    args = [place] + used + [wm, we, bias] + ([prev] if prev is not None else [])
    return pl.pallas_call(
        functools.partial(epi_kernel, tuple(pieces), v0, v1, int(prev is not None)),
        grid_spec=pltpu.PrefetchScalarGridSpec(
            num_scalar_prefetch=1, grid=(1,),
            in_specs=[anyspec] * len(used) + [full(wm), full(we), full(bias)] + [anyspec] * (prev is not None),
            out_specs=anyspec,
            scratch_shapes=[
                pltpu.VMEM((total + 2, nv + 2, n, C), bf16),
                pltpu.VMEM((2, 2, nv, n, C), bf16),
                pltpu.SemaphoreType.DMA((4 * len(pieces),)),
                pltpu.SemaphoreType.DMA((2,)),
            ],
        ),
        out_shape=jax.ShapeDtypeStruct((total, V, 1, n, C), bf16),
        input_output_aliases={len(args) - 1: 0} if prev is not None else {},
        compiler_params=pltpu.CompilerParams(vmem_limit_bytes=48 * 2**20),
        cost_estimate=pl.CostEstimate(flops=2 * total * nv * n * 27 * C * C, bytes_accessed=total * (2 * nv + 2) * n * C * 2, transcendentals=0),
        name="epi",
    )(*args)
CHUNKS = ((0, 6), (6, 12))

def shards(features, analysis_kernel, norm_floor, norm_mixing, epipolar_kernel, epipolar_bias):
    U, V = features.shape[:2]
    views, bands = lax.axis_size("view"), lax.axis_size("rows")
    total = U * views
    w = lax.axis_index("view")
    place = jnp.stack([w, w, w ^ 2, w ^ 1, w ^ 3]).astype(jnp.int32)
    wm, we = conv_weights(analysis_kernel)
    em, ee = epi_weights(epipolar_kernel)
    floor, bias = norm_floor[None], epipolar_bias[None]
    both = ("view", "rows")
    swap = [(v * bands + r, (v ^ 2) * bands + r) for v in range(views) for r in range(bands)]
    def hop(flip):
        pairs = []
        for v in range(views):
            step = 1 if (v < 2) != (flip > 0) else -1
            pairs += [(v * bands + r, (v ^ flip) * bands + r + step) for r in range(bands) if 0 <= r + step < bands]
        return pairs
    core = [(v, v ^ 1) for v in range(views)]
    sources = []
    out = None
    done = 0
    for i, (lo, hi) in enumerate(CHUNKS):
        own, oth, h1, h2 = conv_chunk(place, features, wm, we, lo, hi - lo)
        h1 = lax.ppermute(h1, both, hop(0))
        h2 = lax.ppermute(h2, both, hop(2))
        oth = lax.ppermute(oth, both, swap)
        mine, give = norm_chunk(place, own, oth, h1, h2, floor, norm_mixing)
        flipped = lax.ppermute(give, "view", core)
        sources.append((mine, flipped))
        upto = V if hi == V else hi - 1
        out = epi_chunk(place, sources, CHUNKS[:i + 1], done, upto, out, em, ee, bias, total, V)
        done = upto
    return out


def solution(mesh):
    in_specs = (P("view", None, "rows", None, None), P(), P(), P(), P(), P())
    out_specs = P(None, None, ("rows", "view"), None, None)
    return jax.shard_map(shards, mesh=mesh, in_specs=in_specs, out_specs=out_specs, check_vma=False)
```

time: 379 us -> 143 us (0.38)
  the two profiles are of different devices: /device:TPU:121 before, /device:TPU:25 now
where the time goes in v1:
time: 143 us
  Pallas kernels  59.4 us (42%)
  waiting for transfers between devices  59.1 us (41%)
  starting transfers between devices  22.2 us (16%)
  local copies, waits for them, and re-layouts  2.03 us (1%)
    ppermute x2, waiting for transfers between devices, shards(): oth = lax.ppermute(oth, both, swap)  48.1 us
    pallas_call x2, Pallas kernels, conv_chunk(): pl.pallas_call(conv_kernel, grid_spec=pltpu.PrefetchScalarGridSpec(num_sc...  28.2 us
    pallas_call x2, Pallas kernels, epi_chunk(): pl.pallas_call(functools.partial(epi_kernel, tuple(pieces), v0, v1, int(p...  25.6 us
    ppermute x2, starting transfers between devices, shards(): h2 = lax.ppermute(h2, both, hop(2))  8.77 us
    ppermute x2, waiting for transfers between devices, shards(): h2 = lax.ppermute(h2, both, hop(2))  8.25 us
    ppermute x2, starting transfers between devices, shards(): h1 = lax.ppermute(h1, both, hop(0))  6.19 us
    ppermute x2, starting transfers between devices, shards(): oth = lax.ppermute(oth, both, swap)  5.85 us
    pallas_call x2, Pallas kernels, norm_chunk(): pl.pallas_call(norm_kernel, grid_spec=pltpu.PrefetchScalarGridSpec(num_sc...  5.6 us
  transfers between devices with their start and end apart: 8, of which 4 were waited for; matrix products, arithmetic and copies ran while one was open for 0% of the time, Pallas kernels for 21%

profile of v1, /device:TPU:25, one launch (start us, length us, event | category | flops | bytes accessed | tf_op | source)
XLA Modules:
  0.0 143.2 jit_solution(9345789517070424452)
XLA Ops:
  0.0 1.3 slice_bitcast_fusion.1
  1.4 0.1 maximum_bitcast_fusion
  1.5 0.1 pad_maximum_fusion
  1.6 0.1 stack.29.view_ref.place_ref
  1.7 14.1 %conv.2 = (bf16[2,3,6,128,128]{4,3,2,1,0:T(8,128)(2,1)S(1)}, bf16[2,3,6,128,128]{4,3,2,1,0:T(8,128)(2,1)S(1)}, bf16[3,6,128,128]{3,2,1,0:T(8,128)(2,1)S(1)}, bf16[3,6,128,128]{3,2,1,0:T(8,128)(2,1)S(1)}) custom-call(s32[5]{0:T(128)S(1)} %stack.29.view_ref.place_ref, bf16[3,12,8,256,128]{4,3,2,1,0:T(8,128)(2,1)} %x_ref.3, bf16[1280,256]{1,0:T(8,128)(2,1)S(1)} %bitcast.35, ...), custom_call_target="tpu_custom_call" | custom-call | flops 7549747200 | bytes 12976128 | tf_op jit(solution)/shard_map/conv/pallas_call | solution.py:66
  15.8 3.5 %collective-permute-start.1 = (bf16[3,6,128,128]{3,2,1,0:T(8,128)(2,1)S(1)}, bf16[3,6,128,128]{3,2,1,0:T(8,128)(2,1)S(1)}, u32[]{:S(2)}, u32[]{:S(2)}) collective-permute-start(bf16[3,6,128,128]{3,2,1,0:T(8,128)(2,1)S(1)} %get-tuple-element.19), channel_id=1, source_target_pairs={{0,1},{1,2},{2,3},{3,4},{4,5},{5,6},{6,7},{7,8},{8,9},{9,10},{10,1... | collective-permute-start | bytes 1769480 | tf_op jit(solution)/shard_map/ppermute | solution.py:226
  19.3 0.0 copy-start
  19.3 0.0 copy-start.1
  19.3 5.8 %collective-permute-start = (bf16[2,3,6,128,128]{4,3,2,1,0:T(8,128)(2,1)S(1)}, bf16[2,3,6,128,128]{4,3,2,1,0:T(8,128)(2,1)S(1)}, u32[]{:S(2)}, u32[]{:S(2)}) collective-permute-start(bf16[2,3,6,128,128]{4,3,2,1,0:T(8,128)(2,1)S(1)} %get-tuple-element.18), channel_id=1, source_target_pairs={{0,64},{1,65},{2,66},{3,67},{4,68},{5,69},{6,70},{7,71},{8,72},{9,... | collective-permute-start | bytes 3538952 | tf_op jit(solution)/shard_map/ppermute | solution.py:228
  25.1 14.1 %conv.3 = (bf16[2,3,6,128,128]{4,3,2,1,0:T(8,128)(2,1)S(1)}, bf16[2,3,6,128,128]{4,3,2,1,0:T(8,128)(2,1)S(1)}, bf16[3,6,128,128]{3,2,1,0:T(8,128)(2,1)S(1)}, bf16[3,6,128,128]{3,2,1,0:T(8,128)(2,1)S(1)}) custom-call(s32[5]{0:T(128)S(1)} %stack.29.view_ref.place_ref, bf16[3,12,8,256,128]{4,3,2,1,0:T(8,128)(2,1)} %x_ref.3, bf16[1280,256]{1,0:T(8,128)(2,1)S(1)} %bitcast.36, ...), custom_call_target="tpu_custom_call" | custom-call | flops 7549747200 | bytes 12976128 | tf_op jit(solution)/shard_map/conv/pallas_call | solution.py:66
  39.2 0.1 collective-permute-start.4
  39.3 3.8 %collective-permute-start.2 = (bf16[3,6,128,128]{3,2,1,0:T(8,128)(2,1)S(1)}, bf16[3,6,128,128]{3,2,1,0:T(8,128)(2,1)S(1)}, u32[]{:S(2)}, u32[]{:S(2)}) collective-permute-start(bf16[3,6,128,128]{3,2,1,0:T(8,128)(2,1)S(1)} %get-tuple-element.20), channel_id=1, source_target_pairs={{1,64},{2,65},{3,66},{4,67},{5,68},{6,69},{7,70},{8,71},{9,72},{10... | collective-permute-start | bytes 1769480 | tf_op jit(solution)/shard_map/ppermute | solution.py:227
  43.1 2.6 %collective-permute-start.5 = (bf16[3,6,128,128]{3,2,1,0:T(8,128)(2,1)S(1)}, bf16[3,6,128,128]{3,2,1,0:T(8,128)(2,1)S(1)}, u32[]{:S(2)}, u32[]{:S(2)}) collective-permute-start(bf16[3,6,128,128]{3,2,1,0:T(8,128)(2,1)S(1)} %get-tuple-element.25), channel_id=1, source_target_pairs={{0,1},{1,2},{2,3},{3,4},{4,5},{5,6},{6,7},{7,8},{8,9},{9,10},{10,1... | collective-permute-start | bytes 1769480 | tf_op jit(solution)/shard_map/ppermute | solution.py:226
  45.8 0.0 collective-permute-done.1.h1_ref
  45.8 5.0 %collective-permute-start.6 = (bf16[3,6,128,128]{3,2,1,0:T(8,128)(2,1)S(1)}, bf16[3,6,128,128]{3,2,1,0:T(8,128)(2,1)S(1)}, u32[]{:S(2)}, u32[]{:S(2)}) collective-permute-start(bf16[3,6,128,128]{3,2,1,0:T(8,128)(2,1)S(1)} %get-tuple-element.26), channel_id=1, source_target_pairs={{1,64},{2,65},{3,66},{4,67},{5,68},{6,69},{7,70},{8,71},{9,72},{10... | collective-permute-start | bytes 1769480 | tf_op jit(solution)/shard_map/ppermute | solution.py:227
  50.8 8.2 %collective-permute-done.2.h2_ref = bf16[3,6,128,128]{3,2,1,0:T(8,128)(2,1)S(1)} collective-permute-done((bf16[3,6,128,128]{3,2,1,0:T(8,128)(2,1)S(1)}, bf16[3,6,128,128]{3,2,1,0:T(8,128)(2,1)S(1)}, u32[]{:S(2)}, u32[]{:S(2)}) %collective-permute-start.2) | collective-permute-done | bytes 589856 | tf_op jit(solution)/shard_map/ppermute | solution.py:227
  59.0 29.2 %collective-permute-done.oth_ref = bf16[2,3,6,128,128]{4,3,2,1,0:T(8,128)(2,1)S(1)} collective-permute-done((bf16[2,3,6,128,128]{4,3,2,1,0:T(8,128)(2,1)S(1)}, bf16[2,3,6,128,128]{4,3,2,1,0:T(8,128)(2,1)S(1)}, u32[]{:S(2)}, u32[]{:S(2)}) %collective-permute-start) | collective-permute-done | bytes 1179680 | tf_op jit(solution)/shard_map/ppermute | solution.py:228
  88.2 0.0 copy-done
  88.2 0.0 copy-done.1
  88.2 2.8 %norm.2 = (bf16[2,3,6,128,128]{4,3,2,1,0:T(8,128)(2,1)S(1)}, bf16[2,3,6,128,128]{4,3,2,1,0:T(8,128)(2,1)S(1)}) custom-call(s32[5]{0:T(128)S(1)} %stack.29.view_ref.place_ref, bf16[2,3,6,128,128]{4,3,2,1,0:T(8,128)(2,1)S(1)} %get-tuple-element.17.own_ref, bf16[2,3,6,128,128]{4,3,2,1,0:T(8,128)(2,1)S(1)} %collective-permute-done.oth_ref, ...), custom_call_target="tpu_custom_call" | custom-call | flops 301989888 | bytes 5898240 | tf_op jit(solution)/shard_map/norm/pallas_call | solution.py:99
  91.0 0.7 collective-permute-start.3
  91.7 2.8 %collective-permute-done.5.h1_ref = bf16[3,6,128,128]{3,2,1,0:T(8,128)(2,1)S(1)} collective-permute-done((bf16[3,6,128,128]{3,2,1,0:T(8,128)(2,1)S(1)}, bf16[3,6,128,128]{3,2,1,0:T(8,128)(2,1)S(1)}, u32[]{:S(2)}, u32[]{:S(2)}) %collective-permute-start.5) | collective-permute-done | bytes 589856 | tf_op jit(solution)/shard_map/ppermute | solution.py:226
  94.5 0.0 collective-permute-done.6.h2_ref
  94.5 18.9 %collective-permute-done.4.oth_ref = bf16[2,3,6,128,128]{4,3,2,1,0:T(8,128)(2,1)S(1)} collective-permute-done((bf16[2,3,6,128,128]{4,3,2,1,0:T(8,128)(2,1)S(1)}, bf16[2,3,6,128,128]{4,3,2,1,0:T(8,128)(2,1)S(1)}, u32[]{:S(2)}, u32[]{:S(2)}) %collective-permute-start.4) | collective-permute-done | bytes 1179680 | tf_op jit(solution)/shard_map/ppermute | solution.py:228
  113.4 0.0 copy-start.3
  113.4 2.8 %norm.3 = (bf16[2,3,6,128,128]{4,3,2,1,0:T(8,128)(2,1)S(1)}, bf16[2,3,6,128,128]{4,3,2,1,0:T(8,128)(2,1)S(1)}) custom-call(s32[5]{0:T(128)S(1)} %stack.29.view_ref.place_ref, bf16[2,3,6,128,128]{4,3,2,1,0:T(8,128)(2,1)S(1)} %get-tuple-element.23.own_ref, bf16[2,3,6,128,128]{4,3,2,1,0:T(8,128)(2,1)S(1)} %collective-permute-done.4.oth_ref, ...), custom_call_target="tpu_custom_call" | custom-call | flops 301989888 | bytes 5898240 | tf_op jit(solution)/shard_map/norm/pallas_call | solution.py:99
  116.3 0.6 collective-permute-start.7
  116.9 0.0 copy-done.3
  116.9 0.1 slice_bitcast_fusion
  117.0 0.0 copy-start.2
  117.0 0.1 fusion.4
  117.1 0.1 pad_maximum_fusion.1.refs_2_.refs_4_
  117.1 0.0 collective-permute-done.3.refs_1_
  117.2 0.5 copy-done.2
  117.6 10.9 %epi.2.refs_7_ = bf16[12,12,1,128,128]{4,3,2,1,0:T(8,128)(2,1)} custom-call(s32[5]{0:T(128)S(1)} %stack.29.view_ref.place_ref, bf16[2,3,6,128,128]{4,3,2,1,0:T(8,128)(2,1)S(1)} %get-tuple-element.21.refs_0_, bf16[2,3,6,128,128]{4,3,2,1,0:T(8,128)(2,1)S(1)} %collective-permute-done.3.refs_1_, bf16[1152,256]{1,0:T(8,128)(2,1)S(1)} %pad_maximum_fusion.1.refs_2_.refs_4_, ...), custom_call_target="tpu_custom_call" | custom-call | flops 6794772480 | bytes 4718592 | tf_op jit(solution)/shard_map/epi/pallas_call | solution.py:182
  128.6 0.0 collective-permute-done.7.refs_3_
  128.6 14.6 %epi.3 = bf16[12,12,1,128,128]{4,3,2,1,0:T(8,128)(2,1)} custom-call(s32[5]{0:T(128)S(1)} %stack.29.view_ref.place_ref, bf16[2,3,6,128,128]{4,3,2,1,0:T(8,128)(2,1)S(1)} %get-tuple-element.21.refs_0_, bf16[2,3,6,128,128]{4,3,2,1,0:T(8,128)(2,1)S(1)} %collective-permute-done.3.refs_1_, ...), custom_call_target="tpu_custom_call", output_to_operand_aliasing={{}: (8, {})} | custom-call | flops 9512681472 | bytes 6291456 | tf_op jit(solution)/shard_map/epi/pallas_call | solution.py:182
  (2 shorter events, 0.1 us)
Async XLA Ops:
  15.8 30.0 %collective-permute-start.1 = (bf16[3,6,128,128]{3,2,1,0:T(8,128)(2,1)S(1)}, bf16[3,6,128,128]{3,2,1,0:T(8,128)(2,1)S(1)}, u32[]{:S(2)}, u32[]{:S(2)}) collective-permute-start(bf16[3,6,128,128]{3,2,1,0:T(8,128)(2,1)S(1)} %get-tuple-element.19), channel_id=1, source_target_pairs={{0,1},{1,2},{2,3},{3,4},{4,5},{5,6},{6,7},{7,8},{8,9},{9,10},{10,1... | collective-permute-start | bytes 1769480 | tf_op jit(solution)/shard_map/ppermute | solution.py:226
  19.3 68.9 %copy-start = (f32[128,128]{1,0:T(8,128)S(1)}, f32[128,128]{1,0:T(8,128)}, u32[]{:S(2)}) copy-start(f32[128,128]{1,0:T(8,128)} %mix_ref.3) | copy-start | bytes 196612
  19.3 68.8 %copy-start.1 = (f32[128]{0:T(128)S(1)}, f32[128]{0:T(128)}, u32[]{:S(2)}) copy-start(f32[128]{0:T(128)} %param.8) | copy-start | bytes 1540
  19.3 68.8 %collective-permute-start = (bf16[2,3,6,128,128]{4,3,2,1,0:T(8,128)(2,1)S(1)}, bf16[2,3,6,128,128]{4,3,2,1,0:T(8,128)(2,1)S(1)}, u32[]{:S(2)}, u32[]{:S(2)}) collective-permute-start(bf16[2,3,6,128,128]{4,3,2,1,0:T(8,128)(2,1)S(1)} %get-tuple-element.18), channel_id=1, source_target_pairs={{0,64},{1,65},{2,66},{3,67},{4,68},{5,69},{6,70},{7,71},{8,72},{9,... | collective-permute-start | bytes 3538952 | tf_op jit(solution)/shard_map/ppermute | solution.py:228
  39.2 74.2 %collective-permute-start.4 = (bf16[2,3,6,128,128]{4,3,2,1,0:T(8,128)(2,1)S(1)}, bf16[2,3,6,128,128]{4,3,2,1,0:T(8,128)(2,1)S(1)}, u32[]{:S(2)}, u32[]{:S(2)}) collective-permute-start(bf16[2,3,6,128,128]{4,3,2,1,0:T(8,128)(2,1)S(1)} %get-tuple-element.24), channel_id=1, source_target_pairs={{0,64},{1,65},{2,66},{3,67},{4,68},{5,69},{6,70},{7,71},{8,72},{9,... | collective-permute-start | bytes 3538952 | tf_op jit(solution)/shard_map/ppermute | solution.py:228
  39.3 19.7 %collective-permute-start.2 = (bf16[3,6,128,128]{3,2,1,0:T(8,128)(2,1)S(1)}, bf16[3,6,128,128]{3,2,1,0:T(8,128)(2,1)S(1)}, u32[]{:S(2)}, u32[]{:S(2)}) collective-permute-start(bf16[3,6,128,128]{3,2,1,0:T(8,128)(2,1)S(1)} %get-tuple-element.20), channel_id=1, source_target_pairs={{1,64},{2,65},{3,66},{4,67},{5,68},{6,69},{7,70},{8,71},{9,72},{10... | collective-permute-start | bytes 1769480 | tf_op jit(solution)/shard_map/ppermute | solution.py:227
  43.1 51.4 %collective-permute-start.5 = (bf16[3,6,128,128]{3,2,1,0:T(8,128)(2,1)S(1)}, bf16[3,6,128,128]{3,2,1,0:T(8,128)(2,1)S(1)}, u32[]{:S(2)}, u32[]{:S(2)}) collective-permute-start(bf16[3,6,128,128]{3,2,1,0:T(8,128)(2,1)S(1)} %get-tuple-element.25), channel_id=1, source_target_pairs={{0,1},{1,2},{2,3},{3,4},{4,5},{5,6},{6,7},{7,8},{8,9},{9,10},{10,1... | collective-permute-start | bytes 1769480 | tf_op jit(solution)/shard_map/ppermute | solution.py:226
  45.8 48.8 %collective-permute-start.6 = (bf16[3,6,128,128]{3,2,1,0:T(8,128)(2,1)S(1)}, bf16[3,6,128,128]{3,2,1,0:T(8,128)(2,1)S(1)}, u32[]{:S(2)}, u32[]{:S(2)}) collective-permute-start(bf16[3,6,128,128]{3,2,1,0:T(8,128)(2,1)S(1)} %get-tuple-element.26), channel_id=1, source_target_pairs={{1,64},{2,65},{3,66},{4,67},{5,68},{6,69},{7,70},{8,71},{9,72},{10... | collective-permute-start | bytes 1769480 | tf_op jit(solution)/shard_map/ppermute | solution.py:227
  91.0 26.2 %collective-permute-start.3 = (bf16[2,3,6,128,128]{4,3,2,1,0:T(8,128)(2,1)S(1)}, bf16[2,3,6,128,128]{4,3,2,1,0:T(8,128)(2,1)S(1)}, u32[]{:S(2)}, u32[]{:S(2)}) collective-permute-start(bf16[2,3,6,128,128]{4,3,2,1,0:T(8,128)(2,1)S(1)} %get-tuple-element.22), channel_id=1, source_target_pairs={{0,32},{32,0},{64,96},{96,64},{1,33},{33,1},{65,97},{97,65},{2,34}... | collective-permute-start | bytes 3538952 | tf_op jit(solution)/shard_map/ppermute | solution.py:230
  113.4 3.4 %copy-start.3 = (bf16[3,3,3,128,128]{4,3,2,1,0:T(8,128)(2,1)S(1)}, bf16[3,3,3,128,128]{4,3,2,1,0:T(8,128)(2,1)}, u32[]{:S(2)}) copy-start(bf16[3,3,3,128,128]{4,3,2,1,0:T(8,128)(2,1)} %param.10) | copy-start | bytes 2654212
  116.3 12.3 %collective-permute-start.7 = (bf16[2,3,6,128,128]{4,3,2,1,0:T(8,128)(2,1)S(1)}, bf16[2,3,6,128,128]{4,3,2,1,0:T(8,128)(2,1)S(1)}, u32[]{:S(2)}, u32[]{:S(2)}) collective-permute-start(bf16[2,3,6,128,128]{4,3,2,1,0:T(8,128)(2,1)S(1)} %get-tuple-element.28), channel_id=1, source_target_pairs={{0,32},{32,0},{64,96},{96,64},{1,33},{33,1},{65,97},{97,65},{2,34}... | collective-permute-start | bytes 3538952 | tf_op jit(solution)/shard_map/ppermute | solution.py:230
  117.0 0.7 copy-start.2

commit v2 on v1

v2 whole, which is shorter than its diff:
```python
import functools
import jax, jax.numpy as jnp
from jax import lax
from jax.experimental import pallas as pl
from jax.experimental.pallas import tpu as pltpu
from jax.sharding import PartitionSpec as P

bf16, f32 = jnp.bfloat16, jnp.float32

SMALL = pl.CostEstimate(flops=1000, bytes_accessed=1000, transcendentals=0)


def shifted_sum(before, here, after, cols):
    rows = before.shape[0]
    place = lax.broadcasted_iota(jnp.int32, before.shape, 0) % cols
    down = jnp.where(place == 0, 0.0, pltpu.roll(before, 1, 0))
    up = jnp.where(place == cols - 1, 0.0, pltpu.roll(after, rows - 1, 0))
    return down + here + up

def split_columns(x_ref, v, i, wide, ev, od, at):
    n = wide.shape[0] // 2
    wide[...] = x_ref[v, 0, i].astype(f32)
    ev[v, at] = wide[pl.ds(0, n, 2), :].astype(bf16)
    od[v, at] = wide[pl.ds(1, n, 2), :].astype(bf16)


def main_weights(k_ref, wm_ref):
    c = k_ref.shape[2]
    for a in range(5):
        for p in range(2):
            for s in range(2):
                wm_ref[(2 * a + p) * c:(2 * a + p + 1) * c, s * c:(s + 1) * c] = k_ref[a, 2 * s + p]


def side_blocks(refs, blocks, m):
    return jnp.concatenate([refs[p][:, i].reshape(m, -1) for p, i in blocks], axis=1)


def halo_kernel(view_ref, top_ref, bottom_ref, k_ref, h1_ref, h2_ref, wide, ev, od, wm_ref, we_ref):
    g, wid, c = top_ref.shape[0], top_ref.shape[3], top_ref.shape[4]
    n = wid // 2
    m = g * n

    @pl.when(pl.program_id(0) == 0)
    def _():
        main_weights(k_ref, wm_ref)
        z = jnp.zeros((c, c), bf16)
        for r, (left, right) in enumerate(((4, None), (None, 0), (None, 1))):
            we_ref[r * c:(r + 1) * c, :c] = z if left is None else k_ref[left, 4]
            we_ref[r * c:(r + 1) * c, c:] = z if right is None else k_ref[right, 4]

    for v in range(g):
        split_columns(top_ref, v, 0, wide, ev, od, 0)
        split_columns(bottom_ref, v, 0, wide, ev, od, 1)
        split_columns(bottom_ref, v, 1, wide, ev, od, 2)
    first = view_ref[0] < 2
    refs = (ev, od)
    side = jnp.dot(side_blocks(refs, [(0, 0), (0, 1), (0, 2)], m), we_ref[...], preferred_element_type=f32)
    up = jnp.dot(side_blocks(refs, [(0, 0), (1, 0)], m), wm_ref[8 * c:, :], preferred_element_type=f32)
    up = shifted_sum(up[:, :c], up[:, c:], side[:, :c], n).astype(bf16).reshape(g, n, c)
    dn = jnp.dot(side_blocks(refs, [(0, 1), (1, 1), (0, 2), (1, 2)], m), wm_ref[:4 * c, :], preferred_element_type=f32)
    dn = shifted_sum(dn[:, :c], dn[:, c:], side[:, c:], n).astype(bf16).reshape(g, n, c)
    h1_ref[:, 0] = jnp.where(first, dn, up)
    h2_ref[:, 0] = jnp.where(first, up, dn)


def halo_sums(place, features, kernel):
    U, V, H, W, C = features.shape
    n = W // 2
    out = pl.BlockSpec((U, 1, n, C), lambda t, s: (0, t, 0, 0))
    return pl.pallas_call(
        halo_kernel,
        grid_spec=pltpu.PrefetchScalarGridSpec(
            num_scalar_prefetch=1, grid=(V,),
            in_specs=[
                pl.BlockSpec((U, 1, 1, W, C), lambda t, s: (0, t, 0, 0, 0)),
                pl.BlockSpec((U, 1, 2, W, C), lambda t, s: (0, t, H // 2 - 1, 0, 0)),
                pl.BlockSpec(kernel.shape, lambda t, s: (0, 0, 0, 0)),
            ],
            out_specs=[out, out],
            scratch_shapes=[
                pltpu.VMEM((W, C), f32), pltpu.VMEM((U, 3, n, C), bf16), pltpu.VMEM((U, 3, n, C), bf16),
                pltpu.VMEM((10 * C, 2 * C), bf16), pltpu.VMEM((3 * C, 2 * C), bf16),
            ],
        ),
        out_shape=[jax.ShapeDtypeStruct((U, V, n, C), bf16)] * 2,
        compiler_params=pltpu.CompilerParams(vmem_limit_bytes=48 * 2**20),
        cost_estimate=SMALL,
        name="halo",
    )(place, features, features, kernel)


def conv_kernel(view_ref, x_ref, k_ref, own_ref, oth_ref, wide, ev, od, wm_ref, we_ref):
    g, rows, wid, c = x_ref.shape[0], x_ref.shape[2], x_ref.shape[3], x_ref.shape[4]
    n = wid // 2
    m = g * n

    @pl.when(pl.program_id(0) == 0)
    def _():
        main_weights(k_ref, wm_ref)
        z = jnp.zeros((c, c), bf16)
        for j in range(7):
            we_ref[j * c:(j + 1) * c, :c] = k_ref[j, 4] if j < 5 else z
            we_ref[j * c:(j + 1) * c, c:] = k_ref[j - 2, 4] if j > 1 else z

    for v in range(g):
        for i in range(rows):
            split_columns(x_ref, v, i, wide, ev, od, i)
    first = view_ref[0] < 2
    refs = (ev, od)

    def main(lo, hi, a):
        lhs = side_blocks(refs, [(p, i) for i in range(lo, hi) for p in range(2)], m)
        return jnp.dot(lhs, wm_ref[a * 2 * c:(a + hi - lo) * 2 * c, :], preferred_element_type=f32)

    def side(lo, hi, a):
        lhs = side_blocks(refs, [(0, i) for i in range(lo, hi)], m)
        return jnp.dot(lhs, we_ref[a * c:(a + hi - lo) * c, :], preferred_element_type=f32)

    def row(mn, sd):
        return shifted_sum(mn[:, :c], mn[:, c:], sd, n).astype(bf16).reshape(g, n, c)

    pair = side(0, 5, 2)
    r0 = row(main(0, 3, 2), pair[:, :c])
    r1 = row(main(0, 5, 0), pair[:, c:])
    pair = side(2, 8, 0)
    r2 = row(main(2, 7, 0), pair[:, :c])
    r3 = row(main(4, 8, 0), pair[:, c:])
    own_ref[0, :, 0] = jnp.where(first, r0, r2)
    own_ref[1, :, 0] = jnp.where(first, r1, r3)
    oth_ref[0, :, 0] = jnp.where(first, r2, r0)
    oth_ref[1, :, 0] = jnp.where(first, r3, r1)


def conv_chunk(place, features, kernel, lo, cv):
    U, V, H, W, C = features.shape
    n = W // 2
    out = pl.BlockSpec((2, U, 1, n, C), lambda t, s: (0, 0, t, 0, 0))
    return pl.pallas_call(
        conv_kernel,
        grid_spec=pltpu.PrefetchScalarGridSpec(
            num_scalar_prefetch=1, grid=(cv,),
            in_specs=[
                pl.BlockSpec((U, 1, H, W, C), lambda t, s: (0, lo + t, 0, 0, 0)),
                pl.BlockSpec(kernel.shape, lambda t, s: (0, 0, 0, 0)),
            ],
            out_specs=[out, out],
            scratch_shapes=[
                pltpu.VMEM((W, C), f32), pltpu.VMEM((U, H, n, C), bf16), pltpu.VMEM((U, H, n, C), bf16),
                pltpu.VMEM((10 * C, 2 * C), bf16), pltpu.VMEM((7 * C, 2 * C), bf16),
            ],
        ),
        out_shape=[jax.ShapeDtypeStruct((2, U, cv, n, C), bf16)] * 2,
        compiler_params=pltpu.CompilerParams(vmem_limit_bytes=48 * 2**20),
        cost_estimate=SMALL,
        name="conv",
    )(place, features, kernel)


def norm_kernel(place_ref, own_ref, oth_ref, h1_ref, h2_ref, floor_ref, mix_ref, mine_ref, give0_ref, give1_ref):
    first = place_ref[0] < 2
    upper = place_ref[0] % 2 == 0
    g, n, c = h1_ref.shape[0], h1_ref.shape[2], h1_ref.shape[3]
    mix = mix_ref[...].astype(bf16)
    for j, (raw_ref, part_ref) in enumerate(((own_ref, h1_ref), (oth_ref, h2_ref))):
        part = part_ref[:, 0].reshape(g * n, c).astype(f32)
        coded = []
        for r in range(2):
            x = raw_ref[r, :, 0].reshape(g * n, c).astype(f32)
            x = x + jnp.where(first == (r == 0), part, 0.0)
            energy = jnp.dot((x * x).astype(bf16), mix, preferred_element_type=f32)
            coded.append((x * lax.rsqrt(floor_ref[...] + energy)).astype(bf16).reshape(g, n, c))
        mine_ref[j, :, 0] = jnp.where(upper, coded[0], coded[1])
        (give0_ref, give1_ref)[j][:, 0] = jnp.where(upper, coded[1], coded[0])

def norm_chunk(place, own, oth, h1, h2, floor, mix, lo):
    _, U, cv, n, C = own.shape
    spec = lambda lead, at=0: pl.BlockSpec(lead + (U, 1, n, C), lambda t, s: (0,) * len(lead) + (0, at + t, 0, 0))
    full = lambda a: pl.BlockSpec(a.shape, lambda t, s: (0,) * a.ndim)
    return pl.pallas_call(
        norm_kernel,
        grid_spec=pltpu.PrefetchScalarGridSpec(
            num_scalar_prefetch=1, grid=(cv,),
            in_specs=[spec((2,)), spec((2,)), spec((), lo), spec((), lo), full(floor), full(mix)],
            out_specs=[spec((2,)), spec(()), spec(())],
        ),
        out_shape=[jax.ShapeDtypeStruct((2, U, cv, n, C), bf16)] + [jax.ShapeDtypeStruct((U, cv, n, C), bf16)] * 2,
        compiler_params=pltpu.CompilerParams(vmem_limit_bytes=48 * 2**20),
        cost_estimate=SMALL,
        name="norm",
    )(place, own, oth, h1, h2, floor, mix)

def epi_kernel(pieces, v0, v1, has_prev, place_ref, *refs):
    k = len(pieces)
    srcs = refs[:3 * k]
    wm_ref, we_ref, bias_ref = refs[3 * k:3 * k + 3]
    rest = refs[3 * k + 3 + has_prev:]
    out_ref, cod, obuf, sem_in, sem_out = rest
    U = srcs[0].shape[1]
    n, c = cod.shape[2], cod.shape[3]
    V = out_ref.shape[1]
    total = out_ref.shape[0]
    nv = v1 - v0
    copies = []
    for p, (s0, s1, d0) in enumerate(pieces):
        for j in range(4):
            src = srcs[3 * p].at[j] if j < 2 else srcs[3 * p + j - 1]
            blk = place_ref[1 + j]
            cp = pltpu.make_async_copy(src.at[:, s0:s1], cod.at[pl.ds(1 + U * blk, U), d0:d0 + s1 - s0], sem_in.at[4 * p + j])
            cp.start()
            copies.append(cp)
    edge = jnp.zeros((nv + 2, n, c), bf16)
    cod[0] = edge
    cod[total + 1] = edge
    if v0 == 0:
        cod[:, 0] = jnp.zeros((total + 2, n, c), bf16)
    if v1 == V:
        cod[:, nv + 1] = jnp.zeros((total + 2, n, c), bf16)
    for cp in copies:
        cp.wait()
    m = nv * n
    steps = total // 2
    def out_copy(t, slot):
        return pltpu.make_async_copy(obuf.at[slot], out_ref.at[pl.ds(2 * t, 2), v0:v1, 0], sem_out.at[slot])
    def step(t, carry):
        slot = lax.rem(t, 2)
        @pl.when(t >= 2)
        def _():
            out_copy(t - 2, slot).wait()
        def block(i, j):
            return cod[2 * t + i, j:j + nv].reshape(m, c)
        blocks = [[block(i, j) for j in range(3)] for i in range(4)]
        ex = jnp.dot(jnp.concatenate(sum(blocks, []), axis=1), we_ref[...], preferred_element_type=f32)
        for h in range(2):
            mn = jnp.dot(jnp.concatenate(sum(blocks[h:h + 3], []), axis=1), wm_ref[...], preferred_element_type=f32)
            res = shifted_sum(mn[:, :c], mn[:, c:], ex[:, h * c:(h + 1) * c], n) + bias_ref[...]
            obuf[slot, h] = res.astype(bf16).reshape(nv, n, c)
        out_copy(t, slot).start()
        return carry
    lax.fori_loop(0, steps, step, 0)
    for t in (steps - 2, steps - 1):
        out_copy(t, t % 2).wait()

def epi_weights(k):
    c = k.shape[3]
    main = jnp.concatenate([k[:, :, 0], k[:, :, 1]], -1).reshape(-1, 2 * c)
    z = jnp.zeros((1,) + k.shape[1:2] + k.shape[3:], k.dtype)
    last = jnp.concatenate([jnp.concatenate([k[:, :, 2], z], 0), jnp.concatenate([z, k[:, :, 2]], 0)], -1)
    return main, last.reshape(-1, 2 * c)

def epi_chunk(place, sources, spans, v0, v1, prev, wm, we, bias, total, V):
    used, pieces = [], []
    for (mine, flipped), (lo, hi) in zip(sources, spans):
        a, b = max(lo, v0 - 1), min(hi, v1 + 1)
        if a < b:
            used += [mine, *flipped]
            pieces.append((a - lo, b - lo, a - (v0 - 1)))
    _, U, _, n, C = used[0].shape
    anyspec = pl.BlockSpec(memory_space=pl.ANY)
    full = lambda a: pl.BlockSpec(a.shape, lambda t, s: (0,) * a.ndim)
    nv = v1 - v0
    args = [place] + used + [wm, we, bias] + ([prev] if prev is not None else [])
    return pl.pallas_call(
        functools.partial(epi_kernel, tuple(pieces), v0, v1, int(prev is not None)),
        grid_spec=pltpu.PrefetchScalarGridSpec(
            num_scalar_prefetch=1, grid=(1,),
            in_specs=[anyspec] * len(used) + [full(wm), full(we), full(bias)] + [anyspec] * (prev is not None),
            out_specs=anyspec,
            scratch_shapes=[
                pltpu.VMEM((total + 2, nv + 2, n, C), bf16),
                pltpu.VMEM((2, 2, nv, n, C), bf16),
                pltpu.SemaphoreType.DMA((4 * len(pieces),)),
                pltpu.SemaphoreType.DMA((2,)),
            ],
        ),
        out_shape=jax.ShapeDtypeStruct((total, V, 1, n, C), bf16),
        input_output_aliases={len(args) - 1: 0} if prev is not None else {},
        compiler_params=pltpu.CompilerParams(vmem_limit_bytes=48 * 2**20),
        cost_estimate=SMALL,
        name="epi",
    )(*args)

CHUNKS = ((0, 5), (5, 9), (9, 12))


def shards(features, analysis_kernel, norm_floor, norm_mixing, epipolar_kernel, epipolar_bias):
    U, V = features.shape[:2]
    views, bands = lax.axis_size("view"), lax.axis_size("rows")
    total = U * views
    w = lax.axis_index("view")
    place = jnp.stack([w, w, w ^ 2, w ^ 1, w ^ 3]).astype(jnp.int32)
    em, ee = epi_weights(epipolar_kernel)
    floor, bias = norm_floor[None], epipolar_bias[None]
    both = ("view", "rows")
    swap = [(v * bands + r, (v ^ 2) * bands + r) for v in range(views) for r in range(bands)]
    def hop(flip):
        pairs = []
        for v in range(views):
            step = 1 if (v < 2) != (flip > 0) else -1
            pairs += [(v * bands + r, (v ^ flip) * bands + r + step) for r in range(bands) if 0 <= r + step < bands]
        return pairs
    core = [(v, v ^ 1) for v in range(views)]
    h1_sum, h2_sum = halo_sums(place, features, analysis_kernel)
    h1 = lax.ppermute(h1_sum, both, hop(0))
    h2 = lax.ppermute(h2_sum, both, hop(2))
    rows, sent = [], []
    turn, last = place, h1_sum
    for lo, hi in CHUNKS:
        turn, last = lax.optimization_barrier((turn, last))
        own, oth = conv_chunk(turn, features, analysis_kernel, lo, hi - lo)
        rows.append(own)
        sent.append(lax.ppermute(oth, both, swap))
        last = own
    sources = []
    out = None
    done = 0
    for i, (lo, hi) in enumerate(CHUNKS):
        own, oth = rows[i], sent[i]
        if out is None:
            oth, rows[-1] = lax.optimization_barrier((oth, rows[-1]))
        else:
            oth, out = lax.optimization_barrier((oth, out))
        mine, *give = norm_chunk(place, own, oth, h1, h2, floor, norm_mixing, lo)
        flipped = [lax.ppermute(g, "view", core) for g in give]
        sources.append((mine, flipped))
        upto = V if hi == V else hi - 1
        out = epi_chunk(place, sources, CHUNKS[:i + 1], done, upto, out, em, ee, bias, total, V)
        done = upto
    return out


def solution(mesh):
    in_specs = (P("view", None, "rows", None, None), P(), P(), P(), P(), P())
    out_specs = P(None, None, ("rows", "view"), None, None)
    return jax.shard_map(shards, mesh=mesh, in_specs=in_specs, out_specs=out_specs, check_vma=False)
```

time: 143 us -> 119 us (0.83)
  the two profiles are of different devices: /device:TPU:25 before, /device:TPU:121 now
where the time goes in v2:
time: 119 us; the launch traced here: 118 us
  Pallas kernels  76.2 us (64%)
  waiting for transfers between devices  25.7 us (22%)
  starting transfers between devices  13.7 us (12%)
  local copies, waits for them, and re-layouts  2.37 us (2%)
    pallas_call x3, Pallas kernels, epi_chunk(): pl.pallas_call(functools.partial(epi_kernel, tuple(pieces), v0, v1, int(p...  28.7 us
    pallas_call x3, Pallas kernels, conv_chunk(): pl.pallas_call(conv_kernel, grid_spec=pltpu.PrefetchScalarGridSpec(num_sc...  28.1 us
    ppermute x3, waiting for transfers between devices, shards(): sent.append(lax.ppermute(oth, both, swap))  20.6 us
    pallas_call x1, Pallas kernels, halo_sums(): pl.pallas_call(halo_kernel, grid_spec=pltpu.PrefetchScalarGridSpec(num_sc...  11.2 us
    pallas_call x3, Pallas kernels, norm_chunk(): pl.pallas_call(norm_kernel, grid_spec=pltpu.PrefetchScalarGridSpec(num_sc...  8.13 us
    ppermute x3, starting transfers between devices, shards(): sent.append(lax.ppermute(oth, both, swap))  7.81 us
    ppermute x6, waiting for transfers between devices, shards(): flipped = [lax.ppermute(g, 'view', core) for g in give]  5.11 us
  transfers between devices with their start and end apart: 11, of which 7 were waited for; matrix products, arithmetic and copies ran while one was open for 0% of the time, Pallas kernels for 45%

profile of v2, /device:TPU:121, one launch (start us, length us, event | category | flops | bytes accessed | tf_op | source)
XLA Modules:
  0.0 118.3 jit_solution(600185459072755937)
XLA Ops:
  0.0 0.1 stack.20.view_ref.place_ref
  0.1 0.0 copy-start
  0.1 1.1 copy-done
  1.2 11.2 %halo.1 = (bf16[3,12,128,128]{3,2,1,0:T(8,128)(2,1)S(1)}, bf16[3,12,128,128]{3,2,1,0:T(8,128)(2,1)S(1)}) custom-call(s32[5]{0:T(128)S(1)} %stack.20.view_ref.place_ref, bf16[3,12,8,256,128]{4,3,2,1,0:T(8,128)(2,1)} %x_ref.5, bf16[3,12,8,256,128]{4,3,2,1,0:T(8,128)(2,1)} %x_ref.5, bf16[5,5,128,128]{3,2,1,0:T(8,128)(2,1)S(1)} %copy-done), custom_call_target="tpu_custom_call" | custom-call | flops 1000 | bytes 1000 | tf_op jit(solution)/shard_map/halo/pallas_call | solution.py:71
  12.5 1.9 %collective-permute-start.3 = (bf16[3,12,128,128]{3,2,1,0:T(8,128)(2,1)S(1)}, bf16[3,12,128,128]{3,2,1,0:T(8,128)(2,1)S(1)}, u32[]{:S(2)}, u32[]{:S(2)}) collective-permute-start(bf16[3,12,128,128]{3,2,1,0:T(8,128)(2,1)S(1)} %get-tuple-element.41), channel_id=1, source_target_pairs={{1,64},{2,65},{3,66},{4,67},{5,68},{6,69},{7,70},{8,71},{9,72},{10... | collective-permute-start | bytes 3538952 | tf_op jit(solution)/shard_map/ppermute | solution.py:305
  14.4 2.0 %collective-permute-start.2 = (bf16[3,12,128,128]{3,2,1,0:T(8,128)(2,1)S(1)}, bf16[3,12,128,128]{3,2,1,0:T(8,128)(2,1)S(1)}, u32[]{:S(2)}, u32[]{:S(2)}) collective-permute-start(bf16[3,12,128,128]{3,2,1,0:T(8,128)(2,1)S(1)} %get-tuple-element.31), channel_id=1, source_target_pairs={{0,1},{1,2},{2,3},{3,4},{4,5},{5,6},{6,7},{7,8},{8,9},{9,10},{10,1... | collective-permute-start | bytes 3538952 | tf_op jit(solution)/shard_map/ppermute | solution.py:304
  16.4 11.2 %conv.3 = (bf16[2,3,5,128,128]{4,3,2,1,0:T(8,128)(2,1)S(1)}, bf16[2,3,5,128,128]{4,3,2,1,0:T(8,128)(2,1)S(1)}) custom-call(s32[5]{0:T(128)S(1)} %stack.20.view_ref.place_ref, bf16[3,12,8,256,128]{4,3,2,1,0:T(8,128)(2,1)} %x_ref.5, bf16[5,5,128,128]{3,2,1,0:T(8,128)(2,1)S(1)} %copy-done), custom_call_target="tpu_custom_call" | custom-call | flops 1000 | bytes 1000 | tf_op jit(solution)/shard_map/conv/pallas_call | solution.py:139
  27.6 4.7 %collective-permute-start.1 = (bf16[2,3,5,128,128]{4,3,2,1,0:T(8,128)(2,1)S(1)}, bf16[2,3,5,128,128]{4,3,2,1,0:T(8,128)(2,1)S(1)}, u32[]{:S(2)}, u32[]{:S(2)}) collective-permute-start(bf16[2,3,5,128,128]{4,3,2,1,0:T(8,128)(2,1)S(1)} %get-tuple-element.37), channel_id=1, source_target_pairs={{0,64},{1,65},{2,66},{3,67},{4,68},{5,69},{6,70},{7,71},{8,72},{9,... | collective-permute-start | bytes 2949128 | tf_op jit(solution)/shard_map/ppermute | solution.py:312
  32.3 9.4 %conv.4 = (bf16[2,3,4,128,128]{4,3,2,1,0:T(8,128)(2,1)S(1)}, bf16[2,3,4,128,128]{4,3,2,1,0:T(8,128)(2,1)S(1)}) custom-call(s32[5]{0:T(128)S(1)} %stack.20.view_ref.place_ref, bf16[3,12,8,256,128]{4,3,2,1,0:T(8,128)(2,1)} %x_ref.5, bf16[5,5,128,128]{3,2,1,0:T(8,128)(2,1)S(1)} %copy-done), custom_call_target="tpu_custom_call" | custom-call | flops 1000 | bytes 1000 | tf_op jit(solution)/shard_map/conv/pallas_call | solution.py:139
  41.7 0.1 collective-permute-start
  41.8 0.0 copy-start.3
  41.8 0.0 copy-start.5
  41.8 7.6 %conv.5 = (bf16[2,3,3,128,128]{4,3,2,1,0:T(8,128)(2,1)S(1)}, bf16[2,3,3,128,128]{4,3,2,1,0:T(8,128)(2,1)S(1)}) custom-call(s32[5]{0:T(128)S(1)} %stack.20.view_ref.place_ref, bf16[3,12,8,256,128]{4,3,2,1,0:T(8,128)(2,1)} %x_ref.5, bf16[5,5,128,128]{3,2,1,0:T(8,128)(2,1)S(1)} %copy-done), custom_call_target="tpu_custom_call" | custom-call | flops 1000 | bytes 1000 | tf_op jit(solution)/shard_map/conv/pallas_call | solution.py:139
  49.4 3.0 %collective-permute-start.8 = (bf16[2,3,3,128,128]{4,3,2,1,0:T(8,128)(2,1)S(1)}, bf16[2,3,3,128,128]{4,3,2,1,0:T(8,128)(2,1)S(1)}, u32[]{:S(2)}, u32[]{:S(2)}) collective-permute-start(bf16[2,3,3,128,128]{4,3,2,1,0:T(8,128)(2,1)S(1)} %get-tuple-element.50), channel_id=1, source_target_pairs={{0,64},{1,65},{2,66},{3,67},{4,68},{5,69},{6,70},{7,71},{8,72},{9,... | collective-permute-start | bytes 1769480 | tf_op jit(solution)/shard_map/ppermute | solution.py:312
  52.4 20.6 %collective-permute-done.1.oth_ref = bf16[2,3,5,128,128]{4,3,2,1,0:T(8,128)(2,1)S(1)} collective-permute-done((bf16[2,3,5,128,128]{4,3,2,1,0:T(8,128)(2,1)S(1)}, bf16[2,3,5,128,128]{4,3,2,1,0:T(8,128)(2,1)S(1)}, u32[]{:S(2)}, u32[]{:S(2)}) %collective-permute-start.1) | collective-permute-done | bytes 983072 | tf_op jit(solution)/shard_map/ppermute | solution.py:312
  73.0 0.0 collective-permute-done.3.h2_ref
  73.0 0.0 copy-start.1
  73.0 0.0 collective-permute-done.2.h1_ref
  73.0 1.0 copy-done.1
  74.0 0.0 copy-done.3
  74.0 0.0 copy-done.5
  74.1 4.3 %norm.3 = (bf16[2,3,5,128,128]{4,3,2,1,0:T(8,128)(2,1)S(1)}, bf16[3,5,128,128]{3,2,1,0:T(8,128)(2,1)S(1)}, bf16[3,5,128,128]{3,2,1,0:T(8,128)(2,1)S(1)}) custom-call(s32[5]{0:T(128)S(1)} %stack.20.view_ref.place_ref, bf16[2,3,5,128,128]{4,3,2,1,0:T(8,128)(2,1)S(1)} %get-tuple-element.33.own_ref, ...), custom_call_target="tpu_custom_call" | custom-call | flops 1000 | bytes 1000 | tf_op jit(solution)/shard_map/norm/pallas_call | solution.py:180
  78.4 0.7 collective-permute-start.4
  79.1 0.1 collective-permute-start.5
  79.2 0.0 copy-done.6
  79.2 0.1 slice_bitcast_fusion
  79.3 0.0 copy-start.4
  79.3 0.1 fusion.2
  79.3 0.1 pad_maximum_fusion.refs_3_.refs_6_
  79.4 1.1 collective-permute-done.4.refs_1_
  80.6 0.7 collective-permute-done.5.refs_2_
  81.3 0.0 copy-done.4
  81.3 9.5 %epi.3.refs_9_ = bf16[12,12,1,128,128]{4,3,2,1,0:T(8,128)(2,1)} custom-call(s32[5]{0:T(128)S(1)} %stack.20.view_ref.place_ref, bf16[2,3,5,128,128]{4,3,2,1,0:T(8,128)(2,1)S(1)} %get-tuple-element.42.refs_0_, bf16[3,5,128,128]{3,2,1,0:T(8,128)(2,1)S(1)} %collective-permute-done.4.refs_1_, bf16[3,5,128,128]{3,2,1,0:T(8,128)(2,1)S(1)} %collective-permute-done.5.refs_2_, ...), custom_call_target="tpu_custom_call" | custom-call | flops 1000 | bytes 1000 | tf_op jit(solution)/shard_map/epi/pallas_call | solution.py:263
  90.8 0.0 collective-permute-done.oth_ref
  90.8 0.0 copy-done.2
  90.8 2.1 %norm.4 = (bf16[2,3,4,128,128]{4,3,2,1,0:T(8,128)(2,1)S(1)}, bf16[3,4,128,128]{3,2,1,0:T(8,128)(2,1)S(1)}, bf16[3,4,128,128]{3,2,1,0:T(8,128)(2,1)S(1)}) custom-call(s32[5]{0:T(128)S(1)} %stack.20.view_ref.place_ref, bf16[2,3,4,128,128]{4,3,2,1,0:T(8,128)(2,1)S(1)} %get-tuple-element.35.own_ref, ...), custom_call_target="tpu_custom_call" | custom-call | flops 1000 | bytes 1000 | tf_op jit(solution)/shard_map/norm/pallas_call | solution.py:180
  92.9 0.5 collective-permute-start.6
  93.3 0.1 collective-permute-start.7
  93.5 1.2 %collective-permute-done.6.refs_4_.refs_1_ = bf16[3,4,128,128]{3,2,1,0:T(8,128)(2,1)S(1)} collective-permute-done((bf16[3,4,128,128]{3,2,1,0:T(8,128)(2,1)S(1)}, bf16[3,4,128,128]{3,2,1,0:T(8,128)(2,1)S(1)}, u32[]{:S(2)}, u32[]{:S(2)}) %collective-permute-start.6) | collective-permute-done | bytes 393248 | tf_op jit(solution)/shard_map/ppermute | solution.py:324
  94.7 0.6 collective-permute-done.7.refs_5_.refs_2_
  95.3 9.7 %epi.4.refs_9_ = bf16[12,12,1,128,128]{4,3,2,1,0:T(8,128)(2,1)} custom-call(s32[5]{0:T(128)S(1)} %stack.20.view_ref.place_ref, bf16[2,3,5,128,128]{4,3,2,1,0:T(8,128)(2,1)S(1)} %get-tuple-element.42.refs_0_, bf16[3,5,128,128]{3,2,1,0:T(8,128)(2,1)S(1)} %collective-permute-done.4.refs_1_, ...), custom_call_target="tpu_custom_call", output_to_operand_aliasing={{}: (10, {})} | custom-call | flops 1000 | bytes 1000 | tf_op jit(solution)/shard_map/epi/pallas_call | solution.py:263
  104.9 0.0 collective-permute-done.8.oth_ref
  104.9 1.7 %norm.5 = (bf16[2,3,3,128,128]{4,3,2,1,0:T(8,128)(2,1)S(1)}, bf16[3,3,128,128]{3,2,1,0:T(8,128)(2,1)S(1)}, bf16[3,3,128,128]{3,2,1,0:T(8,128)(2,1)S(1)}) custom-call(s32[5]{0:T(128)S(1)} %stack.20.view_ref.place_ref, bf16[2,3,3,128,128]{4,3,2,1,0:T(8,128)(2,1)S(1)} %get-tuple-element.49.own_ref, ...), custom_call_target="tpu_custom_call" | custom-call | flops 1000 | bytes 1000 | tf_op jit(solution)/shard_map/norm/pallas_call | solution.py:180
  106.7 0.5 collective-permute-start.9
  107.1 0.1 collective-permute-start.10
  107.2 1.1 collective-permute-done.9.refs_4_
  108.3 0.4 collective-permute-done.10.refs_5_
  108.7 9.6 %epi.5 = bf16[12,12,1,128,128]{4,3,2,1,0:T(8,128)(2,1)} custom-call(s32[5]{0:T(128)S(1)} %stack.20.view_ref.place_ref, bf16[2,3,4,128,128]{4,3,2,1,0:T(8,128)(2,1)S(1)} %get-tuple-element.46.refs_3_.refs_0_, bf16[3,4,128,128]{3,2,1,0:T(8,128)(2,1)S(1)} %collective-permute-done.6.refs_4_.refs_1_, ...), custom_call_target="tpu_custom_call", output_to_operand_aliasing={{}: (10, {})} | custom-call | flops 1000 | bytes 1000 | tf_op jit(solution)/shard_map/epi/pallas_call | solution.py:263
  (2 shorter events, 0.0 us)
Async XLA Ops:
  0.1 1.1 copy-start
  12.5 60.5 %collective-permute-start.3 = (bf16[3,12,128,128]{3,2,1,0:T(8,128)(2,1)S(1)}, bf16[3,12,128,128]{3,2,1,0:T(8,128)(2,1)S(1)}, u32[]{:S(2)}, u32[]{:S(2)}) collective-permute-start(bf16[3,12,128,128]{3,2,1,0:T(8,128)(2,1)S(1)} %get-tuple-element.41), channel_id=1, source_target_pairs={{1,64},{2,65},{3,66},{4,67},{5,68},{6,69},{7,70},{8,71},{9,72},{10... | collective-permute-start | bytes 3538952 | tf_op jit(solution)/shard_map/ppermute | solution.py:305
  14.4 58.6 %collective-permute-start.2 = (bf16[3,12,128,128]{3,2,1,0:T(8,128)(2,1)S(1)}, bf16[3,12,128,128]{3,2,1,0:T(8,128)(2,1)S(1)}, u32[]{:S(2)}, u32[]{:S(2)}) collective-permute-start(bf16[3,12,128,128]{3,2,1,0:T(8,128)(2,1)S(1)} %get-tuple-element.31), channel_id=1, source_target_pairs={{0,1},{1,2},{2,3},{3,4},{4,5},{5,6},{6,7},{7,8},{8,9},{9,10},{10,1... | collective-permute-start | bytes 3538952 | tf_op jit(solution)/shard_map/ppermute | solution.py:304
  27.6 45.4 %collective-permute-start.1 = (bf16[2,3,5,128,128]{4,3,2,1,0:T(8,128)(2,1)S(1)}, bf16[2,3,5,128,128]{4,3,2,1,0:T(8,128)(2,1)S(1)}, u32[]{:S(2)}, u32[]{:S(2)}) collective-permute-start(bf16[2,3,5,128,128]{4,3,2,1,0:T(8,128)(2,1)S(1)} %get-tuple-element.37), channel_id=1, source_target_pairs={{0,64},{1,65},{2,66},{3,67},{4,68},{5,69},{6,70},{7,71},{8,72},{9,... | collective-permute-start | bytes 2949128 | tf_op jit(solution)/shard_map/ppermute | solution.py:312
  41.7 49.1 %collective-permute-start = (bf16[2,3,4,128,128]{4,3,2,1,0:T(8,128)(2,1)S(1)}, bf16[2,3,4,128,128]{4,3,2,1,0:T(8,128)(2,1)S(1)}, u32[]{:S(2)}, u32[]{:S(2)}) collective-permute-start(bf16[2,3,4,128,128]{4,3,2,1,0:T(8,128)(2,1)S(1)} %get-tuple-element.36), channel_id=1, source_target_pairs={{0,64},{1,65},{2,66},{3,67},{4,68},{5,69},{6,70},{7,71},{8,72},{9,... | collective-permute-start | bytes 2359304 | tf_op jit(solution)/shard_map/ppermute | solution.py:312
  41.8 32.3 %copy-start.3 = (f32[128,128]{1,0:T(8,128)S(1)}, f32[128,128]{1,0:T(8,128)}, u32[]{:S(2)}) copy-start(f32[128,128]{1,0:T(8,128)} %mix_ref.5) | copy-start | bytes 196612
  41.8 32.3 %copy-start.5 = (f32[128]{0:T(128)S(1)}, f32[128]{0:T(128)}, u32[]{:S(2)}) copy-start(f32[128]{0:T(128)} %param.8) | copy-start | bytes 1540
  49.4 55.6 %collective-permute-start.8 = (bf16[2,3,3,128,128]{4,3,2,1,0:T(8,128)(2,1)S(1)}, bf16[2,3,3,128,128]{4,3,2,1,0:T(8,128)(2,1)S(1)}, u32[]{:S(2)}, u32[]{:S(2)}) collective-permute-start(bf16[2,3,3,128,128]{4,3,2,1,0:T(8,128)(2,1)S(1)} %get-tuple-element.50), channel_id=1, source_target_pairs={{0,64},{1,65},{2,66},{3,67},{4,68},{5,69},{6,70},{7,71},{8,72},{9,... | collective-permute-start | bytes 1769480 | tf_op jit(solution)/shard_map/ppermute | solution.py:312
  73.0 1.0 copy-start.1
  74.0 5.1 %copy-start.6 = (bf16[3,3,3,128,128]{4,3,2,1,0:T(8,128)(2,1)S(1)}, bf16[3,3,3,128,128]{4,3,2,1,0:T(8,128)(2,1)}, u32[]{:S(2)}) copy-start(bf16[3,3,3,128,128]{4,3,2,1,0:T(8,128)(2,1)} %param.10) | copy-start | bytes 2654212
  78.4 2.2 %collective-permute-start.4 = (bf16[3,5,128,128]{3,2,1,0:T(8,128)(2,1)S(1)}, bf16[3,5,128,128]{3,2,1,0:T(8,128)(2,1)S(1)}, u32[]{:S(2)}, u32[]{:S(2)}) collective-permute-start(bf16[3,5,128,128]{3,2,1,0:T(8,128)(2,1)S(1)} %get-tuple-element.43), channel_id=1, source_target_pairs={{0,32},{32,0},{64,96},{96,64},{1,33},{33,1},{65,97},{97,65},{2,34}... | collective-permute-start | bytes 1474568 | tf_op jit(solution)/shard_map/ppermute | solution.py:324
  79.1 2.2 %collective-permute-start.5 = (bf16[3,5,128,128]{3,2,1,0:T(8,128)(2,1)S(1)}, bf16[3,5,128,128]{3,2,1,0:T(8,128)(2,1)S(1)}, u32[]{:S(2)}, u32[]{:S(2)}) collective-permute-start(bf16[3,5,128,128]{3,2,1,0:T(8,128)(2,1)S(1)} %get-tuple-element.44), channel_id=1, source_target_pairs={{0,32},{32,0},{64,96},{96,64},{1,33},{33,1},{65,97},{97,65},{2,34}... | collective-permute-start | bytes 1474568 | tf_op jit(solution)/shard_map/ppermute | solution.py:324
  79.3 2.0 %copy-start.4 = (f32[128]{0:T(128)S(1)}, f32[128]{0:T(128)}, u32[]{:S(2)}) copy-start(f32[128]{0:T(128)} %param.11) | copy-start | bytes 1540
  81.3 9.5 %copy-start.2 = (bf16[3,12,128,128]{3,2,1,0:T(8,128)(2,1)S(1)}, bf16[3,12,128,128]{3,2,1,0:T(8,128)(2,1)}, u32[]{:S(2)}) copy-start(bf16[3,12,128,128]{3,2,1,0:T(8,128)(2,1)} %copy-done.1) | copy-start | bytes 3538948
  92.9 1.8 %collective-permute-start.6 = (bf16[3,4,128,128]{3,2,1,0:T(8,128)(2,1)S(1)}, bf16[3,4,128,128]{3,2,1,0:T(8,128)(2,1)S(1)}, u32[]{:S(2)}, u32[]{:S(2)}) collective-permute-start(bf16[3,4,128,128]{3,2,1,0:T(8,128)(2,1)S(1)} %get-tuple-element.47), channel_id=1, source_target_pairs={{0,32},{32,0},{64,96},{96,64},{1,33},{33,1},{65,97},{97,65},{2,34}... | collective-permute-start | bytes 1179656 | tf_op jit(solution)/shard_map/ppermute | solution.py:324
  93.3 1.9 %collective-permute-start.7 = (bf16[3,4,128,128]{3,2,1,0:T(8,128)(2,1)S(1)}, bf16[3,4,128,128]{3,2,1,0:T(8,128)(2,1)S(1)}, u32[]{:S(2)}, u32[]{:S(2)}) collective-permute-start(bf16[3,4,128,128]{3,2,1,0:T(8,128)(2,1)S(1)} %get-tuple-element.48), channel_id=1, source_target_pairs={{0,32},{32,0},{64,96},{96,64},{1,33},{33,1},{65,97},{97,65},{2,34}... | collective-permute-start | bytes 1179656 | tf_op jit(solution)/shard_map/ppermute | solution.py:324
  106.7 1.7 %collective-permute-start.9 = (bf16[3,3,128,128]{3,2,1,0:T(8,128)(2,1)S(1)}, bf16[3,3,128,128]{3,2,1,0:T(8,128)(2,1)S(1)}, u32[]{:S(2)}, u32[]{:S(2)}) collective-permute-start(bf16[3,3,128,128]{3,2,1,0:T(8,128)(2,1)S(1)} %get-tuple-element.54), channel_id=1, source_target_pairs={{0,32},{32,0},{64,96},{96,64},{1,33},{33,1},{65,97},{97,65},{2,34}... | collective-permute-start | bytes 884744 | tf_op jit(solution)/shard_map/ppermute | solution.py:324
  107.1 1.6 %collective-permute-start.10 = (bf16[3,3,128,128]{3,2,1,0:T(8,128)(2,1)S(1)}, bf16[3,3,128,128]{3,2,1,0:T(8,128)(2,1)S(1)}, u32[]{:S(2)}, u32[]{:S(2)}) collective-permute-start(bf16[3,3,128,128]{3,2,1,0:T(8,128)(2,1)S(1)} %get-tuple-element.55), channel_id=1, source_target_pairs={{0,32},{32,0},{64,96},{96,64},{1,33},{33,1},{65,97},{97,65},{2,34}... | collective-permute-start | bytes 884744 | tf_op jit(solution)/shard_map/ppermute | solution.py:324

commit v3 on v2

--- a/solution.py
+++ b/solution.py
@@ -18,10 +18,10 @@
     return down + here + up
 
 def split_columns(x_ref, v, i, wide, ev, od, at):
-    n = wide.shape[0] // 2
-    wide[...] = x_ref[v, 0, i].astype(f32)
-    ev[v, at] = wide[pl.ds(0, n, 2), :].astype(bf16)
-    od[v, at] = wide[pl.ds(1, n, 2), :].astype(bf16)
+    n = wide.shape[1] // 2
+    wide[at] = x_ref[v, i].astype(f32)
+    ev[v, at] = wide[at, pl.ds(0, n, 2), :].astype(bf16)
+    od[v, at] = wide[at, pl.ds(1, n, 2), :].astype(bf16)
 
 
 def main_weights(k_ref, wm_ref):
@@ -37,7 +37,7 @@
 
 
 def halo_kernel(view_ref, top_ref, bottom_ref, k_ref, h1_ref, h2_ref, wide, ev, od, wm_ref, we_ref):
-    g, wid, c = top_ref.shape[0], top_ref.shape[3], top_ref.shape[4]
+    g, vs, wid, c = top_ref.shape[0], top_ref.shape[1], top_ref.shape[3], top_ref.shape[4]
     n = wid // 2
     m = g * n
 
@@ -49,37 +49,39 @@
             we_ref[r * c:(r + 1) * c, :c] = z if left is None else k_ref[left, 4]
             we_ref[r * c:(r + 1) * c, c:] = z if right is None else k_ref[right, 4]
 
-    for v in range(g):
-        split_columns(top_ref, v, 0, wide, ev, od, 0)
-        split_columns(bottom_ref, v, 0, wide, ev, od, 1)
-        split_columns(bottom_ref, v, 1, wide, ev, od, 2)
     first = view_ref[0] < 2
     refs = (ev, od)
-    side = jnp.dot(side_blocks(refs, [(0, 0), (0, 1), (0, 2)], m), we_ref[...], preferred_element_type=f32)
-    up = jnp.dot(side_blocks(refs, [(0, 0), (1, 0)], m), wm_ref[8 * c:, :], preferred_element_type=f32)
-    up = shifted_sum(up[:, :c], up[:, c:], side[:, :c], n).astype(bf16).reshape(g, n, c)
-    dn = jnp.dot(side_blocks(refs, [(0, 1), (1, 1), (0, 2), (1, 2)], m), wm_ref[:4 * c, :], preferred_element_type=f32)
-    dn = shifted_sum(dn[:, :c], dn[:, c:], side[:, c:], n).astype(bf16).reshape(g, n, c)
-    h1_ref[:, 0] = jnp.where(first, dn, up)
-    h2_ref[:, 0] = jnp.where(first, up, dn)
+    for b in range(vs):
+        for v in range(g):
+            split_columns(top_ref.at[:, b], v, 0, wide, ev, od, 0)
+            split_columns(bottom_ref.at[:, b], v, 0, wide, ev, od, 1)
+            split_columns(bottom_ref.at[:, b], v, 1, wide, ev, od, 2)
+        side = jnp.dot(side_blocks(refs, [(0, 0), (0, 1), (0, 2)], m), we_ref[...], preferred_element_type=f32)
+        up = jnp.dot(side_blocks(refs, [(0, 0), (1, 0)], m), wm_ref[8 * c:, :], preferred_element_type=f32)
+        up = shifted_sum(up[:, :c], up[:, c:], side[:, :c], n).astype(bf16).reshape(g, n, c)
+        dn = jnp.dot(side_blocks(refs, [(0, 1), (1, 1), (0, 2), (1, 2)], m), wm_ref[:4 * c, :], preferred_element_type=f32)
+        dn = shifted_sum(dn[:, :c], dn[:, c:], side[:, c:], n).astype(bf16).reshape(g, n, c)
+        h1_ref[:, b] = jnp.where(first, dn, up)
+        h2_ref[:, b] = jnp.where(first, up, dn)
 
 
 def halo_sums(place, features, kernel):
     U, V, H, W, C = features.shape
     n = W // 2
-    out = pl.BlockSpec((U, 1, n, C), lambda t, s: (0, t, 0, 0))
+    vs = HALO_STEP if V % HALO_STEP == 0 else 1
+    out = pl.BlockSpec((U, vs, n, C), lambda t, s: (0, t, 0, 0))
     return pl.pallas_call(
         halo_kernel,
         grid_spec=pltpu.PrefetchScalarGridSpec(
-            num_scalar_prefetch=1, grid=(V,),
+            num_scalar_prefetch=1, grid=(V // vs,),
             in_specs=[
-                pl.BlockSpec((U, 1, 1, W, C), lambda t, s: (0, t, 0, 0, 0)),
-                pl.BlockSpec((U, 1, 2, W, C), lambda t, s: (0, t, H // 2 - 1, 0, 0)),
-                pl.BlockSpec(kernel.shape, lambda t, s: (0, 0, 0, 0)),
+                pl.BlockSpec((U, vs, 1, W, C), lambda t, s: (0, t, 0, 0, 0)),
+                pl.BlockSpec((U, vs, 2, W, C), lambda t, s: (0, t, H // 2 - 1, 0, 0)),
+                pl.BlockSpec(memory_space=pltpu.VMEM),
             ],
             out_specs=[out, out],
             scratch_shapes=[
-                pltpu.VMEM((W, C), f32), pltpu.VMEM((U, 3, n, C), bf16), pltpu.VMEM((U, 3, n, C), bf16),
+                pltpu.VMEM((3, W, C), f32), pltpu.VMEM((U, 3, n, C), bf16), pltpu.VMEM((U, 3, n, C), bf16),
                 pltpu.VMEM((10 * C, 2 * C), bf16), pltpu.VMEM((3 * C, 2 * C), bf16),
             ],
         ),
@@ -90,7 +92,8 @@
     )(place, features, features, kernel)
 
 
-def conv_kernel(view_ref, x_ref, k_ref, own_ref, oth_ref, wide, ev, od, wm_ref, we_ref):
+def conv_kernel(starts, view_ref, x_ref, k_ref, *rest):
+    outs, (wide, ev, od, wm_ref, we_ref) = rest[:-5], rest[-5:]
     g, rows, wid, c = x_ref.shape[0], x_ref.shape[2], x_ref.shape[3], x_ref.shape[4]
     n = wid // 2
     m = g * n
@@ -105,7 +108,7 @@
 
     for v in range(g):
         for i in range(rows):
-            split_columns(x_ref, v, i, wide, ev, od, i)
+            split_columns(x_ref.at[:, 0], v, i, wide, ev, od, i)
     first = view_ref[0] < 2
     refs = (ev, od)
 
@@ -120,75 +123,91 @@
     def row(mn, sd):
         return shifted_sum(mn[:, :c], mn[:, c:], sd, n).astype(bf16).reshape(g, n, c)
 
-    pair = side(0, 5, 2)
-    r0 = row(main(0, 3, 2), pair[:, :c])
-    r1 = row(main(0, 5, 0), pair[:, c:])
-    pair = side(2, 8, 0)
-    r2 = row(main(2, 7, 0), pair[:, :c])
-    r3 = row(main(4, 8, 0), pair[:, c:])
-    own_ref[0, :, 0] = jnp.where(first, r0, r2)
-    own_ref[1, :, 0] = jnp.where(first, r1, r3)
-    oth_ref[0, :, 0] = jnp.where(first, r2, r0)
-    oth_ref[1, :, 0] = jnp.where(first, r3, r1)
-
-
-def conv_chunk(place, features, kernel, lo, cv):
+    def rows_of_step(own_ref, oth_ref):
+        pair = side(0, 5, 2)
+        r0 = row(main(0, 3, 2), pair[:, :c])
+        r1 = row(main(0, 5, 0), pair[:, c:])
+        pair = side(2, 8, 0)
+        r2 = row(main(2, 7, 0), pair[:, :c])
+        r3 = row(main(4, 8, 0), pair[:, c:])
+        own_ref[0, :, 0] = jnp.where(first, r0, r2)
+        own_ref[1, :, 0] = jnp.where(first, r1, r3)
+        oth_ref[0, :, 0] = jnp.where(first, r2, r0)
+        oth_ref[1, :, 0] = jnp.where(first, r3, r1)
+
+    t = pl.program_id(0)
+    for q, start in enumerate(starts):
+        inside = t >= start
+        if q + 1 < len(starts):
+            inside = jnp.logical_and(inside, t < starts[q + 1])
+        pl.when(inside)(functools.partial(rows_of_step, outs[2 * q], outs[2 * q + 1]))
+
+
+def conv_chunks(place, features, kernel, spans):
     U, V, H, W, C = features.shape
     n = W // 2
-    out = pl.BlockSpec((2, U, 1, n, C), lambda t, s: (0, 0, t, 0, 0))
+    base = spans[0][0]
+    starts = tuple(lo - base for lo, _ in spans)
+
+    def out(lo, hi):
+        return pl.BlockSpec((2, U, 1, n, C), lambda t, s: (0, 0, jnp.clip(t - (lo - base), 0, hi - lo - 1), 0, 0))
+
     return pl.pallas_call(
-        conv_kernel,
+        functools.partial(conv_kernel, starts),
         grid_spec=pltpu.PrefetchScalarGridSpec(
-            num_scalar_prefetch=1, grid=(cv,),
+            num_scalar_prefetch=1, grid=(spans[-1][1] - base,),
             in_specs=[
-                pl.BlockSpec((U, 1, H, W, C), lambda t, s: (0, lo + t, 0, 0, 0)),
-                pl.BlockSpec(kernel.shape, lambda t, s: (0, 0, 0, 0)),
-            ],
-            out_specs=[out, out],
+                pl.BlockSpec((U, 1, H, W, C), lambda t, s: (0, base + t, 0, 0, 0)),
+                pl.BlockSpec(memory_space=pltpu.VMEM),
+            ],
+            out_specs=[out(*span) for span in spans for _ in range(2)],
             scratch_shapes=[
-                pltpu.VMEM((W, C), f32), pltpu.VMEM((U, H, n, C), bf16), pltpu.VMEM((U, H, n, C), bf16),
+                pltpu.VMEM((H, W, C), f32), pltpu.VMEM((U, H, n, C), bf16), pltpu.VMEM((U, H, n, C), bf16),
                 pltpu.VMEM((10 * C, 2 * C), bf16), pltpu.VMEM((7 * C, 2 * C), bf16),
             ],
         ),
-        out_shape=[jax.ShapeDtypeStruct((2, U, cv, n, C), bf16)] * 2,
+        out_shape=[jax.ShapeDtypeStruct((2, U, hi - lo, n, C), bf16) for lo, hi in spans for _ in range(2)],
         compiler_params=pltpu.CompilerParams(vmem_limit_bytes=48 * 2**20),
         cost_estimate=SMALL,
         name="conv",
     )(place, features, kernel)
 
 
-def norm_kernel(place_ref, own_ref, oth_ref, h1_ref, h2_ref, floor_ref, mix_ref, mine_ref, give0_ref, give1_ref):
+def norm_kernel(lo, place_ref, own_ref, oth_ref, h1_ref, h2_ref, floor_ref, mix_ref, mine_ref, give0_ref, give1_ref):
     first = place_ref[0] < 2
     upper = place_ref[0] % 2 == 0
-    g, n, c = h1_ref.shape[0], h1_ref.shape[2], h1_ref.shape[3]
+    _, g, cv, n, c = own_ref.shape
     mix = mix_ref[...].astype(bf16)
-    for j, (raw_ref, part_ref) in enumerate(((own_ref, h1_ref), (oth_ref, h2_ref))):
-        part = part_ref[:, 0].reshape(g * n, c).astype(f32)
-        coded = []
-        for r in range(2):
-            x = raw_ref[r, :, 0].reshape(g * n, c).astype(f32)
-            x = x + jnp.where(first == (r == 0), part, 0.0)
-            energy = jnp.dot((x * x).astype(bf16), mix, preferred_element_type=f32)
-            coded.append((x * lax.rsqrt(floor_ref[...] + energy)).astype(bf16).reshape(g, n, c))
-        mine_ref[j, :, 0] = jnp.where(upper, coded[0], coded[1])
-        (give0_ref, give1_ref)[j][:, 0] = jnp.where(upper, coded[1], coded[0])
+
+    def step(v, carry):
+        for j, (raw_ref, part_ref) in enumerate(((own_ref, h1_ref), (oth_ref, h2_ref))):
+            part = part_ref[:, lo + v].reshape(g * n, c).astype(f32)
+            coded = []
+            for r in range(2):
+                x = raw_ref[r, :, v].reshape(g * n, c).astype(f32)
+                x = x + jnp.where(first == (r == 0), part, 0.0)
+                energy = jnp.dot((x * x).astype(bf16), mix, preferred_element_type=f32)
+                coded.append((x * lax.rsqrt(floor_ref[...] + energy)).astype(bf16).reshape(g, n, c))
+            mine_ref[j, :, v] = jnp.where(upper, coded[0], coded[1])
+            (give0_ref, give1_ref)[j][:, v] = jnp.where(upper, coded[1], coded[0])
+        return carry
+
+    lax.fori_loop(0, cv, step, 0)
+
 
 def norm_chunk(place, own, oth, h1, h2, floor, mix, lo):
     _, U, cv, n, C = own.shape
-    spec = lambda lead, at=0: pl.BlockSpec(lead + (U, 1, n, C), lambda t, s: (0,) * len(lead) + (0, at + t, 0, 0))
-    full = lambda a: pl.BlockSpec(a.shape, lambda t, s: (0,) * a.ndim)
+    whole = pl.BlockSpec(memory_space=pltpu.VMEM)
     return pl.pallas_call(
-        norm_kernel,
-        grid_spec=pltpu.PrefetchScalarGridSpec(
-            num_scalar_prefetch=1, grid=(cv,),
-            in_specs=[spec((2,)), spec((2,)), spec((), lo), spec((), lo), full(floor), full(mix)],
-            out_specs=[spec((2,)), spec(()), spec(())],
-        ),
+        functools.partial(norm_kernel, lo),
+        in_specs=[pl.BlockSpec(memory_space=pltpu.SMEM)] + [whole] * 6,
+        out_specs=[whole] * 3,
         out_shape=[jax.ShapeDtypeStruct((2, U, cv, n, C), bf16)] + [jax.ShapeDtypeStruct((U, cv, n, C), bf16)] * 2,
-        compiler_params=pltpu.CompilerParams(vmem_limit_bytes=48 * 2**20),
+        compiler_params=pltpu.CompilerParams(vmem_limit_bytes=16 * 2**20),
         cost_estimate=SMALL,
         name="norm",
     )(place, own, oth, h1, h2, floor, mix)
+
 
 def epi_kernel(pieces, v0, v1, has_prev, place_ref, *refs):
     k = len(pieces)
@@ -201,14 +220,12 @@
     V = out_ref.shape[1]
     total = out_ref.shape[0]
     nv = v1 - v0
-    copies = []
     for p, (s0, s1, d0) in enumerate(pieces):
         for j in range(4):
             src = srcs[3 * p].at[j] if j < 2 else srcs[3 * p + j - 1]
             blk = place_ref[1 + j]
-            cp = pltpu.make_async_copy(src.at[:, s0:s1], cod.at[pl.ds(1 + U * blk, U), d0:d0 + s1 - s0], sem_in.at[4 * p + j])
+            cp = pltpu.make_async_copy(src.at[:, s0:s1], cod.at[pl.ds(1 + U * blk, U), d0:d0 + s1 - s0], sem_in.at[4 * p + blk])
             cp.start()
-            copies.append(cp)
     edge = jnp.zeros((nv + 2, n, c), bf16)
     cod[0] = edge
     cod[total + 1] = edge
@@ -216,14 +233,21 @@
         cod[:, 0] = jnp.zeros((total + 2, n, c), bf16)
     if v1 == V:
         cod[:, nv + 1] = jnp.zeros((total + 2, n, c), bf16)
-    for cp in copies:
-        cp.wait()
+
+    def arrived(b):
+        for p, (s0, s1, d0) in enumerate(pieces):
+            pltpu.make_async_copy(
+                srcs[3 * p].at[0, :, s0:s1], cod.at[1 + U * b:1 + U * (b + 1), d0:d0 + s1 - s0], sem_in.at[4 * p + b]
+            ).wait()
     m = nv * n
     steps = total // 2
     def out_copy(t, slot):
         return pltpu.make_async_copy(obuf.at[slot], out_ref.at[pl.ds(2 * t, 2), v0:v1, 0], sem_out.at[slot])
     def step(t, carry):
         slot = lax.rem(t, 2)
+        for b in range(total // U):
+            pl.when(t == max(0, -(-(U * b - 2) // 2)))(functools.partial(arrived, b))
+
         @pl.when(t >= 2)
         def _():
             out_copy(t - 2, slot).wait()
@@ -257,14 +281,14 @@
             pieces.append((a - lo, b - lo, a - (v0 - 1)))
     _, U, _, n, C = used[0].shape
     anyspec = pl.BlockSpec(memory_space=pl.ANY)
-    full = lambda a: pl.BlockSpec(a.shape, lambda t, s: (0,) * a.ndim)
+    whole = pl.BlockSpec(memory_space=pltpu.VMEM)
     nv = v1 - v0
     args = [place] + used + [wm, we, bias] + ([prev] if prev is not None else [])
     return pl.pallas_call(
         functools.partial(epi_kernel, tuple(pieces), v0, v1, int(prev is not None)),
         grid_spec=pltpu.PrefetchScalarGridSpec(
             num_scalar_prefetch=1, grid=(1,),
-            in_specs=[anyspec] * len(used) + [full(wm), full(we), full(bias)] + [anyspec] * (prev is not None),
+            in_specs=[anyspec] * len(used) + [whole] * 3 + [anyspec] * (prev is not None),
             out_specs=anyspec,
             scratch_shapes=[
                 pltpu.VMEM((total + 2, nv + 2, n, C), bf16),
@@ -275,12 +299,14 @@
         ),
         out_shape=jax.ShapeDtypeStruct((total, V, 1, n, C), bf16),
         input_output_aliases={len(args) - 1: 0} if prev is not None else {},
-        compiler_params=pltpu.CompilerParams(vmem_limit_bytes=48 * 2**20),
+        compiler_params=pltpu.CompilerParams(vmem_limit_bytes=24 * 2**20),
         cost_estimate=SMALL,
         name="epi",
     )(*args)
 
-CHUNKS = ((0, 5), (5, 9), (9, 12))
+
+CHUNKS = ((0, 4), (4, 9), (9, 12))
+HALO_STEP = 3
 
 
 def shards(features, analysis_kernel, norm_floor, norm_mixing, epipolar_kernel, epipolar_bias):
@@ -305,12 +331,13 @@
     h2 = lax.ppermute(h2_sum, both, hop(2))
     rows, sent = [], []
     turn, last = place, h1_sum
-    for lo, hi in CHUNKS:
+    for spans in (CHUNKS[:1], CHUNKS[1:]):
         turn, last = lax.optimization_barrier((turn, last))
-        own, oth = conv_chunk(turn, features, analysis_kernel, lo, hi - lo)
-        rows.append(own)
-        sent.append(lax.ppermute(oth, both, swap))
-        last = own
+        done = conv_chunks(turn, features, analysis_kernel, spans)
+        for own, oth in zip(done[::2], done[1::2]):
+            rows.append(own)
+            sent.append(lax.ppermute(oth, both, swap))
+        last = done[0]
     sources = []
     out = None
     done = 0

time: 119 us -> 116 us (0.975)
  Pallas kernels: 76.2 us -> 67.7 us
  waiting for transfers between devices: 25.7 us -> 32.5 us
    ppermute x3, waiting for transfers between devices: 20.6 us -> 27.4 us  [shards(): sent.append(lax.ppermute(oth, both, swap))]
    pallas_call x6 -> x5, Pallas kernels: 36.2 us -> 31.4 us  [the longest x2 26.3 us: conv_chunks(): pl.pallas_call(functools.partial(conv_kernel, starts), grid_spec=pltpu.Pr...]
    pallas_call x1, Pallas kernels: 11.2 us -> 7.49 us  [halo_sums(): pl.pallas_call(halo_kernel, grid_spec=pltpu.PrefetchScalarGridSpec(num_sc...]
  transfers between devices with their start and end apart: 11 -> 11, of which waited for: 7 -> 8; matrix products, arithmetic and copies ran while one was open for 0% -> 0% of each run, Pallas kernels for 45% -> 43%
where the time goes in v3:
time: 116 us
  Pallas kernels  67.7 us (58%)
  waiting for transfers between devices  32.5 us (28%)
  starting transfers between devices  13.8 us (12%)
  local copies, waits for them, and re-layouts  1.33 us (1%)
    pallas_call x3, Pallas kernels, epi_chunk(): pl.pallas_call(functools.partial(epi_kernel, tuple(pieces), v0, v1, int(p...  28.8 us
    ppermute x3, waiting for transfers between devices, shards(): sent.append(lax.ppermute(oth, both, swap))  27.4 us
    pallas_call x2, Pallas kernels, conv_chunks(): pl.pallas_call(functools.partial(conv_kernel, starts), grid_spec=pltpu.Pr...  26.3 us
    ppermute x3, starting transfers between devices, shards(): sent.append(lax.ppermute(oth, both, swap))  7.75 us
    pallas_call x1, Pallas kernels, halo_sums(): pl.pallas_call(halo_kernel, grid_spec=pltpu.PrefetchScalarGridSpec(num_sc...  7.49 us
    ppermute x6, waiting for transfers between devices, shards(): flipped = [lax.ppermute(g, 'view', core) for g in give]  5.16 us
    pallas_call x3, Pallas kernels, norm_chunk(): pl.pallas_call(functools.partial(norm_kernel, lo), in_specs=[pl.BlockSpec...  5.12 us
  transfers between devices with their start and end apart: 11, of which 8 were waited for; matrix products, arithmetic and copies ran while one was open for 0% of the time, Pallas kernels for 43%

profile of v3, /device:TPU:121, one launch (start us, length us, event | category | flops | bytes accessed | tf_op | source)
XLA Modules:
  0.0 115.7 jit_solution(9075382775588204702)
XLA Ops:
  0.0 0.1 stack.20.view_ref.place_ref
  0.1 0.0 copy-start
  0.1 1.1 copy-done
  1.2 7.5 %halo.1 = (bf16[3,12,128,128]{3,2,1,0:T(8,128)(2,1)S(1)}, bf16[3,12,128,128]{3,2,1,0:T(8,128)(2,1)S(1)}) custom-call(s32[5]{0:T(128)S(1)} %stack.20.view_ref.place_ref, bf16[3,12,8,256,128]{4,3,2,1,0:T(8,128)(2,1)} %x_ref.3, bf16[3,12,8,256,128]{4,3,2,1,0:T(8,128)(2,1)} %x_ref.3, bf16[5,5,128,128]{3,2,1,0:T(8,128)(2,1)S(1)} %copy-done), custom_call_target="tpu_custom_call" | custom-call | flops 1000 | bytes 1000 | tf_op jit(solution)/shard_map/halo/pallas_call | solution.py:73
  8.7 1.9 %collective-permute-start.3 = (bf16[3,12,128,128]{3,2,1,0:T(8,128)(2,1)S(1)}, bf16[3,12,128,128]{3,2,1,0:T(8,128)(2,1)S(1)}, u32[]{:S(2)}, u32[]{:S(2)}) collective-permute-start(bf16[3,12,128,128]{3,2,1,0:T(8,128)(2,1)S(1)} %get-tuple-element.39), channel_id=1, source_target_pairs={{1,64},{2,65},{3,66},{4,67},{5,68},{6,69},{7,70},{8,71},{9,72},{10... | collective-permute-start | bytes 3538952 | tf_op jit(solution)/shard_map/ppermute | solution.py:331
  10.7 2.0 %collective-permute-start.2 = (bf16[3,12,128,128]{3,2,1,0:T(8,128)(2,1)S(1)}, bf16[3,12,128,128]{3,2,1,0:T(8,128)(2,1)S(1)}, u32[]{:S(2)}, u32[]{:S(2)}) collective-permute-start(bf16[3,12,128,128]{3,2,1,0:T(8,128)(2,1)S(1)} %get-tuple-element.30), channel_id=1, source_target_pairs={{0,1},{1,2},{2,3},{3,4},{4,5},{5,6},{6,7},{7,8},{8,9},{9,10},{10,1... | collective-permute-start | bytes 3538952 | tf_op jit(solution)/shard_map/ppermute | solution.py:330
  12.7 9.4 %conv.2 = (bf16[2,3,4,128,128]{4,3,2,1,0:T(8,128)(2,1)S(1)}, bf16[2,3,4,128,128]{4,3,2,1,0:T(8,128)(2,1)S(1)}) custom-call(s32[5]{0:T(128)S(1)} %stack.20.view_ref.place_ref, bf16[3,12,8,256,128]{4,3,2,1,0:T(8,128)(2,1)} %x_ref.3, bf16[5,5,128,128]{3,2,1,0:T(8,128)(2,1)S(1)} %copy-done), custom_call_target="tpu_custom_call" | custom-call | flops 1000 | bytes 1000 | tf_op jit(solution)/shard_map/conv/pallas_call | solution.py:155
  22.1 4.7 %collective-permute-start.1 = (bf16[2,3,4,128,128]{4,3,2,1,0:T(8,128)(2,1)S(1)}, bf16[2,3,4,128,128]{4,3,2,1,0:T(8,128)(2,1)S(1)}, u32[]{:S(2)}, u32[]{:S(2)}) collective-permute-start(bf16[2,3,4,128,128]{4,3,2,1,0:T(8,128)(2,1)S(1)} %get-tuple-element.36), channel_id=1, source_target_pairs={{0,64},{1,65},{2,66},{3,67},{4,68},{5,69},{6,70},{7,71},{8,72},{9,... | collective-permute-start | bytes 2359304 | tf_op jit(solution)/shard_map/ppermute | solution.py:339
  26.8 0.0 copy-start.1
  26.8 0.0 copy-start.3
  26.8 16.9 %conv.3 = (bf16[2,3,5,128,128]{4,3,2,1,0:T(8,128)(2,1)S(1)}, bf16[2,3,5,128,128]{4,3,2,1,0:T(8,128)(2,1)S(1)}, bf16[2,3,3,128,128]{4,3,2,1,0:T(8,128)(2,1)S(1)}, bf16[2,3,3,128,128]{4,3,2,1,0:T(8,128)(2,1)S(1)}) custom-call(s32[5]{0:T(128)S(1)} %stack.20.view_ref.place_ref, bf16[3,12,8,256,128]{4,3,2,1,0:T(8,128)(2,1)} %x_ref.3, ...), custom_call_target="tpu_custom_call" | custom-call | flops 1000 | bytes 1000 | tf_op jit(solution)/shard_map/conv/pallas_call | solution.py:155
  43.7 0.1 collective-permute-start
  43.8 2.9 %collective-permute-start.8 = (bf16[2,3,3,128,128]{4,3,2,1,0:T(8,128)(2,1)S(1)}, bf16[2,3,3,128,128]{4,3,2,1,0:T(8,128)(2,1)S(1)}, u32[]{:S(2)}, u32[]{:S(2)}) collective-permute-start(bf16[2,3,3,128,128]{4,3,2,1,0:T(8,128)(2,1)S(1)} %get-tuple-element.48), channel_id=1, source_target_pairs={{0,64},{1,65},{2,66},{3,67},{4,68},{5,69},{6,70},{7,71},{8,72},{9,... | collective-permute-start | bytes 1769480 | tf_op jit(solution)/shard_map/ppermute | solution.py:339
  46.8 18.3 %collective-permute-done.1.oth_ref = bf16[2,3,4,128,128]{4,3,2,1,0:T(8,128)(2,1)S(1)} collective-permute-done((bf16[2,3,4,128,128]{4,3,2,1,0:T(8,128)(2,1)S(1)}, bf16[2,3,4,128,128]{4,3,2,1,0:T(8,128)(2,1)S(1)}, u32[]{:S(2)}, u32[]{:S(2)}) %collective-permute-start.1) | collective-permute-done | bytes 786464 | tf_op jit(solution)/shard_map/ppermute | solution.py:339
  65.1 0.0 collective-permute-done.3.h2_ref
  65.1 0.0 collective-permute-done.2.h1_ref
  65.1 0.0 copy-done.1
  65.1 0.0 copy-done.3
  65.1 0.0 copy-start.4
  65.1 1.7 %norm.3 = (bf16[2,3,4,128,128]{4,3,2,1,0:T(8,128)(2,1)S(1)}, bf16[3,4,128,128]{3,2,1,0:T(8,128)(2,1)S(1)}, bf16[3,4,128,128]{3,2,1,0:T(8,128)(2,1)S(1)}) custom-call(s32[5]{0:T(128)S(1)} %stack.20.view_ref.place_ref, bf16[2,3,4,128,128]{4,3,2,1,0:T(8,128)(2,1)S(1)} %get-tuple-element.32.own_ref, ...), custom_call_target="tpu_custom_call" | custom-call | flops 1000 | bytes 1000 | tf_op jit(solution)/shard_map/norm/pallas_call | solution.py:201
  66.8 0.7 collective-permute-start.4
  67.5 0.1 collective-permute-start.5
  67.6 0.0 copy-done.4
  67.6 0.1 slice_bitcast_fusion
  67.7 0.0 copy-start.2
  67.7 0.1 pad_maximum_fusion.refs_3_.refs_6_
  67.7 0.1 fusion.2
  67.8 1.0 collective-permute-done.4.refs_1_
  68.8 0.6 collective-permute-done.5.refs_2_
  69.4 0.0 copy-done.2
  69.4 7.6 %epi.3.refs_9_ = bf16[12,12,1,128,128]{4,3,2,1,0:T(8,128)(2,1)} custom-call(s32[5]{0:T(128)S(1)} %stack.20.view_ref.place_ref, bf16[2,3,4,128,128]{4,3,2,1,0:T(8,128)(2,1)S(1)} %get-tuple-element.40.refs_0_, bf16[3,4,128,128]{3,2,1,0:T(8,128)(2,1)S(1)} %collective-permute-done.4.refs_1_, bf16[3,4,128,128]{3,2,1,0:T(8,128)(2,1)S(1)} %collective-permute-done.5.refs_2_, ...), custom_call_target="tpu_custom_call" | custom-call | flops 1000 | bytes 1000 | tf_op jit(solution)/shard_map/epi/pallas_call | solution.py:287
  77.0 9.1 %collective-permute-done.oth_ref = bf16[2,3,5,128,128]{4,3,2,1,0:T(8,128)(2,1)S(1)} collective-permute-done((bf16[2,3,5,128,128]{4,3,2,1,0:T(8,128)(2,1)S(1)}, bf16[2,3,5,128,128]{4,3,2,1,0:T(8,128)(2,1)S(1)}, u32[]{:S(2)}, u32[]{:S(2)}) %collective-permute-start) | collective-permute-done | bytes 983072 | tf_op jit(solution)/shard_map/ppermute | solution.py:339
  86.1 2.0 %norm.4 = (bf16[2,3,5,128,128]{4,3,2,1,0:T(8,128)(2,1)S(1)}, bf16[3,5,128,128]{3,2,1,0:T(8,128)(2,1)S(1)}, bf16[3,5,128,128]{3,2,1,0:T(8,128)(2,1)S(1)}) custom-call(s32[5]{0:T(128)S(1)} %stack.20.view_ref.place_ref, bf16[2,3,5,128,128]{4,3,2,1,0:T(8,128)(2,1)S(1)} %get-tuple-element.34.own_ref, ...), custom_call_target="tpu_custom_call" | custom-call | flops 1000 | bytes 1000 | tf_op jit(solution)/shard_map/norm/pallas_call | solution.py:201
  88.1 0.7 collective-permute-start.6
  88.8 0.1 collective-permute-start.7
  88.9 1.4 %collective-permute-done.6.refs_4_.refs_1_ = bf16[3,5,128,128]{3,2,1,0:T(8,128)(2,1)S(1)} collective-permute-done((bf16[3,5,128,128]{3,2,1,0:T(8,128)(2,1)S(1)}, bf16[3,5,128,128]{3,2,1,0:T(8,128)(2,1)S(1)}, u32[]{:S(2)}, u32[]{:S(2)}) %collective-permute-start.6) | collective-permute-done | bytes 491552 | tf_op jit(solution)/shard_map/ppermute | solution.py:351
  90.3 0.7 collective-permute-done.7.refs_5_.refs_2_
  91.0 11.5 %epi.4.refs_9_ = bf16[12,12,1,128,128]{4,3,2,1,0:T(8,128)(2,1)} custom-call(s32[5]{0:T(128)S(1)} %stack.20.view_ref.place_ref, bf16[2,3,4,128,128]{4,3,2,1,0:T(8,128)(2,1)S(1)} %get-tuple-element.40.refs_0_, bf16[3,4,128,128]{3,2,1,0:T(8,128)(2,1)S(1)} %collective-permute-done.4.refs_1_, ...), custom_call_target="tpu_custom_call", output_to_operand_aliasing={{}: (10, {})} | custom-call | flops 1000 | bytes 1000 | tf_op jit(solution)/shard_map/epi/pallas_call | solution.py:287
  102.5 0.0 collective-permute-done.8.oth_ref
  102.5 1.4 %norm.5 = (bf16[2,3,3,128,128]{4,3,2,1,0:T(8,128)(2,1)S(1)}, bf16[3,3,128,128]{3,2,1,0:T(8,128)(2,1)S(1)}, bf16[3,3,128,128]{3,2,1,0:T(8,128)(2,1)S(1)}) custom-call(s32[5]{0:T(128)S(1)} %stack.20.view_ref.place_ref, bf16[2,3,3,128,128]{4,3,2,1,0:T(8,128)(2,1)S(1)} %get-tuple-element.47.own_ref, ...), custom_call_target="tpu_custom_call" | custom-call | flops 1000 | bytes 1000 | tf_op jit(solution)/shard_map/norm/pallas_call | solution.py:201
  104.0 0.5 collective-permute-start.9
  104.4 0.1 collective-permute-start.10
  104.5 1.1 collective-permute-done.9.refs_4_
  105.6 0.4 collective-permute-done.10.refs_5_
  106.1 9.6 %epi.5 = bf16[12,12,1,128,128]{4,3,2,1,0:T(8,128)(2,1)} custom-call(s32[5]{0:T(128)S(1)} %stack.20.view_ref.place_ref, bf16[2,3,5,128,128]{4,3,2,1,0:T(8,128)(2,1)S(1)} %get-tuple-element.44.refs_3_.refs_0_, bf16[3,5,128,128]{3,2,1,0:T(8,128)(2,1)S(1)} %collective-permute-done.6.refs_4_.refs_1_, ...), custom_call_target="tpu_custom_call", output_to_operand_aliasing={{}: (10, {})} | custom-call | flops 1000 | bytes 1000 | tf_op jit(solution)/shard_map/epi/pallas_call | solution.py:287
Async XLA Ops:
  0.1 1.1 copy-start
  8.7 56.3 %collective-permute-start.3 = (bf16[3,12,128,128]{3,2,1,0:T(8,128)(2,1)S(1)}, bf16[3,12,128,128]{3,2,1,0:T(8,128)(2,1)S(1)}, u32[]{:S(2)}, u32[]{:S(2)}) collective-permute-start(bf16[3,12,128,128]{3,2,1,0:T(8,128)(2,1)S(1)} %get-tuple-element.39), channel_id=1, source_target_pairs={{1,64},{2,65},{3,66},{4,67},{5,68},{6,69},{7,70},{8,71},{9,72},{10... | collective-permute-start | bytes 3538952 | tf_op jit(solution)/shard_map/ppermute | solution.py:331
  10.7 54.4 %collective-permute-start.2 = (bf16[3,12,128,128]{3,2,1,0:T(8,128)(2,1)S(1)}, bf16[3,12,128,128]{3,2,1,0:T(8,128)(2,1)S(1)}, u32[]{:S(2)}, u32[]{:S(2)}) collective-permute-start(bf16[3,12,128,128]{3,2,1,0:T(8,128)(2,1)S(1)} %get-tuple-element.30), channel_id=1, source_target_pairs={{0,1},{1,2},{2,3},{3,4},{4,5},{5,6},{6,7},{7,8},{8,9},{9,10},{10,1... | collective-permute-start | bytes 3538952 | tf_op jit(solution)/shard_map/ppermute | solution.py:330
  22.1 42.9 %collective-permute-start.1 = (bf16[2,3,4,128,128]{4,3,2,1,0:T(8,128)(2,1)S(1)}, bf16[2,3,4,128,128]{4,3,2,1,0:T(8,128)(2,1)S(1)}, u32[]{:S(2)}, u32[]{:S(2)}) collective-permute-start(bf16[2,3,4,128,128]{4,3,2,1,0:T(8,128)(2,1)S(1)} %get-tuple-element.36), channel_id=1, source_target_pairs={{0,64},{1,65},{2,66},{3,67},{4,68},{5,69},{6,70},{7,71},{8,72},{9,... | collective-permute-start | bytes 2359304 | tf_op jit(solution)/shard_map/ppermute | solution.py:339
  26.8 38.2 %copy-start.1 = (f32[128,128]{1,0:T(8,128)S(1)}, f32[128,128]{1,0:T(8,128)}, u32[]{:S(2)}) copy-start(f32[128,128]{1,0:T(8,128)} %mix_ref.5) | copy-start | bytes 196612
  26.8 38.2 %copy-start.3 = (f32[128]{0:T(128)S(1)}, f32[128]{0:T(128)}, u32[]{:S(2)}) copy-start(f32[128]{0:T(128)} %param.8) | copy-start | bytes 1540
  43.7 42.4 %collective-permute-start = (bf16[2,3,5,128,128]{4,3,2,1,0:T(8,128)(2,1)S(1)}, bf16[2,3,5,128,128]{4,3,2,1,0:T(8,128)(2,1)S(1)}, u32[]{:S(2)}, u32[]{:S(2)}) collective-permute-start(bf16[2,3,5,128,128]{4,3,2,1,0:T(8,128)(2,1)S(1)} %get-tuple-element.35), channel_id=1, source_target_pairs={{0,64},{1,65},{2,66},{3,67},{4,68},{5,69},{6,70},{7,71},{8,72},{9,... | collective-permute-start | bytes 2949128 | tf_op jit(solution)/shard_map/ppermute | solution.py:339
  43.8 58.7 %collective-permute-start.8 = (bf16[2,3,3,128,128]{4,3,2,1,0:T(8,128)(2,1)S(1)}, bf16[2,3,3,128,128]{4,3,2,1,0:T(8,128)(2,1)S(1)}, u32[]{:S(2)}, u32[]{:S(2)}) collective-permute-start(bf16[2,3,3,128,128]{4,3,2,1,0:T(8,128)(2,1)S(1)} %get-tuple-element.48), channel_id=1, source_target_pairs={{0,64},{1,65},{2,66},{3,67},{4,68},{5,69},{6,70},{7,71},{8,72},{9,... | collective-permute-start | bytes 1769480 | tf_op jit(solution)/shard_map/ppermute | solution.py:339
  65.1 2.5 %copy-start.4 = (bf16[3,3,3,128,128]{4,3,2,1,0:T(8,128)(2,1)S(1)}, bf16[3,3,3,128,128]{4,3,2,1,0:T(8,128)(2,1)}, u32[]{:S(2)}) copy-start(bf16[3,3,3,128,128]{4,3,2,1,0:T(8,128)(2,1)} %param.10) | copy-start | bytes 2654212
  66.8 2.0 %collective-permute-start.4 = (bf16[3,4,128,128]{3,2,1,0:T(8,128)(2,1)S(1)}, bf16[3,4,128,128]{3,2,1,0:T(8,128)(2,1)S(1)}, u32[]{:S(2)}, u32[]{:S(2)}) collective-permute-start(bf16[3,4,128,128]{3,2,1,0:T(8,128)(2,1)S(1)} %get-tuple-element.41), channel_id=1, source_target_pairs={{0,32},{32,0},{64,96},{96,64},{1,33},{33,1},{65,97},{97,65},{2,34}... | collective-permute-start | bytes 1179656 | tf_op jit(solution)/shard_map/ppermute | solution.py:351
  67.5 1.9 %collective-permute-start.5 = (bf16[3,4,128,128]{3,2,1,0:T(8,128)(2,1)S(1)}, bf16[3,4,128,128]{3,2,1,0:T(8,128)(2,1)S(1)}, u32[]{:S(2)}, u32[]{:S(2)}) collective-permute-start(bf16[3,4,128,128]{3,2,1,0:T(8,128)(2,1)S(1)} %get-tuple-element.42), channel_id=1, source_target_pairs={{0,32},{32,0},{64,96},{96,64},{1,33},{33,1},{65,97},{97,65},{2,34}... | collective-permute-start | bytes 1179656 | tf_op jit(solution)/shard_map/ppermute | solution.py:351
  67.7 1.7 %copy-start.2 = (f32[128]{0:T(128)S(1)}, f32[128]{0:T(128)}, u32[]{:S(2)}) copy-start(f32[128]{0:T(128)} %param.11) | copy-start | bytes 1540
  88.1 2.2 %collective-permute-start.6 = (bf16[3,5,128,128]{3,2,1,0:T(8,128)(2,1)S(1)}, bf16[3,5,128,128]{3,2,1,0:T(8,128)(2,1)S(1)}, u32[]{:S(2)}, u32[]{:S(2)}) collective-permute-start(bf16[3,5,128,128]{3,2,1,0:T(8,128)(2,1)S(1)} %get-tuple-element.45), channel_id=1, source_target_pairs={{0,32},{32,0},{64,96},{96,64},{1,33},{33,1},{65,97},{97,65},{2,34}... | collective-permute-start | bytes 1474568 | tf_op jit(solution)/shard_map/ppermute | solution.py:351
  88.8 2.2 %collective-permute-start.7 = (bf16[3,5,128,128]{3,2,1,0:T(8,128)(2,1)S(1)}, bf16[3,5,128,128]{3,2,1,0:T(8,128)(2,1)S(1)}, u32[]{:S(2)}, u32[]{:S(2)}) collective-permute-start(bf16[3,5,128,128]{3,2,1,0:T(8,128)(2,1)S(1)} %get-tuple-element.46), channel_id=1, source_target_pairs={{0,32},{32,0},{64,96},{96,64},{1,33},{33,1},{65,97},{97,65},{2,34}... | collective-permute-start | bytes 1474568 | tf_op jit(solution)/shard_map/ppermute | solution.py:351
  104.0 1.7 %collective-permute-start.9 = (bf16[3,3,128,128]{3,2,1,0:T(8,128)(2,1)S(1)}, bf16[3,3,128,128]{3,2,1,0:T(8,128)(2,1)S(1)}, u32[]{:S(2)}, u32[]{:S(2)}) collective-permute-start(bf16[3,3,128,128]{3,2,1,0:T(8,128)(2,1)S(1)} %get-tuple-element.52), channel_id=1, source_target_pairs={{0,32},{32,0},{64,96},{96,64},{1,33},{33,1},{65,97},{97,65},{2,34}... | collective-permute-start | bytes 884744 | tf_op jit(solution)/shard_map/ppermute | solution.py:351
  104.4 1.6 %collective-permute-start.10 = (bf16[3,3,128,128]{3,2,1,0:T(8,128)(2,1)S(1)}, bf16[3,3,128,128]{3,2,1,0:T(8,128)(2,1)S(1)}, u32[]{:S(2)}, u32[]{:S(2)}) collective-permute-start(bf16[3,3,128,128]{3,2,1,0:T(8,128)(2,1)S(1)} %get-tuple-element.53), channel_id=1, source_target_pairs={{0,32},{32,0},{64,96},{96,64},{1,33},{33,1},{65,97},{97,65},{2,34}... | collective-permute-start | bytes 884744 | tf_op jit(solution)/shard_map/ppermute | solution.py:351

commit v4 on v3

--- a/solution.py
+++ b/solution.py
@@ -336,8 +336,11 @@
         done = conv_chunks(turn, features, analysis_kernel, spans)
         for own, oth in zip(done[::2], done[1::2]):
             rows.append(own)
-            sent.append(lax.ppermute(oth, both, swap))
+            sent.append(oth)
         last = done[0]
+    sent[0] = lax.ppermute(sent[0], both, swap)
+    sent[1], h1, h2 = lax.optimization_barrier((sent[1], h1, h2))
+    sent[1] = lax.ppermute(sent[1], both, swap)
     sources = []
     out = None
     done = 0
@@ -353,6 +356,9 @@
         upto = V if hi == V else hi - 1
         out = epi_chunk(place, sources, CHUNKS[:i + 1], done, upto, out, em, ee, bias, total, V)
         done = upto
+        if i + 2 < len(CHUNKS):
+            later, out = lax.optimization_barrier((sent[i + 2], out))
+            sent[i + 2] = lax.ppermute(later, both, swap)
     return out
 
 

time: 116 us -> 116 us (level)
  waiting for transfers between devices: 32.5 us -> 35.1 us
  starting transfers between devices: 13.8 us -> 11.3 us
    ppermute x3, starting transfers between devices: 7.75 us -> 5.19 us  [the longest x1 4.7 us: shards(): sent[0] = lax.ppermute(sent[0], both, swap)]
    ppermute x3, waiting for transfers between devices: 27.4 us -> 29.9 us  [the longest x1 20.9 us: shards(): sent[0] = lax.ppermute(sent[0], both, swap)]
where the time goes in v4:
time: 116 us
  Pallas kernels  67.7 us (58%)
  waiting for transfers between devices  35.1 us (30%)
  starting transfers between devices  11.3 us (10%)
  local copies, waits for them, and re-layouts  1.33 us (1%)
    pallas_call x3, Pallas kernels, epi_chunk(): pl.pallas_call(functools.partial(epi_kernel, tuple(pieces), v0, v1, int(p...  28.8 us
    pallas_call x2, Pallas kernels, conv_chunks(): pl.pallas_call(functools.partial(conv_kernel, starts), grid_spec=pltpu.Pr...  26.3 us
    ppermute x1, waiting for transfers between devices, shards(): sent[0] = lax.ppermute(sent[0], both, swap)  20.9 us
    ppermute x1, waiting for transfers between devices, shards(): sent[1] = lax.ppermute(sent[1], both, swap)  9.01 us
    pallas_call x1, Pallas kernels, halo_sums(): pl.pallas_call(halo_kernel, grid_spec=pltpu.PrefetchScalarGridSpec(num_sc...  7.49 us
    ppermute x6, waiting for transfers between devices, shards(): flipped = [lax.ppermute(g, 'view', core) for g in give]  5.16 us
    pallas_call x3, Pallas kernels, norm_chunk(): pl.pallas_call(functools.partial(norm_kernel, lo), in_specs=[pl.BlockSpec...  5.12 us
    ppermute x1, starting transfers between devices, shards(): sent[0] = lax.ppermute(sent[0], both, swap)  4.7 us
  transfers between devices with their start and end apart: 11, of which 8 were waited for; matrix products, arithmetic and copies ran while one was open for 0% of the time, Pallas kernels for 43%

profile of v4, /device:TPU:121, one launch (start us, length us, event | category | flops | bytes accessed | tf_op | source)
XLA Modules:
  0.0 115.7 jit_solution(477366007100994956)
XLA Ops:
  0.0 0.1 stack.20.view_ref.place_ref
  0.1 0.0 copy-start
  0.1 1.1 copy-done
  1.2 7.5 %halo.1 = (bf16[3,12,128,128]{3,2,1,0:T(8,128)(2,1)S(1)}, bf16[3,12,128,128]{3,2,1,0:T(8,128)(2,1)S(1)}) custom-call(s32[5]{0:T(128)S(1)} %stack.20.view_ref.place_ref, bf16[3,12,8,256,128]{4,3,2,1,0:T(8,128)(2,1)} %x_ref.3, bf16[3,12,8,256,128]{4,3,2,1,0:T(8,128)(2,1)} %x_ref.3, bf16[5,5,128,128]{3,2,1,0:T(8,128)(2,1)S(1)} %copy-done), custom_call_target="tpu_custom_call" | custom-call | flops 1000 | bytes 1000 | tf_op jit(solution)/shard_map/halo/pallas_call | solution.py:73
  8.7 1.9 %collective-permute-start.1 = (bf16[3,12,128,128]{3,2,1,0:T(8,128)(2,1)S(1)}, bf16[3,12,128,128]{3,2,1,0:T(8,128)(2,1)S(1)}, u32[]{:S(2)}, u32[]{:S(2)}) collective-permute-start(bf16[3,12,128,128]{3,2,1,0:T(8,128)(2,1)S(1)} %get-tuple-element.41), channel_id=1, source_target_pairs={{1,64},{2,65},{3,66},{4,67},{5,68},{6,69},{7,70},{8,71},{9,72},{10... | collective-permute-start | bytes 3538952 | tf_op jit(solution)/shard_map/ppermute | solution.py:331
  10.7 2.0 %collective-permute-start = (bf16[3,12,128,128]{3,2,1,0:T(8,128)(2,1)S(1)}, bf16[3,12,128,128]{3,2,1,0:T(8,128)(2,1)S(1)}, u32[]{:S(2)}, u32[]{:S(2)}) collective-permute-start(bf16[3,12,128,128]{3,2,1,0:T(8,128)(2,1)S(1)} %get-tuple-element.35), channel_id=1, source_target_pairs={{0,1},{1,2},{2,3},{3,4},{4,5},{5,6},{6,7},{7,8},{8,9},{9,10},{10,1... | collective-permute-start | bytes 3538952 | tf_op jit(solution)/shard_map/ppermute | solution.py:330
  12.7 9.4 %conv.2 = (bf16[2,3,4,128,128]{4,3,2,1,0:T(8,128)(2,1)S(1)}, bf16[2,3,4,128,128]{4,3,2,1,0:T(8,128)(2,1)S(1)}) custom-call(s32[5]{0:T(128)S(1)} %stack.20.view_ref.place_ref, bf16[3,12,8,256,128]{4,3,2,1,0:T(8,128)(2,1)} %x_ref.3, bf16[5,5,128,128]{3,2,1,0:T(8,128)(2,1)S(1)} %copy-done), custom_call_target="tpu_custom_call" | custom-call | flops 1000 | bytes 1000 | tf_op jit(solution)/shard_map/conv/pallas_call | solution.py:155
  22.1 4.7 %collective-permute-start.3 = (bf16[2,3,4,128,128]{4,3,2,1,0:T(8,128)(2,1)S(1)}, bf16[2,3,4,128,128]{4,3,2,1,0:T(8,128)(2,1)S(1)}, u32[]{:S(2)}, u32[]{:S(2)}) collective-permute-start(bf16[2,3,4,128,128]{4,3,2,1,0:T(8,128)(2,1)S(1)} %get-tuple-element.44), channel_id=1, source_target_pairs={{0,64},{1,65},{2,66},{3,67},{4,68},{5,69},{6,70},{7,71},{8,72},{9,... | collective-permute-start | bytes 2359304 | tf_op jit(solution)/shard_map/ppermute | solution.py:341
  26.8 0.0 copy-start.1
  26.8 0.0 copy-start.3
  26.8 16.9 %conv.3 = (bf16[2,3,5,128,128]{4,3,2,1,0:T(8,128)(2,1)S(1)}, bf16[2,3,5,128,128]{4,3,2,1,0:T(8,128)(2,1)S(1)}, bf16[2,3,3,128,128]{4,3,2,1,0:T(8,128)(2,1)S(1)}, bf16[2,3,3,128,128]{4,3,2,1,0:T(8,128)(2,1)S(1)}) custom-call(s32[5]{0:T(128)S(1)} %stack.20.view_ref.place_ref, bf16[3,12,8,256,128]{4,3,2,1,0:T(8,128)(2,1)} %x_ref.3, ...), custom_call_target="tpu_custom_call" | custom-call | flops 1000 | bytes 1000 | tf_op jit(solution)/shard_map/conv/pallas_call | solution.py:155
  43.7 0.0 collective-permute-done.1.h2_ref
  43.7 0.0 collective-permute-done.h1_ref
  43.8 0.4 collective-permute-start.2
  44.2 20.9 %collective-permute-done.3.oth_ref = bf16[2,3,4,128,128]{4,3,2,1,0:T(8,128)(2,1)S(1)} collective-permute-done((bf16[2,3,4,128,128]{4,3,2,1,0:T(8,128)(2,1)S(1)}, bf16[2,3,4,128,128]{4,3,2,1,0:T(8,128)(2,1)S(1)}, u32[]{:S(2)}, u32[]{:S(2)}) %collective-permute-start.3) | collective-permute-done | bytes 786464 | tf_op jit(solution)/shard_map/ppermute | solution.py:341
  65.1 0.0 copy-done.1
  65.1 0.0 copy-done.3
  65.1 0.0 copy-start.4
  65.1 1.7 %norm.3 = (bf16[2,3,4,128,128]{4,3,2,1,0:T(8,128)(2,1)S(1)}, bf16[3,4,128,128]{3,2,1,0:T(8,128)(2,1)S(1)}, bf16[3,4,128,128]{3,2,1,0:T(8,128)(2,1)S(1)}) custom-call(s32[5]{0:T(128)S(1)} %stack.20.view_ref.place_ref, bf16[2,3,4,128,128]{4,3,2,1,0:T(8,128)(2,1)S(1)} %get-tuple-element.37.own_ref, ...), custom_call_target="tpu_custom_call" | custom-call | flops 1000 | bytes 1000 | tf_op jit(solution)/shard_map/norm/pallas_call | solution.py:201
  66.8 0.7 collective-permute-start.4
  67.4 0.1 collective-permute-start.5
  67.5 0.0 copy-done.4
  67.5 0.1 slice_bitcast_fusion
  67.6 0.0 copy-start.2
  67.6 0.1 fusion.2
  67.7 0.1 pad_maximum_fusion.refs_3_.refs_6_
  67.8 1.0 collective-permute-done.4.refs_1_
  68.8 0.6 collective-permute-done.5.refs_2_
  69.4 0.0 copy-done.2
  69.4 7.6 %epi.3.refs_9_ = bf16[12,12,1,128,128]{4,3,2,1,0:T(8,128)(2,1)} custom-call(s32[5]{0:T(128)S(1)} %stack.20.view_ref.place_ref, bf16[2,3,4,128,128]{4,3,2,1,0:T(8,128)(2,1)S(1)} %get-tuple-element.49.refs_0_, bf16[3,4,128,128]{3,2,1,0:T(8,128)(2,1)S(1)} %collective-permute-done.4.refs_1_, bf16[3,4,128,128]{3,2,1,0:T(8,128)(2,1)S(1)} %collective-permute-done.5.refs_2_, ...), custom_call_target="tpu_custom_call" | custom-call | flops 1000 | bytes 1000 | tf_op jit(solution)/shard_map/epi/pallas_call | solution.py:287
  77.0 0.1 collective-permute-start.8
  77.1 9.0 %collective-permute-done.2.oth_ref = bf16[2,3,5,128,128]{4,3,2,1,0:T(8,128)(2,1)S(1)} collective-permute-done((bf16[2,3,5,128,128]{4,3,2,1,0:T(8,128)(2,1)S(1)}, bf16[2,3,5,128,128]{4,3,2,1,0:T(8,128)(2,1)S(1)}, u32[]{:S(2)}, u32[]{:S(2)}) %collective-permute-start.2) | collective-permute-done | bytes 983072 | tf_op jit(solution)/shard_map/ppermute | solution.py:343
  86.1 2.0 %norm.4 = (bf16[2,3,5,128,128]{4,3,2,1,0:T(8,128)(2,1)S(1)}, bf16[3,5,128,128]{3,2,1,0:T(8,128)(2,1)S(1)}, bf16[3,5,128,128]{3,2,1,0:T(8,128)(2,1)S(1)}) custom-call(s32[5]{0:T(128)S(1)} %stack.20.view_ref.place_ref, bf16[2,3,5,128,128]{4,3,2,1,0:T(8,128)(2,1)S(1)} %get-tuple-element.39.own_ref, ...), custom_call_target="tpu_custom_call" | custom-call | flops 1000 | bytes 1000 | tf_op jit(solution)/shard_map/norm/pallas_call | solution.py:201
  88.1 0.7 collective-permute-start.6
  88.8 0.1 collective-permute-start.7
  88.9 1.4 %collective-permute-done.6.refs_4_.refs_1_ = bf16[3,5,128,128]{3,2,1,0:T(8,128)(2,1)S(1)} collective-permute-done((bf16[3,5,128,128]{3,2,1,0:T(8,128)(2,1)S(1)}, bf16[3,5,128,128]{3,2,1,0:T(8,128)(2,1)S(1)}, u32[]{:S(2)}, u32[]{:S(2)}) %collective-permute-start.6) | collective-permute-done | bytes 491552 | tf_op jit(solution)/shard_map/ppermute | solution.py:354
  90.3 0.7 collective-permute-done.7.refs_5_.refs_2_
  91.0 11.5 %epi.4.refs_9_ = bf16[12,12,1,128,128]{4,3,2,1,0:T(8,128)(2,1)} custom-call(s32[5]{0:T(128)S(1)} %stack.20.view_ref.place_ref, bf16[2,3,4,128,128]{4,3,2,1,0:T(8,128)(2,1)S(1)} %get-tuple-element.49.refs_0_, bf16[3,4,128,128]{3,2,1,0:T(8,128)(2,1)S(1)} %collective-permute-done.4.refs_1_, ...), custom_call_target="tpu_custom_call", output_to_operand_aliasing={{}: (10, {})} | custom-call | flops 1000 | bytes 1000 | tf_op jit(solution)/shard_map/epi/pallas_call | solution.py:287
  102.5 0.0 collective-permute-done.8.oth_ref
  102.5 1.4 %norm.5 = (bf16[2,3,3,128,128]{4,3,2,1,0:T(8,128)(2,1)S(1)}, bf16[3,3,128,128]{3,2,1,0:T(8,128)(2,1)S(1)}, bf16[3,3,128,128]{3,2,1,0:T(8,128)(2,1)S(1)}) custom-call(s32[5]{0:T(128)S(1)} %stack.20.view_ref.place_ref, bf16[2,3,3,128,128]{4,3,2,1,0:T(8,128)(2,1)S(1)} %get-tuple-element.57.own_ref, ...), custom_call_target="tpu_custom_call" | custom-call | flops 1000 | bytes 1000 | tf_op jit(solution)/shard_map/norm/pallas_call | solution.py:201
  104.0 0.5 collective-permute-start.9
  104.4 0.1 collective-permute-start.10
  104.5 1.1 collective-permute-done.9.refs_4_
  105.6 0.4 collective-permute-done.10.refs_5_
  106.1 9.6 %epi.5 = bf16[12,12,1,128,128]{4,3,2,1,0:T(8,128)(2,1)} custom-call(s32[5]{0:T(128)S(1)} %stack.20.view_ref.place_ref, bf16[2,3,5,128,128]{4,3,2,1,0:T(8,128)(2,1)S(1)} %get-tuple-element.54.refs_3_.refs_0_, bf16[3,5,128,128]{3,2,1,0:T(8,128)(2,1)S(1)} %collective-permute-done.6.refs_4_.refs_1_, ...), custom_call_target="tpu_custom_call", output_to_operand_aliasing={{}: (10, {})} | custom-call | flops 1000 | bytes 1000 | tf_op jit(solution)/shard_map/epi/pallas_call | solution.py:287
Async XLA Ops:
  0.1 1.1 copy-start
  8.7 35.0 %collective-permute-start.1 = (bf16[3,12,128,128]{3,2,1,0:T(8,128)(2,1)S(1)}, bf16[3,12,128,128]{3,2,1,0:T(8,128)(2,1)S(1)}, u32[]{:S(2)}, u32[]{:S(2)}) collective-permute-start(bf16[3,12,128,128]{3,2,1,0:T(8,128)(2,1)S(1)} %get-tuple-element.41), channel_id=1, source_target_pairs={{1,64},{2,65},{3,66},{4,67},{5,68},{6,69},{7,70},{8,71},{9,72},{10... | collective-permute-start | bytes 3538952 | tf_op jit(solution)/shard_map/ppermute | solution.py:331
  10.7 33.1 %collective-permute-start = (bf16[3,12,128,128]{3,2,1,0:T(8,128)(2,1)S(1)}, bf16[3,12,128,128]{3,2,1,0:T(8,128)(2,1)S(1)}, u32[]{:S(2)}, u32[]{:S(2)}) collective-permute-start(bf16[3,12,128,128]{3,2,1,0:T(8,128)(2,1)S(1)} %get-tuple-element.35), channel_id=1, source_target_pairs={{0,1},{1,2},{2,3},{3,4},{4,5},{5,6},{6,7},{7,8},{8,9},{9,10},{10,1... | collective-permute-start | bytes 3538952 | tf_op jit(solution)/shard_map/ppermute | solution.py:330
  22.1 42.9 %collective-permute-start.3 = (bf16[2,3,4,128,128]{4,3,2,1,0:T(8,128)(2,1)S(1)}, bf16[2,3,4,128,128]{4,3,2,1,0:T(8,128)(2,1)S(1)}, u32[]{:S(2)}, u32[]{:S(2)}) collective-permute-start(bf16[2,3,4,128,128]{4,3,2,1,0:T(8,128)(2,1)S(1)} %get-tuple-element.44), channel_id=1, source_target_pairs={{0,64},{1,65},{2,66},{3,67},{4,68},{5,69},{6,70},{7,71},{8,72},{9,... | collective-permute-start | bytes 2359304 | tf_op jit(solution)/shard_map/ppermute | solution.py:341
  26.8 38.2 %copy-start.1 = (f32[128,128]{1,0:T(8,128)S(1)}, f32[128,128]{1,0:T(8,128)}, u32[]{:S(2)}) copy-start(f32[128,128]{1,0:T(8,128)} %mix_ref.5) | copy-start | bytes 196612
  26.8 38.2 %copy-start.3 = (f32[128]{0:T(128)S(1)}, f32[128]{0:T(128)}, u32[]{:S(2)}) copy-start(f32[128]{0:T(128)} %param.8) | copy-start | bytes 1540
  43.8 42.4 %collective-permute-start.2 = (bf16[2,3,5,128,128]{4,3,2,1,0:T(8,128)(2,1)S(1)}, bf16[2,3,5,128,128]{4,3,2,1,0:T(8,128)(2,1)S(1)}, u32[]{:S(2)}, u32[]{:S(2)}) collective-permute-start(bf16[2,3,5,128,128]{4,3,2,1,0:T(8,128)(2,1)S(1)} %get-tuple-element.42), channel_id=1, source_target_pairs={{0,64},{1,65},{2,66},{3,67},{4,68},{5,69},{6,70},{7,71},{8,72},{9,... | collective-permute-start | bytes 2949128 | tf_op jit(solution)/shard_map/ppermute | solution.py:343
  65.1 2.5 %copy-start.4 = (bf16[3,3,3,128,128]{4,3,2,1,0:T(8,128)(2,1)S(1)}, bf16[3,3,3,128,128]{4,3,2,1,0:T(8,128)(2,1)}, u32[]{:S(2)}) copy-start(bf16[3,3,3,128,128]{4,3,2,1,0:T(8,128)(2,1)} %param.10) | copy-start | bytes 2654212
  66.8 2.0 %collective-permute-start.4 = (bf16[3,4,128,128]{3,2,1,0:T(8,128)(2,1)S(1)}, bf16[3,4,128,128]{3,2,1,0:T(8,128)(2,1)S(1)}, u32[]{:S(2)}, u32[]{:S(2)}) collective-permute-start(bf16[3,4,128,128]{3,2,1,0:T(8,128)(2,1)S(1)} %get-tuple-element.50), channel_id=1, source_target_pairs={{0,32},{32,0},{64,96},{96,64},{1,33},{33,1},{65,97},{97,65},{2,34}... | collective-permute-start | bytes 1179656 | tf_op jit(solution)/shard_map/ppermute | solution.py:354
  67.4 1.9 %collective-permute-start.5 = (bf16[3,4,128,128]{3,2,1,0:T(8,128)(2,1)S(1)}, bf16[3,4,128,128]{3,2,1,0:T(8,128)(2,1)S(1)}, u32[]{:S(2)}, u32[]{:S(2)}) collective-permute-start(bf16[3,4,128,128]{3,2,1,0:T(8,128)(2,1)S(1)} %get-tuple-element.51), channel_id=1, source_target_pairs={{0,32},{32,0},{64,96},{96,64},{1,33},{33,1},{65,97},{97,65},{2,34}... | collective-permute-start | bytes 1179656 | tf_op jit(solution)/shard_map/ppermute | solution.py:354
  67.6 1.7 %copy-start.2 = (f32[128]{0:T(128)S(1)}, f32[128]{0:T(128)}, u32[]{:S(2)}) copy-start(f32[128]{0:T(128)} %param.11) | copy-start | bytes 1540
  77.0 25.5 %collective-permute-start.8 = (bf16[2,3,3,128,128]{4,3,2,1,0:T(8,128)(2,1)S(1)}, bf16[2,3,3,128,128]{4,3,2,1,0:T(8,128)(2,1)S(1)}, u32[]{:S(2)}, u32[]{:S(2)}) collective-permute-start(bf16[2,3,3,128,128]{4,3,2,1,0:T(8,128)(2,1)S(1)} %get-tuple-element.58), channel_id=1, source_target_pairs={{0,64},{1,65},{2,66},{3,67},{4,68},{5,69},{6,70},{7,71},{8,72},{9,... | collective-permute-start | bytes 1769480 | tf_op jit(solution)/shard_map/ppermute | solution.py:361
  88.1 2.2 %collective-permute-start.6 = (bf16[3,5,128,128]{3,2,1,0:T(8,128)(2,1)S(1)}, bf16[3,5,128,128]{3,2,1,0:T(8,128)(2,1)S(1)}, u32[]{:S(2)}, u32[]{:S(2)}) collective-permute-start(bf16[3,5,128,128]{3,2,1,0:T(8,128)(2,1)S(1)} %get-tuple-element.55), channel_id=1, source_target_pairs={{0,32},{32,0},{64,96},{96,64},{1,33},{33,1},{65,97},{97,65},{2,34}... | collective-permute-start | bytes 1474568 | tf_op jit(solution)/shard_map/ppermute | solution.py:354
  88.8 2.2 %collective-permute-start.7 = (bf16[3,5,128,128]{3,2,1,0:T(8,128)(2,1)S(1)}, bf16[3,5,128,128]{3,2,1,0:T(8,128)(2,1)S(1)}, u32[]{:S(2)}, u32[]{:S(2)}) collective-permute-start(bf16[3,5,128,128]{3,2,1,0:T(8,128)(2,1)S(1)} %get-tuple-element.56), channel_id=1, source_target_pairs={{0,32},{32,0},{64,96},{96,64},{1,33},{33,1},{65,97},{97,65},{2,34}... | collective-permute-start | bytes 1474568 | tf_op jit(solution)/shard_map/ppermute | solution.py:354
  104.0 1.7 %collective-permute-start.9 = (bf16[3,3,128,128]{3,2,1,0:T(8,128)(2,1)S(1)}, bf16[3,3,128,128]{3,2,1,0:T(8,128)(2,1)S(1)}, u32[]{:S(2)}, u32[]{:S(2)}) collective-permute-start(bf16[3,3,128,128]{3,2,1,0:T(8,128)(2,1)S(1)} %get-tuple-element.62), channel_id=1, source_target_pairs={{0,32},{32,0},{64,96},{96,64},{1,33},{33,1},{65,97},{97,65},{2,34}... | collective-permute-start | bytes 884744 | tf_op jit(solution)/shard_map/ppermute | solution.py:354
  104.4 1.6 %collective-permute-start.10 = (bf16[3,3,128,128]{3,2,1,0:T(8,128)(2,1)S(1)}, bf16[3,3,128,128]{3,2,1,0:T(8,128)(2,1)S(1)}, u32[]{:S(2)}, u32[]{:S(2)}) collective-permute-start(bf16[3,3,128,128]{3,2,1,0:T(8,128)(2,1)S(1)} %get-tuple-element.63), channel_id=1, source_target_pairs={{0,32},{32,0},{64,96},{96,64},{1,33},{33,1},{65,97},{97,65},{2,34}... | collective-permute-start | bytes 884744 | tf_op jit(solution)/shard_map/ppermute | solution.py:354

commit v5 on v4

v5 whole, which is shorter than its diff:
```python
import functools
import jax, jax.numpy as jnp
from jax import lax
from jax.experimental import pallas as pl
from jax.experimental.pallas import tpu as pltpu
from jax.sharding import PartitionSpec as P

bf16, f32 = jnp.bfloat16, jnp.float32

SMALL = pl.CostEstimate(flops=1000, bytes_accessed=1000, transcendentals=0)


def shifted_sum(before, here, after, cols):
    rows = before.shape[0]
    place = lax.broadcasted_iota(jnp.int32, before.shape, 0) % cols
    down = jnp.where(place == 0, 0.0, pltpu.roll(before, 1, 0))
    up = jnp.where(place == cols - 1, 0.0, pltpu.roll(after, rows - 1, 0))
    return down + here + up

def split_columns(x_ref, v, i, wide, ev, od, at):
    n = wide.shape[1] // 2
    wide[at] = x_ref[v, i].astype(f32)
    ev[v, at] = wide[at, pl.ds(0, n, 2), :].astype(bf16)
    od[v, at] = wide[at, pl.ds(1, n, 2), :].astype(bf16)


def main_weights(k_ref, wm_ref):
    c = k_ref.shape[2]
    for a in range(5):
        for p in range(2):
            for s in range(2):
                wm_ref[(2 * a + p) * c:(2 * a + p + 1) * c, s * c:(s + 1) * c] = k_ref[a, 2 * s + p]


def side_blocks(refs, blocks, m):
    return jnp.concatenate([refs[p][:, i].reshape(m, -1) for p, i in blocks], axis=1)


def halo_kernel(x_ref, k_ref, h1_ref, h2_ref, wm_ref, we_ref, top, bottom, kern, wide, ev, od, sems):
    g, views, _, wid, c = top.shape
    rows = x_ref.shape[2]
    n = wid // 2
    m = g * n
    weights = pltpu.make_async_copy(k_ref, kern, sems.at[2 * views])
    weights.start()

    def pieces(b):
        return (
            pltpu.make_async_copy(x_ref.at[:, b, 0:1], top.at[:, b], sems.at[2 * b]),
            pltpu.make_async_copy(x_ref.at[:, b, rows - 2:rows], bottom.at[:, b], sems.at[2 * b + 1]),
        )

    for b in range(views):
        for piece in pieces(b):
            piece.start()
    weights.wait()
    main_weights(kern, wm_ref)
    z = jnp.zeros((c, c), bf16)
    for j in range(7):
        we_ref[j * c:(j + 1) * c, :c] = kern[j, 4] if j < 5 else z
        we_ref[j * c:(j + 1) * c, c:] = kern[j - 2, 4] if j > 1 else z
    first = lax.axis_index("view") < 2
    refs = (ev, od)

    def step(b, carry):
        for piece in pieces(b):
            piece.wait()
        for v in range(g):
            split_columns(top.at[:, b], v, 0, wide, ev, od, 0)
            split_columns(bottom.at[:, b], v, 0, wide, ev, od, 1)
            split_columns(bottom.at[:, b], v, 1, wide, ev, od, 2)
        up = jnp.dot(side_blocks(refs, [(0, 0), (1, 0)], m), wm_ref[8 * c:, :], preferred_element_type=f32)
        side = jnp.dot(side_blocks(refs, [(0, 0)], m), we_ref[4 * c:5 * c, :c], preferred_element_type=f32)
        up = shifted_sum(up[:, :c], up[:, c:], side, n).astype(bf16).reshape(g, n, c)
        dn = jnp.dot(side_blocks(refs, [(0, 1), (1, 1), (0, 2), (1, 2)], m), wm_ref[:4 * c, :], preferred_element_type=f32)
        side = jnp.dot(side_blocks(refs, [(0, 1), (0, 2)], m), we_ref[:2 * c, :c], preferred_element_type=f32)
        dn = shifted_sum(dn[:, :c], dn[:, c:], side, n).astype(bf16).reshape(g, n, c)
        h1_ref[:, b] = jnp.where(first, dn, up)
        h2_ref[:, b] = jnp.where(first, up, dn)
        return carry

    lax.fori_loop(0, views, step, 0)


def halo_sums(features, kernel):
    U, V, H, W, C = features.shape
    n = W // 2
    whole = pl.BlockSpec(memory_space=pltpu.VMEM)
    return pl.pallas_call(
        halo_kernel,
        in_specs=[pl.BlockSpec(memory_space=pl.ANY)] * 2,
        out_specs=[whole] * 4,
        scratch_shapes=[
            pltpu.VMEM((U, V, 1, W, C), bf16), pltpu.VMEM((U, V, 2, W, C), bf16), pltpu.VMEM(kernel.shape, bf16),
            pltpu.VMEM((3, W, C), f32), pltpu.VMEM((U, 3, n, C), bf16), pltpu.VMEM((U, 3, n, C), bf16),
            pltpu.SemaphoreType.DMA((2 * V + 1,)),
        ],
        out_shape=[jax.ShapeDtypeStruct((U, V, n, C), bf16)] * 2
        + [jax.ShapeDtypeStruct((taps * C, 2 * C), bf16) for taps in (10, 7)],
        compiler_params=pltpu.CompilerParams(vmem_limit_bytes=57 * 2**20),
        cost_estimate=SMALL,
        name="halo",
    )(features, kernel)


def conv_kernel(base, starts, x_ref, wm_ref, we_ref, *rest):
    outs, (xs, wide, ev, od, sems) = rest[:-5], rest[-5:]
    count, g, rows, wid, c = xs.shape
    n = wid // 2
    m = g * n

    def fetch(b):
        return pltpu.make_async_copy(x_ref.at[:, base + b], xs.at[b], sems.at[b])

    for b in range(count):
        fetch(b).start()
    first = lax.axis_index("view") < 2
    refs = (ev, od)

    def main(lo, hi, a):
        lhs = side_blocks(refs, [(p, i) for i in range(lo, hi) for p in range(2)], m)
        return jnp.dot(lhs, wm_ref[a * 2 * c:(a + hi - lo) * 2 * c, :], preferred_element_type=f32)

    def side(lo, hi, a):
        lhs = side_blocks(refs, [(0, i) for i in range(lo, hi)], m)
        return jnp.dot(lhs, we_ref[a * c:(a + hi - lo) * c, :], preferred_element_type=f32)

    def row(mn, sd):
        return shifted_sum(mn[:, :c], mn[:, c:], sd, n).astype(bf16).reshape(g, n, c)

    def step(own_ref, oth_ref, start, b, carry):
        fetch(b).wait()
        for v in range(g):
            for i in range(rows):
                split_columns(xs.at[b], v, i, wide, ev, od, i)
        at = b - start
        pair = side(0, 5, 2)
        r0 = row(main(0, 3, 2), pair[:, :c])
        r1 = row(main(0, 5, 0), pair[:, c:])
        pair = side(2, 8, 0)
        r2 = row(main(2, 7, 0), pair[:, :c])
        r3 = row(main(4, 8, 0), pair[:, c:])
        own_ref[0, :, at] = jnp.where(first, r0, r2)
        own_ref[1, :, at] = jnp.where(first, r1, r3)
        oth_ref[0, :, at] = jnp.where(first, r2, r0)
        oth_ref[1, :, at] = jnp.where(first, r3, r1)
        return carry

    for q, start in enumerate(starts):
        end = starts[q + 1] if q + 1 < len(starts) else count
        lax.fori_loop(start, end, functools.partial(step, outs[2 * q], outs[2 * q + 1], start), 0)


def conv_chunks(features, wm, we, spans):
    U, V, H, W, C = features.shape
    n = W // 2
    base = spans[0][0]
    starts = tuple(lo - base for lo, _ in spans)

    count = spans[-1][1] - base
    whole = pl.BlockSpec(memory_space=pltpu.VMEM)
    return pl.pallas_call(
        functools.partial(conv_kernel, base, starts),
        in_specs=[pl.BlockSpec(memory_space=pl.ANY), whole, whole],
        out_specs=[whole] * (2 * len(spans)),
        scratch_shapes=[
            pltpu.VMEM((count, U, H, W, C), bf16),
            pltpu.VMEM((H, W, C), f32), pltpu.VMEM((U, H, n, C), bf16), pltpu.VMEM((U, H, n, C), bf16),
            pltpu.SemaphoreType.DMA((count,)),
        ],
        out_shape=[jax.ShapeDtypeStruct((2, U, hi - lo, n, C), bf16) for lo, hi in spans for _ in range(2)],
        compiler_params=pltpu.CompilerParams(vmem_limit_bytes=46 * 2**20),
        cost_estimate=SMALL,
        name="conv",
    )(features, wm, we)


def norm_kernel(lo, own_ref, oth_ref, h1_ref, h2_ref, floor_ref, mix_ref, mine_ref, *give_refs):
    place = lax.axis_index("view")
    first = place < 2
    upper = place % 2 == 0
    _, g, cv, n, c = own_ref.shape
    mix = mix_ref[...].astype(bf16)

    def step(v, carry):
        for j, (raw_ref, part_ref) in enumerate(((own_ref, h1_ref), (oth_ref, h2_ref))):
            part = part_ref[:, lo + v].reshape(g * n, c).astype(f32)
            coded = []
            for r in range(2):
                x = raw_ref[r, :, v].reshape(g * n, c).astype(f32)
                x = x + jnp.where(first == (r == 0), part, 0.0)
                energy = jnp.dot((x * x).astype(bf16), mix, preferred_element_type=f32)
                coded.append((x * lax.rsqrt(floor_ref[...] + energy)).astype(bf16).reshape(g, n, c))
            mine_ref[j, :, v] = jnp.where(upper, coded[0], coded[1])
            give = give_refs[j] if len(give_refs) > 1 else give_refs[0].at[j]
            give[:, v] = jnp.where(upper, coded[1], coded[0])
        return carry

    lax.fori_loop(0, cv, step, 0)


def norm_chunk(own, oth, h1, h2, floor, mix, lo, parts):
    _, U, cv, n, C = own.shape
    whole = pl.BlockSpec(memory_space=pltpu.VMEM)
    return pl.pallas_call(
        functools.partial(norm_kernel, lo),
        in_specs=[whole] * 6,
        out_specs=[whole] * (1 + parts),
        out_shape=[jax.ShapeDtypeStruct((2, U, cv, n, C), bf16)]
        + [jax.ShapeDtypeStruct((2,) * (2 - parts) + (U, cv, n, C), bf16)] * parts,
        compiler_params=pltpu.CompilerParams(vmem_limit_bytes=16 * 2**20),
        cost_estimate=SMALL,
        name="norm",
    )(own, oth, h1, h2, floor, mix)


def epi_kernel(pieces, v0, v1, has_prev, *refs):
    k = pieces[-1][0] + 1 + pieces[-1][1]
    srcs = refs[:k]
    wm_ref, we_ref, bias_ref = refs[k:k + 3]
    rest = refs[k + 3 + has_prev:]
    out_ref, cod, obuf, sem_in, sem_out = rest
    U = srcs[0].shape[1]
    n, c = cod.shape[2], cod.shape[3]
    V = out_ref.shape[1]
    total = out_ref.shape[0]
    nv = v1 - v0
    for p, (at, parts, s0, s1, d0) in enumerate(pieces):
        for j in range(4):
            src = srcs[at].at[j] if j < 2 else srcs[at + j - 1] if parts > 1 else srcs[at + 1].at[j - 2]
            blk = lax.axis_index("view") ^ (0, 2, 1, 3)[j]
            cp = pltpu.make_async_copy(src.at[:, s0:s1], cod.at[pl.ds(1 + U * blk, U), d0:d0 + s1 - s0], sem_in.at[4 * p + blk])
            cp.start()
    edge = jnp.zeros((nv + 2, n, c), bf16)
    cod[0] = edge
    cod[total + 1] = edge
    if v0 == 0:
        cod[:, 0] = jnp.zeros((total + 2, n, c), bf16)
    if v1 == V:
        cod[:, nv + 1] = jnp.zeros((total + 2, n, c), bf16)

    def arrived(b):
        for p, (at, parts, s0, s1, d0) in enumerate(pieces):
            pltpu.make_async_copy(
                srcs[at].at[0, :, s0:s1], cod.at[1 + U * b:1 + U * (b + 1), d0:d0 + s1 - s0], sem_in.at[4 * p + b]
            ).wait()
    m = nv * n
    steps = total // 2
    def out_copy(t, slot):
        return pltpu.make_async_copy(obuf.at[slot], out_ref.at[pl.ds(2 * t, 2), v0:v1, 0], sem_out.at[slot])
    def step(t, carry):
        slot = lax.rem(t, 2)
        for b in range(total // U):
            pl.when(t == max(0, -(-(U * b - 2) // 2)))(functools.partial(arrived, b))

        @pl.when(t >= 2)
        def _():
            out_copy(t - 2, slot).wait()
        def block(i, j):
            return cod[2 * t + i, j:j + nv].reshape(m, c)
        blocks = [[block(i, j) for j in range(3)] for i in range(4)]
        ex = jnp.dot(jnp.concatenate(sum(blocks, []), axis=1), we_ref[...], preferred_element_type=f32)
        for h in range(2):
            mn = jnp.dot(jnp.concatenate(sum(blocks[h:h + 3], []), axis=1), wm_ref[...], preferred_element_type=f32)
            res = shifted_sum(mn[:, :c], mn[:, c:], ex[:, h * c:(h + 1) * c], n) + bias_ref[...]
            obuf[slot, h] = res.astype(bf16).reshape(nv, n, c)
        out_copy(t, slot).start()
        return carry
    lax.fori_loop(0, steps, step, 0)
    for t in (steps - 2, steps - 1):
        out_copy(t, t % 2).wait()

def epi_weights(k):
    c = k.shape[3]
    main = jnp.concatenate([k[:, :, 0], k[:, :, 1]], -1).reshape(-1, 2 * c)
    z = jnp.zeros((1,) + k.shape[1:2] + k.shape[3:], k.dtype)
    last = jnp.concatenate([jnp.concatenate([k[:, :, 2], z], 0), jnp.concatenate([z, k[:, :, 2]], 0)], -1)
    return main, last.reshape(-1, 2 * c)

def epi_chunk(sources, spans, v0, v1, prev, wm, we, bias, total, V):
    used, pieces = [], []
    for (mine, flipped), (lo, hi) in zip(sources, spans):
        a, b = max(lo, v0 - 1), min(hi, v1 + 1)
        if a < b:
            pieces.append((len(used), len(flipped), a - lo, b - lo, a - (v0 - 1)))
            used += [mine, *flipped]
    _, U, _, n, C = used[0].shape
    anyspec = pl.BlockSpec(memory_space=pl.ANY)
    whole = pl.BlockSpec(memory_space=pltpu.VMEM)
    nv = v1 - v0
    args = used + [wm, we, bias] + ([prev] if prev is not None else [])
    return pl.pallas_call(
        functools.partial(epi_kernel, tuple(pieces), v0, v1, int(prev is not None)),
        grid=(1,),
        in_specs=[anyspec] * len(used) + [whole] * 3 + [anyspec] * (prev is not None),
        out_specs=anyspec,
        scratch_shapes=[
            pltpu.VMEM((total + 2, nv + 2, n, C), bf16),
            pltpu.VMEM((2, 2, nv, n, C), bf16),
            pltpu.SemaphoreType.DMA((4 * len(pieces),)),
            pltpu.SemaphoreType.DMA((2,)),
        ],
        out_shape=jax.ShapeDtypeStruct((total, V, 1, n, C), bf16),
        input_output_aliases={len(args) - 1: 0} if prev is not None else {},
        compiler_params=pltpu.CompilerParams(vmem_limit_bytes=24 * 2**20),
        cost_estimate=SMALL,
        name="epi",
    )(*args)


CHUNKS = ((0, 4), (4, 9), (9, 12))
PARTS = (1, 2, 1)


def shards(features, analysis_kernel, norm_floor, norm_mixing, epipolar_kernel, epipolar_bias):
    U, V = features.shape[:2]
    views, bands = lax.axis_size("view"), lax.axis_size("rows")
    total = U * views
    em, ee = epi_weights(epipolar_kernel)
    floor, bias = norm_floor[None], epipolar_bias[None]
    both = ("view", "rows")
    swap = [(v * bands + r, (v ^ 2) * bands + r) for v in range(views) for r in range(bands)]
    def hop(flip):
        pairs = []
        for v in range(views):
            step = 1 if (v < 2) != (flip > 0) else -1
            pairs += [(v * bands + r, (v ^ flip) * bands + r + step) for r in range(bands) if 0 <= r + step < bands]
        return pairs
    core = [(v, v ^ 1) for v in range(views)]
    h1_sum, h2_sum, wm, we = halo_sums(features, analysis_kernel)
    h1 = lax.ppermute(h1_sum, both, hop(0))
    h2 = lax.ppermute(h2_sum, both, hop(2))
    rows, sent = [], []
    features, last = lax.optimization_barrier((features, h1_sum))
    for spans in (CHUNKS[:1], CHUNKS[1:]):
        done = conv_chunks(features, wm, we, spans)
        rows += done[::2]
        sent += done[1::2]
        features, last = lax.optimization_barrier((features, done[0]))
    sent[0] = lax.ppermute(sent[0], both, swap)
    sent[1], h1, h2 = lax.optimization_barrier((sent[1], h1, h2))
    sent[1] = lax.ppermute(sent[1], both, swap)
    sources = []
    out = None
    done = 0
    for i, (lo, hi) in enumerate(CHUNKS):
        own, oth = rows[i], sent[i]
        if out is None:
            oth, rows[-1] = lax.optimization_barrier((oth, rows[-1]))
        else:
            oth, out = lax.optimization_barrier((oth, out))
        mine, *give = norm_chunk(own, oth, h1, h2, floor, norm_mixing, lo, PARTS[i])
        flipped = [lax.ppermute(g, "view", core) for g in give]
        sources.append((mine, flipped))
        upto = V if hi == V else hi - 1
        out = epi_chunk(sources, CHUNKS[:i + 1], done, upto, out, em, ee, bias, total, V)
        done = upto
        if i + 2 < len(CHUNKS):
            sent[i + 2], out = lax.optimization_barrier((sent[i + 2], out))
            sent[i + 2] = lax.ppermute(sent[i + 2], both, swap)
    return out


def solution(mesh):
    in_specs = (P("view", None, "rows", None, None), P(), P(), P(), P(), P())
    out_specs = P(None, None, ("rows", "view"), None, None)
    return jax.shard_map(shards, mesh=mesh, in_specs=in_specs, out_specs=out_specs, check_vma=False)
```

time: 116 us -> 114 us (0.983)
  Pallas kernels: 67.7 us -> 60.2 us
  starting transfers between devices: 11.3 us -> 14.4 us
  waiting for transfers between devices: 35.1 us -> 36.4 us
    pallas_call x6, Pallas kernels: 38.9 us -> 33.2 us  [the longest x2 21 us: conv_chunks(): pl.pallas_call(functools.partial(conv_kernel, base, starts), in_specs=[pl...]
    ppermute x1, starting transfers between devices: 0.4 us -> 3.82 us  [shards(): sent[1] = lax.ppermute(sent[1], both, swap)]
    pallas_call x3, Pallas kernels: 28.8 us -> 27 us  [epi_chunk(): pl.pallas_call(functools.partial(epi_kernel, tuple(pieces), v0, v1, int(p...]
    ppermute x6 -> x4, waiting for transfers between devices: 5.16 us -> 5.39 us  [shards(): flipped = [lax.ppermute(g, 'view', core) for g in give]]
  transfers between devices with their start and end apart: 11 -> 9, of which waited for: 8 -> 6; matrix products, arithmetic and copies ran while one was open for 0% -> 0% of each run, Pallas kernels for 43% -> 37%
where the time goes in v5:
time: 114 us
  Pallas kernels  60.2 us (53%)
  waiting for transfers between devices  36.4 us (32%)
  starting transfers between devices  14.4 us (13%)
  local copies, waits for them, and re-layouts  2.2 us (2%)
    pallas_call x3, Pallas kernels, epi_chunk(): pl.pallas_call(functools.partial(epi_kernel, tuple(pieces), v0, v1, int(p...  27 us
    pallas_call x2, Pallas kernels, conv_chunks(): pl.pallas_call(functools.partial(conv_kernel, base, starts), in_specs=[pl...  21 us
    ppermute x1, waiting for transfers between devices, shards(): sent[0] = lax.ppermute(sent[0], both, swap)  20.9 us
    ppermute x1, waiting for transfers between devices, shards(): sent[1] = lax.ppermute(sent[1], both, swap)  10.1 us
    pallas_call x1, Pallas kernels, halo_sums(): pl.pallas_call(halo_kernel, in_specs=[pl.BlockSpec(memory_space=pl.ANY)]...  8.73 us
    ppermute x4, waiting for transfers between devices, shards(): flipped = [lax.ppermute(g, 'view', core) for g in give]  5.39 us
    ppermute x1, starting transfers between devices, shards(): sent[0] = lax.ppermute(sent[0], both, swap)  4.7 us
    ppermute x1, starting transfers between devices, shards(): sent[1] = lax.ppermute(sent[1], both, swap)  3.82 us
  transfers between devices with their start and end apart: 9, of which 6 were waited for; matrix products, arithmetic and copies ran while one was open for 0% of the time, Pallas kernels for 37%

profile of v5, /device:TPU:121, one launch (start us, length us, event | category | flops | bytes accessed | tf_op | source)
XLA Modules:
  0.0 113.6 jit_solution(3031043314673253940)
XLA Ops:
  0.0 8.7 %halo.1 = (bf16[3,12,128,128]{3,2,1,0:T(8,128)(2,1)}, bf16[3,12,128,128]{3,2,1,0:T(8,128)(2,1)}, bf16[1280,256]{1,0:T(8,128)(2,1)}, bf16[896,256]{1,0:T(8,128)(2,1)}) custom-call(bf16[3,12,8,256,128]{4,3,2,1,0:T(8,128)(2,1)} %x_ref.3, bf16[5,5,128,128]{3,2,1,0:T(8,128)(2,1)} %k_ref.1), custom_call_target="tpu_custom_call" | custom-call | flops 1000 | bytes 1000 | tf_op jit(solution)/shard_map/halo/pallas_call | solution.py:89
  8.7 1.9 %collective-permute-start.1 = (bf16[3,12,128,128]{3,2,1,0:T(8,128)(2,1)}, bf16[3,12,128,128]{3,2,1,0:T(8,128)(2,1)S(1)}, u32[]{:S(2)}, u32[]{:S(2)}) collective-permute-start(bf16[3,12,128,128]{3,2,1,0:T(8,128)(2,1)} %get-tuple-element.43), channel_id=1, source_target_pairs={{1,64},{2,65},{3,66},{4,67},{5,68},{6,69},{7,70},{8,71},{9,72},{10... | collective-permute-start | bytes 3538952 | tf_op jit(solution)/shard_map/ppermute | solution.py:332
  10.7 2.0 %collective-permute-start = (bf16[3,12,128,128]{3,2,1,0:T(8,128)(2,1)}, bf16[3,12,128,128]{3,2,1,0:T(8,128)(2,1)S(1)}, u32[]{:S(2)}, u32[]{:S(2)}) collective-permute-start(bf16[3,12,128,128]{3,2,1,0:T(8,128)(2,1)} %get-tuple-element.35), channel_id=1, source_target_pairs={{0,1},{1,2},{2,3},{3,4},{4,5},{5,6},{6,7},{7,8},{8,9},{9,10},{10,1... | collective-permute-start | bytes 3538952 | tf_op jit(solution)/shard_map/ppermute | solution.py:331
  12.7 0.0 copy-start
  12.7 1.1 copy-done
  13.8 0.0 copy-start.1
  13.8 1.0 copy-done.1
  14.8 7.5 %conv.2 = (bf16[2,3,4,128,128]{4,3,2,1,0:T(8,128)(2,1)S(1)}, bf16[2,3,4,128,128]{4,3,2,1,0:T(8,128)(2,1)S(1)}) custom-call(bf16[3,12,8,256,128]{4,3,2,1,0:T(8,128)(2,1)} %x_ref.3, bf16[1280,256]{1,0:T(8,128)(2,1)S(1)} %copy-done, bf16[896,256]{1,0:T(8,128)(2,1)S(1)} %copy-done.1), custom_call_target="tpu_custom_call" | custom-call | flops 1000 | bytes 1000 | tf_op jit(solution)/shard_map/conv/pallas_call | solution.py:162
  22.3 4.7 %collective-permute-start.3 = (bf16[2,3,4,128,128]{4,3,2,1,0:T(8,128)(2,1)S(1)}, bf16[2,3,4,128,128]{4,3,2,1,0:T(8,128)(2,1)S(1)}, u32[]{:S(2)}, u32[]{:S(2)}) collective-permute-start(bf16[2,3,4,128,128]{4,3,2,1,0:T(8,128)(2,1)S(1)} %get-tuple-element.46), channel_id=1, source_target_pairs={{0,64},{1,65},{2,66},{3,67},{4,68},{5,69},{6,70},{7,71},{8,72},{9,... | collective-permute-start | bytes 2359304 | tf_op jit(solution)/shard_map/ppermute | solution.py:340
  27.0 0.0 copy-start.2
  27.0 0.0 copy-start.4
  27.0 13.5 %conv.3 = (bf16[2,3,5,128,128]{4,3,2,1,0:T(8,128)(2,1)S(1)}, bf16[2,3,5,128,128]{4,3,2,1,0:T(8,128)(2,1)S(1)}, bf16[2,3,3,128,128]{4,3,2,1,0:T(8,128)(2,1)S(1)}, bf16[2,3,3,128,128]{4,3,2,1,0:T(8,128)(2,1)S(1)}) custom-call(bf16[3,12,8,256,128]{4,3,2,1,0:T(8,128)(2,1)} %x_ref.3, bf16[1280,256]{1,0:T(8,128)(2,1)S(1)} %copy-done, bf16[896,256]{1,0:T(8,128)(2,1)S(1)} %copy-done.1), custom_call_target="tpu_custom_call" | custom-call | flops 1000 | bytes 1000 | tf_op jit(solution)/shard_map/conv/pallas_call | solution.py:162
  40.5 0.0 collective-permute-done.1.h2_ref
  40.5 0.0 collective-permute-done.h1_ref
  40.5 3.8 %collective-permute-start.2 = (bf16[2,3,5,128,128]{4,3,2,1,0:T(8,128)(2,1)S(1)}, bf16[2,3,5,128,128]{4,3,2,1,0:T(8,128)(2,1)S(1)}, u32[]{:S(2)}, u32[]{:S(2)}) collective-permute-start(bf16[2,3,5,128,128]{4,3,2,1,0:T(8,128)(2,1)S(1)} %get-tuple-element.44), channel_id=1, source_target_pairs={{0,64},{1,65},{2,66},{3,67},{4,68},{5,69},{6,70},{7,71},{8,72},{9,... | collective-permute-start | bytes 2949128 | tf_op jit(solution)/shard_map/ppermute | solution.py:342
  44.4 20.9 %collective-permute-done.3.oth_ref = bf16[2,3,4,128,128]{4,3,2,1,0:T(8,128)(2,1)S(1)} collective-permute-done((bf16[2,3,4,128,128]{4,3,2,1,0:T(8,128)(2,1)S(1)}, bf16[2,3,4,128,128]{4,3,2,1,0:T(8,128)(2,1)S(1)}, u32[]{:S(2)}, u32[]{:S(2)}) %collective-permute-start.3) | collective-permute-done | bytes 786464 | tf_op jit(solution)/shard_map/ppermute | solution.py:340
  65.3 0.0 copy-done.2
  65.3 0.0 copy-done.4
  65.3 0.0 copy-start.5
  65.3 1.2 %norm.3 = (bf16[2,3,4,128,128]{4,3,2,1,0:T(8,128)(2,1)S(1)}, bf16[2,3,4,128,128]{4,3,2,1,0:T(8,128)(2,1)S(1)}) custom-call(bf16[2,3,4,128,128]{4,3,2,1,0:T(8,128)(2,1)S(1)} %get-tuple-element.39.own_ref, bf16[2,3,4,128,128]{4,3,2,1,0:T(8,128)(2,1)S(1)} %collective-permute-done.3.oth_ref, bf16[3,12,128,128]{3,2,1,0:T(8,128)(2,1)S(1)} %collective-permute-done.h1_ref, ...), custom_call_target="tpu_custom_call" | custom-call | flops 1000 | bytes 1000 | tf_op jit(solution)/shard_map/norm/pallas_call | solution.py:205
  66.5 0.7 collective-permute-start.4
  67.1 0.0 copy-done.5
  67.1 0.1 slice_bitcast_fusion
  67.2 0.0 copy-start.3
  67.2 0.1 fusion.2
  67.3 0.1 pad_maximum_fusion.refs_2_.refs_5_
  67.4 1.7 %collective-permute-done.4.refs_1_ = bf16[2,3,4,128,128]{4,3,2,1,0:T(8,128)(2,1)S(1)} collective-permute-done((bf16[2,3,4,128,128]{4,3,2,1,0:T(8,128)(2,1)S(1)}, bf16[2,3,4,128,128]{4,3,2,1,0:T(8,128)(2,1)S(1)}, u32[]{:S(2)}, u32[]{:S(2)}) %collective-permute-start.4) | collective-permute-done | bytes 786464 | tf_op jit(solution)/shard_map/ppermute | solution.py:353
  69.0 0.0 copy-done.3
  69.0 7.1 %epi.3.refs_8_ = bf16[12,12,1,128,128]{4,3,2,1,0:T(8,128)(2,1)} custom-call(bf16[2,3,4,128,128]{4,3,2,1,0:T(8,128)(2,1)S(1)} %get-tuple-element.51.refs_0_, bf16[2,3,4,128,128]{4,3,2,1,0:T(8,128)(2,1)S(1)} %collective-permute-done.4.refs_1_, bf16[1152,256]{1,0:T(8,128)(2,1)S(1)} %pad_maximum_fusion.refs_2_.refs_5_, bf16[1536,256]{1,0:T(8,128)(2,1)S(1)} %bitcast.7, ...), custom_call_target="tpu_custom_call" | custom-call | flops 1000 | bytes 1000 | tf_op jit(solution)/shard_map/epi/pallas_call | solution.py:292
  76.1 0.1 collective-permute-start.7
  76.2 10.1 %collective-permute-done.2.oth_ref = bf16[2,3,5,128,128]{4,3,2,1,0:T(8,128)(2,1)S(1)} collective-permute-done((bf16[2,3,5,128,128]{4,3,2,1,0:T(8,128)(2,1)S(1)}, bf16[2,3,5,128,128]{4,3,2,1,0:T(8,128)(2,1)S(1)}, u32[]{:S(2)}, u32[]{:S(2)}) %collective-permute-start.2) | collective-permute-done | bytes 983072 | tf_op jit(solution)/shard_map/ppermute | solution.py:342
  86.3 1.5 %norm.4 = (bf16[2,3,5,128,128]{4,3,2,1,0:T(8,128)(2,1)S(1)}, bf16[3,5,128,128]{3,2,1,0:T(8,128)(2,1)S(1)}, bf16[3,5,128,128]{3,2,1,0:T(8,128)(2,1)S(1)}) custom-call(bf16[2,3,5,128,128]{4,3,2,1,0:T(8,128)(2,1)S(1)} %get-tuple-element.41.own_ref, bf16[2,3,5,128,128]{4,3,2,1,0:T(8,128)(2,1)S(1)} %collective-permute-done.2.oth_ref, ...), custom_call_target="tpu_custom_call" | custom-call | flops 1000 | bytes 1000 | tf_op jit(solution)/shard_map/norm/pallas_call | solution.py:205
  87.8 0.7 collective-permute-start.5
  88.5 0.1 collective-permute-start.6
  88.6 1.4 %collective-permute-done.5.refs_3_.refs_1_ = bf16[3,5,128,128]{3,2,1,0:T(8,128)(2,1)S(1)} collective-permute-done((bf16[3,5,128,128]{3,2,1,0:T(8,128)(2,1)S(1)}, bf16[3,5,128,128]{3,2,1,0:T(8,128)(2,1)S(1)}, u32[]{:S(2)}, u32[]{:S(2)}) %collective-permute-start.5) | collective-permute-done | bytes 491552 | tf_op jit(solution)/shard_map/ppermute | solution.py:353
  90.0 0.7 collective-permute-done.6.refs_4_.refs_2_
  90.7 10.9 %epi.4.refs_8_ = bf16[12,12,1,128,128]{4,3,2,1,0:T(8,128)(2,1)} custom-call(bf16[2,3,4,128,128]{4,3,2,1,0:T(8,128)(2,1)S(1)} %get-tuple-element.51.refs_0_, bf16[2,3,4,128,128]{4,3,2,1,0:T(8,128)(2,1)S(1)} %collective-permute-done.4.refs_1_, bf16[2,3,5,128,128]{4,3,2,1,0:T(8,128)(2,1)S(1)} %get-tuple-element.55.refs_2_.refs_0_, ...), custom_call_target="tpu_custom_call", output_to_operand_aliasing={{}: (8, {})} | custom-call | flops 1000 | bytes 1000 | tf_op jit(solution)/shard_map/epi/pallas_call | solution.py:292
  101.6 0.0 collective-permute-done.7.oth_ref
  101.6 0.9 norm.5
  102.5 0.5 collective-permute-start.8
  102.9 1.6 %collective-permute-done.8.refs_4_ = bf16[2,3,3,128,128]{4,3,2,1,0:T(8,128)(2,1)S(1)} collective-permute-done((bf16[2,3,3,128,128]{4,3,2,1,0:T(8,128)(2,1)S(1)}, bf16[2,3,3,128,128]{4,3,2,1,0:T(8,128)(2,1)S(1)}, u32[]{:S(2)}, u32[]{:S(2)}) %collective-permute-start.8) | collective-permute-done | bytes 589856 | tf_op jit(solution)/shard_map/ppermute | solution.py:353
  104.6 9.0 %epi.5 = bf16[12,12,1,128,128]{4,3,2,1,0:T(8,128)(2,1)} custom-call(bf16[2,3,5,128,128]{4,3,2,1,0:T(8,128)(2,1)S(1)} %get-tuple-element.55.refs_2_.refs_0_, bf16[3,5,128,128]{3,2,1,0:T(8,128)(2,1)S(1)} %collective-permute-done.5.refs_3_.refs_1_, bf16[3,5,128,128]{3,2,1,0:T(8,128)(2,1)S(1)} %collective-permute-done.6.refs_4_.refs_2_, ...), custom_call_target="tpu_custom_call", output_to_operand_aliasing={{}: (8, {})} | custom-call | flops 1000 | bytes 1000 | tf_op jit(solution)/shard_map/epi/pallas_call | solution.py:292
Async XLA Ops:
  8.7 31.8 %collective-permute-start.1 = (bf16[3,12,128,128]{3,2,1,0:T(8,128)(2,1)}, bf16[3,12,128,128]{3,2,1,0:T(8,128)(2,1)S(1)}, u32[]{:S(2)}, u32[]{:S(2)}) collective-permute-start(bf16[3,12,128,128]{3,2,1,0:T(8,128)(2,1)} %get-tuple-element.43), channel_id=1, source_target_pairs={{1,64},{2,65},{3,66},{4,67},{5,68},{6,69},{7,70},{8,71},{9,72},{10... | collective-permute-start | bytes 3538952 | tf_op jit(solution)/shard_map/ppermute | solution.py:332
  10.7 29.9 %collective-permute-start = (bf16[3,12,128,128]{3,2,1,0:T(8,128)(2,1)}, bf16[3,12,128,128]{3,2,1,0:T(8,128)(2,1)S(1)}, u32[]{:S(2)}, u32[]{:S(2)}) collective-permute-start(bf16[3,12,128,128]{3,2,1,0:T(8,128)(2,1)} %get-tuple-element.35), channel_id=1, source_target_pairs={{0,1},{1,2},{2,3},{3,4},{4,5},{5,6},{6,7},{7,8},{8,9},{9,10},{10,1... | collective-permute-start | bytes 3538952 | tf_op jit(solution)/shard_map/ppermute | solution.py:331
  12.7 1.1 copy-start
  13.8 1.0 copy-start.1
  22.3 43.0 %collective-permute-start.3 = (bf16[2,3,4,128,128]{4,3,2,1,0:T(8,128)(2,1)S(1)}, bf16[2,3,4,128,128]{4,3,2,1,0:T(8,128)(2,1)S(1)}, u32[]{:S(2)}, u32[]{:S(2)}) collective-permute-start(bf16[2,3,4,128,128]{4,3,2,1,0:T(8,128)(2,1)S(1)} %get-tuple-element.46), channel_id=1, source_target_pairs={{0,64},{1,65},{2,66},{3,67},{4,68},{5,69},{6,70},{7,71},{8,72},{9,... | collective-permute-start | bytes 2359304 | tf_op jit(solution)/shard_map/ppermute | solution.py:340
  27.0 38.3 %copy-start.2 = (f32[128,128]{1,0:T(8,128)S(1)}, f32[128,128]{1,0:T(8,128)}, u32[]{:S(2)}) copy-start(f32[128,128]{1,0:T(8,128)} %mix_ref.5) | copy-start | bytes 196612
  27.0 38.3 %copy-start.4 = (f32[128]{0:T(128)S(1)}, f32[128]{0:T(128)}, u32[]{:S(2)}) copy-start(f32[128]{0:T(128)} %param.8) | copy-start | bytes 1540
  40.5 45.8 %collective-permute-start.2 = (bf16[2,3,5,128,128]{4,3,2,1,0:T(8,128)(2,1)S(1)}, bf16[2,3,5,128,128]{4,3,2,1,0:T(8,128)(2,1)S(1)}, u32[]{:S(2)}, u32[]{:S(2)}) collective-permute-start(bf16[2,3,5,128,128]{4,3,2,1,0:T(8,128)(2,1)S(1)} %get-tuple-element.44), channel_id=1, source_target_pairs={{0,64},{1,65},{2,66},{3,67},{4,68},{5,69},{6,70},{7,71},{8,72},{9,... | collective-permute-start | bytes 2949128 | tf_op jit(solution)/shard_map/ppermute | solution.py:342
  65.3 1.8 %copy-start.5 = (bf16[3,3,3,128,128]{4,3,2,1,0:T(8,128)(2,1)S(1)}, bf16[3,3,3,128,128]{4,3,2,1,0:T(8,128)(2,1)}, u32[]{:S(2)}) copy-start(bf16[3,3,3,128,128]{4,3,2,1,0:T(8,128)(2,1)} %param.10) | copy-start | bytes 2654212
  66.5 2.6 %collective-permute-start.4 = (bf16[2,3,4,128,128]{4,3,2,1,0:T(8,128)(2,1)S(1)}, bf16[2,3,4,128,128]{4,3,2,1,0:T(8,128)(2,1)S(1)}, u32[]{:S(2)}, u32[]{:S(2)}) collective-permute-start(bf16[2,3,4,128,128]{4,3,2,1,0:T(8,128)(2,1)S(1)} %get-tuple-element.52), channel_id=1, source_target_pairs={{0,32},{32,0},{64,96},{96,64},{1,33},{33,1},{65,97},{97,65},{2,34}... | collective-permute-start | bytes 2359304 | tf_op jit(solution)/shard_map/ppermute | solution.py:353
  67.2 1.8 %copy-start.3 = (f32[128]{0:T(128)S(1)}, f32[128]{0:T(128)}, u32[]{:S(2)}) copy-start(f32[128]{0:T(128)} %param.11) | copy-start | bytes 1540
  76.1 25.5 %collective-permute-start.7 = (bf16[2,3,3,128,128]{4,3,2,1,0:T(8,128)(2,1)S(1)}, bf16[2,3,3,128,128]{4,3,2,1,0:T(8,128)(2,1)S(1)}, u32[]{:S(2)}, u32[]{:S(2)}) collective-permute-start(bf16[2,3,3,128,128]{4,3,2,1,0:T(8,128)(2,1)S(1)} %get-tuple-element.59), channel_id=1, source_target_pairs={{0,64},{1,65},{2,66},{3,67},{4,68},{5,69},{6,70},{7,71},{8,72},{9,... | collective-permute-start | bytes 1769480 | tf_op jit(solution)/shard_map/ppermute | solution.py:360
  87.8 2.2 %collective-permute-start.5 = (bf16[3,5,128,128]{3,2,1,0:T(8,128)(2,1)S(1)}, bf16[3,5,128,128]{3,2,1,0:T(8,128)(2,1)S(1)}, u32[]{:S(2)}, u32[]{:S(2)}) collective-permute-start(bf16[3,5,128,128]{3,2,1,0:T(8,128)(2,1)S(1)} %get-tuple-element.56), channel_id=1, source_target_pairs={{0,32},{32,0},{64,96},{96,64},{1,33},{33,1},{65,97},{97,65},{2,34}... | collective-permute-start | bytes 1474568 | tf_op jit(solution)/shard_map/ppermute | solution.py:353
  88.5 2.2 %collective-permute-start.6 = (bf16[3,5,128,128]{3,2,1,0:T(8,128)(2,1)S(1)}, bf16[3,5,128,128]{3,2,1,0:T(8,128)(2,1)S(1)}, u32[]{:S(2)}, u32[]{:S(2)}) collective-permute-start(bf16[3,5,128,128]{3,2,1,0:T(8,128)(2,1)S(1)} %get-tuple-element.57), channel_id=1, source_target_pairs={{0,32},{32,0},{64,96},{96,64},{1,33},{33,1},{65,97},{97,65},{2,34}... | collective-permute-start | bytes 1474568 | tf_op jit(solution)/shard_map/ppermute | solution.py:353
  102.5 2.1 %collective-permute-start.8 = (bf16[2,3,3,128,128]{4,3,2,1,0:T(8,128)(2,1)S(1)}, bf16[2,3,3,128,128]{4,3,2,1,0:T(8,128)(2,1)S(1)}, u32[]{:S(2)}, u32[]{:S(2)}) collective-permute-start(bf16[2,3,3,128,128]{4,3,2,1,0:T(8,128)(2,1)S(1)} %get-tuple-element.63), channel_id=1, source_target_pairs={{0,32},{32,0},{64,96},{96,64},{1,33},{33,1},{65,97},{97,65},{2,34}... | collective-permute-start | bytes 1769480 | tf_op jit(solution)/shard_map/ppermute | solution.py:353

commit v6 on v5

--- a/solution.py
+++ b/solution.py
@@ -36,84 +36,39 @@
     return jnp.concatenate([refs[p][:, i].reshape(m, -1) for p, i in blocks], axis=1)
 
 
-def halo_kernel(x_ref, k_ref, h1_ref, h2_ref, wm_ref, we_ref, top, bottom, kern, wide, ev, od, sems):
-    g, views, _, wid, c = top.shape
-    rows = x_ref.shape[2]
+def partial_sums(refs, places, wm_ref, we_ref, h1_ref, h2_ref, b, first):
+    g, _, n, c = refs[0].shape
+    m = g * n
+    top, low, last = places
+    up = jnp.dot(side_blocks(refs, [(0, top), (1, top)], m), wm_ref[8 * c:, :], preferred_element_type=f32)
+    side = jnp.dot(side_blocks(refs, [(0, top)], m), we_ref[4 * c:5 * c, :c], preferred_element_type=f32)
+    up = shifted_sum(up[:, :c], up[:, c:], side, n).astype(bf16).reshape(g, n, c)
+    dn = jnp.dot(side_blocks(refs, [(0, low), (1, low), (0, last), (1, last)], m), wm_ref[:4 * c, :], preferred_element_type=f32)
+    side = jnp.dot(side_blocks(refs, [(0, low), (0, last)], m), we_ref[:2 * c, :c], preferred_element_type=f32)
+    dn = shifted_sum(dn[:, :c], dn[:, c:], side, n).astype(bf16).reshape(g, n, c)
+    h1_ref[:, b] = jnp.where(first, dn, up)
+    h2_ref[:, b] = jnp.where(first, up, dn)
+
+
+def conv_kernel(base, starts, x_ref, k_ref, *rest):
+    outs, (xs, kern, wide, ev, od, wm_ref, we_ref, sems) = rest[:-8], rest[-8:]
+    count, g, rows, wid, c = xs.shape
     n = wid // 2
     m = g * n
-    weights = pltpu.make_async_copy(k_ref, kern, sems.at[2 * views])
+
+    def fetch(b):
+        return pltpu.make_async_copy(x_ref.at[:, base + b], xs.at[b], sems.at[b])
+
+    weights = pltpu.make_async_copy(k_ref, kern, sems.at[count])
     weights.start()
-
-    def pieces(b):
-        return (
-            pltpu.make_async_copy(x_ref.at[:, b, 0:1], top.at[:, b], sems.at[2 * b]),
-            pltpu.make_async_copy(x_ref.at[:, b, rows - 2:rows], bottom.at[:, b], sems.at[2 * b + 1]),
-        )
-
-    for b in range(views):
-        for piece in pieces(b):
-            piece.start()
+    for b in range(count):
+        fetch(b).start()
     weights.wait()
     main_weights(kern, wm_ref)
     z = jnp.zeros((c, c), bf16)
     for j in range(7):
         we_ref[j * c:(j + 1) * c, :c] = kern[j, 4] if j < 5 else z
         we_ref[j * c:(j + 1) * c, c:] = kern[j - 2, 4] if j > 1 else z
-    first = lax.axis_index("view") < 2
-    refs = (ev, od)
-
-    def step(b, carry):
-        for piece in pieces(b):
-            piece.wait()
-        for v in range(g):
-            split_columns(top.at[:, b], v, 0, wide, ev, od, 0)
-            split_columns(bottom.at[:, b], v, 0, wide, ev, od, 1)
-            split_columns(bottom.at[:, b], v, 1, wide, ev, od, 2)
-        up = jnp.dot(side_blocks(refs, [(0, 0), (1, 0)], m), wm_ref[8 * c:, :], preferred_element_type=f32)
-        side = jnp.dot(side_blocks(refs, [(0, 0)], m), we_ref[4 * c:5 * c, :c], preferred_element_type=f32)
-        up = shifted_sum(up[:, :c], up[:, c:], side, n).astype(bf16).reshape(g, n, c)
-        dn = jnp.dot(side_blocks(refs, [(0, 1), (1, 1), (0, 2), (1, 2)], m), wm_ref[:4 * c, :], preferred_element_type=f32)
-        side = jnp.dot(side_blocks(refs, [(0, 1), (0, 2)], m), we_ref[:2 * c, :c], preferred_element_type=f32)
-        dn = shifted_sum(dn[:, :c], dn[:, c:], side, n).astype(bf16).reshape(g, n, c)
-        h1_ref[:, b] = jnp.where(first, dn, up)
-        h2_ref[:, b] = jnp.where(first, up, dn)
-        return carry
-
-    lax.fori_loop(0, views, step, 0)
-
-
-def halo_sums(features, kernel):
-    U, V, H, W, C = features.shape
-    n = W // 2
-    whole = pl.BlockSpec(memory_space=pltpu.VMEM)
-    return pl.pallas_call(
-        halo_kernel,
-        in_specs=[pl.BlockSpec(memory_space=pl.ANY)] * 2,
-        out_specs=[whole] * 4,
-        scratch_shapes=[
-            pltpu.VMEM((U, V, 1, W, C), bf16), pltpu.VMEM((U, V, 2, W, C), bf16), pltpu.VMEM(kernel.shape, bf16),
-            pltpu.VMEM((3, W, C), f32), pltpu.VMEM((U, 3, n, C), bf16), pltpu.VMEM((U, 3, n, C), bf16),
-            pltpu.SemaphoreType.DMA((2 * V + 1,)),
-        ],
-        out_shape=[jax.ShapeDtypeStruct((U, V, n, C), bf16)] * 2
-        + [jax.ShapeDtypeStruct((taps * C, 2 * C), bf16) for taps in (10, 7)],
-        compiler_params=pltpu.CompilerParams(vmem_limit_bytes=57 * 2**20),
-        cost_estimate=SMALL,
-        name="halo",
-    )(features, kernel)
-
-
-def conv_kernel(base, starts, x_ref, wm_ref, we_ref, *rest):
-    outs, (xs, wide, ev, od, sems) = rest[:-5], rest[-5:]
-    count, g, rows, wid, c = xs.shape
-    n = wid // 2
-    m = g * n
-
-    def fetch(b):
-        return pltpu.make_async_copy(x_ref.at[:, base + b], xs.at[b], sems.at[b])
-
-    for b in range(count):
-        fetch(b).start()
     first = lax.axis_index("view") < 2
     refs = (ev, od)
 
@@ -144,6 +99,7 @@
         own_ref[1, :, at] = jnp.where(first, r1, r3)
         oth_ref[0, :, at] = jnp.where(first, r2, r0)
         oth_ref[1, :, at] = jnp.where(first, r3, r1)
+        partial_sums(refs, (0, rows - 2, rows - 1), wm_ref, we_ref, outs[-2], outs[-1], b, first)
         return carry
 
     for q, start in enumerate(starts):
@@ -151,7 +107,7 @@
         lax.fori_loop(start, end, functools.partial(step, outs[2 * q], outs[2 * q + 1], start), 0)
 
 
-def conv_chunks(features, wm, we, spans):
+def conv_chunks(features, kernel, spans, mib):
     U, V, H, W, C = features.shape
     n = W // 2
     base = spans[0][0]
@@ -161,18 +117,20 @@
     whole = pl.BlockSpec(memory_space=pltpu.VMEM)
     return pl.pallas_call(
         functools.partial(conv_kernel, base, starts),
-        in_specs=[pl.BlockSpec(memory_space=pl.ANY), whole, whole],
-        out_specs=[whole] * (2 * len(spans)),
+        in_specs=[pl.BlockSpec(memory_space=pl.ANY)] * 2,
+        out_specs=[whole] * (2 * len(spans) + 2),
         scratch_shapes=[
-            pltpu.VMEM((count, U, H, W, C), bf16),
+            pltpu.VMEM((count, U, H, W, C), bf16), pltpu.VMEM(kernel.shape, bf16),
             pltpu.VMEM((H, W, C), f32), pltpu.VMEM((U, H, n, C), bf16), pltpu.VMEM((U, H, n, C), bf16),
-            pltpu.SemaphoreType.DMA((count,)),
+            pltpu.VMEM((10 * C, 2 * C), bf16), pltpu.VMEM((7 * C, 2 * C), bf16),
+            pltpu.SemaphoreType.DMA((count + 1,)),
         ],
-        out_shape=[jax.ShapeDtypeStruct((2, U, hi - lo, n, C), bf16) for lo, hi in spans for _ in range(2)],
-        compiler_params=pltpu.CompilerParams(vmem_limit_bytes=46 * 2**20),
+        out_shape=[jax.ShapeDtypeStruct((2, U, hi - lo, n, C), bf16) for lo, hi in spans for _ in range(2)]
+        + [jax.ShapeDtypeStruct((U, count, n, C), bf16)] * 2,
+        compiler_params=pltpu.CompilerParams(vmem_limit_bytes=mib * 2**20),
         cost_estimate=SMALL,
         name="conv",
-    )(features, wm, we)
+    )(features, kernel)
 
 
 def norm_kernel(lo, own_ref, oth_ref, h1_ref, h2_ref, floor_ref, mix_ref, mine_ref, *give_refs):
@@ -308,8 +266,8 @@
     )(*args)
 
 
-CHUNKS = ((0, 4), (4, 9), (9, 12))
-PARTS = (1, 2, 1)
+CHUNKS = ((0, 5), (5, 9), (9, 12))
+PARTS = (2, 2, 1)
 
 
 def shards(features, analysis_kernel, norm_floor, norm_mixing, epipolar_kernel, epipolar_bias):
@@ -327,19 +285,16 @@
             pairs += [(v * bands + r, (v ^ flip) * bands + r + step) for r in range(bands) if 0 <= r + step < bands]
         return pairs
     core = [(v, v ^ 1) for v in range(views)]
-    h1_sum, h2_sum, wm, we = halo_sums(features, analysis_kernel)
-    h1 = lax.ppermute(h1_sum, both, hop(0))
-    h2 = lax.ppermute(h2_sum, both, hop(2))
-    rows, sent = [], []
-    features, last = lax.optimization_barrier((features, h1_sum))
-    for spans in (CHUNKS[:1], CHUNKS[1:]):
-        done = conv_chunks(features, wm, we, spans)
-        rows += done[::2]
-        sent += done[1::2]
-        features, last = lax.optimization_barrier((features, done[0]))
-    sent[0] = lax.ppermute(sent[0], both, swap)
-    sent[1], h1, h2 = lax.optimization_barrier((sent[1], h1, h2))
-    sent[1] = lax.ppermute(sent[1], both, swap)
+    cut = CHUNKS[0][1]
+    own0, oth0, h1, h2 = conv_chunks(features, analysis_kernel, CHUNKS[:1], 46)
+    features, own0 = lax.optimization_barrier((features, own0))
+    early = [lax.ppermute(h1, both, hop(0)), lax.ppermute(h2, both, hop(2))]
+    oth0 = lax.ppermute(oth0, both, swap)
+    own1, oth1, own2, oth2, h1, h2 = conv_chunks(features, analysis_kernel, CHUNKS[1:], 46)
+    h1, h2, oth1, *early = lax.optimization_barrier((h1, h2, oth1, *early))
+    late = [lax.ppermute(h1, both, hop(0)), lax.ppermute(h2, both, hop(2))]
+    oth1 = lax.ppermute(oth1, both, swap)
+    rows, sent = [own0, own1, own2], [oth0, oth1, oth2]
     sources = []
     out = None
     done = 0
@@ -349,7 +304,8 @@
             oth, rows[-1] = lax.optimization_barrier((oth, rows[-1]))
         else:
             oth, out = lax.optimization_barrier((oth, out))
-        mine, *give = norm_chunk(own, oth, h1, h2, floor, norm_mixing, lo, PARTS[i])
+        h1, h2 = late if i else early
+        mine, *give = norm_chunk(own, oth, h1, h2, floor, norm_mixing, lo - cut if i else 0, PARTS[i])
         flipped = [lax.ppermute(g, "view", core) for g in give]
         sources.append((mine, flipped))
         upto = V if hi == V else hi - 1

time: 114 us -> 123 us (1.079)
  the two profiles are of different devices: /device:TPU:121 before, /device:TPU:37 now
where the time goes in v6:
time: 123 us
  Pallas kernels  53.9 us (44%)
  waiting for transfers between devices  46.5 us (38%)
  starting transfers between devices  20.5 us (17%)
  local copies, waits for them, and re-layouts  1.25 us (1%)
    pallas_call x3, Pallas kernels, epi_chunk(): pl.pallas_call(functools.partial(epi_kernel, tuple(pieces), v0, v1, int(p...  27 us
    pallas_call x2, Pallas kernels, conv_chunks(): pl.pallas_call(functools.partial(conv_kernel, base, starts), in_specs=[pl...  23.4 us
    ppermute x1, waiting for transfers between devices, shards(): oth1 = lax.ppermute(oth1, both, swap)  16.8 us
    ppermute x2, waiting for transfers between devices, shards(): early = [lax.ppermute(h1, both, hop(0)), lax.ppermute(h2, both, hop(2))]  14.3 us
    ppermute x2, waiting for transfers between devices, shards(): late = [lax.ppermute(h1, both, hop(0)), lax.ppermute(h2, both, hop(2))]  10.1 us
    ppermute x2, starting transfers between devices, shards(): late = [lax.ppermute(h1, both, hop(0)), lax.ppermute(h2, both, hop(2))]  5.46 us
    ppermute x5, waiting for transfers between devices, shards(): flipped = [lax.ppermute(g, 'view', core) for g in give]  5.27 us
    ppermute x2, starting transfers between devices, shards(): early = [lax.ppermute(h1, both, hop(0)), lax.ppermute(h2, both, hop(2))]  5.18 us
  transfers between devices with their start and end apart: 12, of which 9 were waited for; matrix products, arithmetic and copies ran while one was open for 0% of the time, Pallas kernels for 28%

profile of v6, /device:TPU:37, one launch (start us, length us, event | category | flops | bytes accessed | tf_op | source)
XLA Modules:
  0.0 122.5 jit_solution(9305914213155272254)
XLA Ops:
  0.0 0.0 copy-start
  0.0 1.1 copy-done
  1.1 10.0 %conv.2 = (bf16[2,3,5,128,128]{4,3,2,1,0:T(8,128)(2,1)S(1)}, bf16[2,3,5,128,128]{4,3,2,1,0:T(8,128)(2,1)S(1)}, bf16[3,5,128,128]{3,2,1,0:T(8,128)(2,1)S(1)}, bf16[3,5,128,128]{3,2,1,0:T(8,128)(2,1)S(1)}) custom-call(bf16[3,12,8,256,128]{4,3,2,1,0:T(8,128)(2,1)} %x_ref.2, bf16[5,5,128,128]{3,2,1,0:T(8,128)(2,1)S(1)} %copy-done), custom_call_target="tpu_custom_call" | custom-call | flops 1000 | bytes 1000 | tf_op jit(solution)/shard_map/conv/pallas_call | solution.py:118
  11.1 2.8 %collective-permute-start.3 = (bf16[2,3,5,128,128]{4,3,2,1,0:T(8,128)(2,1)S(1)}, bf16[2,3,5,128,128]{4,3,2,1,0:T(8,128)(2,1)S(1)}, u32[]{:S(2)}, u32[]{:S(2)}) collective-permute-start(bf16[2,3,5,128,128]{4,3,2,1,0:T(8,128)(2,1)S(1)} %get-tuple-element.49), channel_id=1, source_target_pairs={{0,64},{1,65},{2,66},{3,67},{4,68},{5,69},{6,70},{7,71},{8,72},{9,... | collective-permute-start | bytes 2949128 | tf_op jit(solution)/shard_map/ppermute | solution.py:292
  13.9 3.3 %collective-permute-start = (bf16[3,5,128,128]{3,2,1,0:T(8,128)(2,1)S(1)}, bf16[3,5,128,128]{3,2,1,0:T(8,128)(2,1)S(1)}, u32[]{:S(2)}, u32[]{:S(2)}) collective-permute-start(bf16[3,5,128,128]{3,2,1,0:T(8,128)(2,1)S(1)} %get-tuple-element.44), channel_id=1, source_target_pairs={{0,1},{1,2},{2,3},{3,4},{4,5},{5,6},{6,7},{7,8},{8,9},{9,10},{10,1... | collective-permute-start | bytes 1474568 | tf_op jit(solution)/shard_map/ppermute | solution.py:291
  17.2 1.9 %collective-permute-start.1 = (bf16[3,5,128,128]{3,2,1,0:T(8,128)(2,1)S(1)}, bf16[3,5,128,128]{3,2,1,0:T(8,128)(2,1)S(1)}, u32[]{:S(2)}, u32[]{:S(2)}) collective-permute-start(bf16[3,5,128,128]{3,2,1,0:T(8,128)(2,1)S(1)} %get-tuple-element.45), channel_id=1, source_target_pairs={{1,64},{2,65},{3,66},{4,67},{5,68},{6,69},{7,70},{8,71},{9,72},{10... | collective-permute-start | bytes 1474568 | tf_op jit(solution)/shard_map/ppermute | solution.py:291
  19.1 0.0 copy-start.1
  19.1 0.0 copy-start.2
  19.1 13.4 %conv.3 = (bf16[2,3,4,128,128]{4,3,2,1,0:T(8,128)(2,1)S(1)}, bf16[2,3,4,128,128]{4,3,2,1,0:T(8,128)(2,1)S(1)}, bf16[2,3,3,128,128]{4,3,2,1,0:T(8,128)(2,1)S(1)},...) custom-call(bf16[3,12,8,256,128]{4,3,2,1,0:T(8,128)(2,1)} %x_ref.2, ...), custom_call_target="tpu_custom_call" | custom-call | flops 1000 | bytes 1000 | tf_op jit(solution)/shard_map/conv/pallas_call | solution.py:118
  32.6 0.0 copy-start.4
  32.6 13.8 %collective-permute-done.h1_ref = bf16[3,5,128,128]{3,2,1,0:T(8,128)(2,1)S(1)} collective-permute-done((bf16[3,5,128,128]{3,2,1,0:T(8,128)(2,1)S(1)}, bf16[3,5,128,128]{3,2,1,0:T(8,128)(2,1)S(1)}, u32[]{:S(2)}, u32[]{:S(2)}) %collective-permute-start) | collective-permute-done | bytes 491552 | tf_op jit(solution)/shard_map/ppermute | solution.py:291
  46.4 0.6 collective-permute-done.1.h2_ref
  46.9 1.9 %collective-permute-start.6 = (bf16[3,7,128,128]{3,2,1,0:T(8,128)(2,1)S(1)}, bf16[3,7,128,128]{3,2,1,0:T(8,128)(2,1)S(1)}, u32[]{:S(2)}, u32[]{:S(2)}) collective-permute-start(bf16[3,7,128,128]{3,2,1,0:T(8,128)(2,1)S(1)} %get-tuple-element.59), channel_id=1, source_target_pairs={{0,1},{1,2},{2,3},{3,4},{4,5},{5,6},{6,7},{7,8},{8,9},{9,10},{10,1... | collective-permute-start | bytes 2064392 | tf_op jit(solution)/shard_map/ppermute | solution.py:295
  48.9 3.5 %collective-permute-start.7 = (bf16[3,7,128,128]{3,2,1,0:T(8,128)(2,1)S(1)}, bf16[3,7,128,128]{3,2,1,0:T(8,128)(2,1)S(1)}, u32[]{:S(2)}, u32[]{:S(2)}) collective-permute-start(bf16[3,7,128,128]{3,2,1,0:T(8,128)(2,1)S(1)} %get-tuple-element.60), channel_id=1, source_target_pairs={{1,64},{2,65},{3,66},{4,67},{5,68},{6,69},{7,70},{8,71},{9,72},{10... | collective-permute-start | bytes 2064392 | tf_op jit(solution)/shard_map/ppermute | solution.py:295
  52.4 2.3 %collective-permute-start.2 = (bf16[2,3,4,128,128]{4,3,2,1,0:T(8,128)(2,1)S(1)}, bf16[2,3,4,128,128]{4,3,2,1,0:T(8,128)(2,1)S(1)}, u32[]{:S(2)}, u32[]{:S(2)}) collective-permute-start(bf16[2,3,4,128,128]{4,3,2,1,0:T(8,128)(2,1)S(1)} %get-tuple-element.46), channel_id=1, source_target_pairs={{0,64},{1,65},{2,66},{3,67},{4,68},{5,69},{6,70},{7,71},{8,72},{9,... | collective-permute-start | bytes 2359304 | tf_op jit(solution)/shard_map/ppermute | solution.py:296
  54.7 0.0 collective-permute-done.3.oth_ref
  54.7 0.0 copy-done.1
  54.7 0.0 copy-done.2
  54.7 1.5 %norm.3 = (bf16[2,3,5,128,128]{4,3,2,1,0:T(8,128)(2,1)S(1)}, bf16[3,5,128,128]{3,2,1,0:T(8,128)(2,1)S(1)}, bf16[3,5,128,128]{3,2,1,0:T(8,128)(2,1)S(1)}) custom-call(bf16[2,3,5,128,128]{4,3,2,1,0:T(8,128)(2,1)S(1)} %get-tuple-element.48.own_ref, bf16[2,3,5,128,128]{4,3,2,1,0:T(8,128)(2,1)S(1)} %collective-permute-done.3.oth_ref, ...), custom_call_target="tpu_custom_call" | custom-call | flops 1000 | bytes 1000 | tf_op jit(solution)/shard_map/norm/pallas_call | solution.py:163
  56.2 1.9 %collective-permute-start.4 = (bf16[3,5,128,128]{3,2,1,0:T(8,128)(2,1)S(1)}, bf16[3,5,128,128]{3,2,1,0:T(8,128)(2,1)S(1)}, u32[]{:S(2)}, u32[]{:S(2)}) collective-permute-start(bf16[3,5,128,128]{3,2,1,0:T(8,128)(2,1)S(1)} %get-tuple-element.55), channel_id=1, source_target_pairs={{0,32},{32,0},{64,96},{96,64},{1,33},{33,1},{65,97},{97,65},{2,34}... | collective-permute-start | bytes 1474568 | tf_op jit(solution)/shard_map/ppermute | solution.py:309
  58.1 0.1 collective-permute-start.5
  58.2 0.0 copy-done.4
  58.2 0.1 slice_bitcast_fusion
  58.3 0.0 copy-start.3
  58.3 0.1 fusion.2
  58.4 0.1 pad_maximum_fusion.refs_3_.refs_6_.refs_5_
  58.5 1.1 collective-permute-done.4.refs_1_
  59.6 0.7 collective-permute-done.5.refs_2_
  60.3 0.0 copy-done.3
  60.3 8.9 %epi.3.refs_9_ = bf16[12,12,1,128,128]{4,3,2,1,0:T(8,128)(2,1)} custom-call(bf16[2,3,5,128,128]{4,3,2,1,0:T(8,128)(2,1)S(1)} %get-tuple-element.54.refs_0_, bf16[3,5,128,128]{3,2,1,0:T(8,128)(2,1)S(1)} %collective-permute-done.4.refs_1_, bf16[3,5,128,128]{3,2,1,0:T(8,128)(2,1)S(1)} %collective-permute-done.5.refs_2_, ...), custom_call_target="tpu_custom_call" | custom-call | flops 1000 | bytes 1000 | tf_op jit(solution)/shard_map/epi/pallas_call | solution.py:250
  69.3 0.1 collective-permute-start.10
  69.3 16.8 %collective-permute-done.2.oth_ref = bf16[2,3,4,128,128]{4,3,2,1,0:T(8,128)(2,1)S(1)} collective-permute-done((bf16[2,3,4,128,128]{4,3,2,1,0:T(8,128)(2,1)S(1)}, bf16[2,3,4,128,128]{4,3,2,1,0:T(8,128)(2,1)S(1)}, u32[]{:S(2)}, u32[]{:S(2)}) %collective-permute-start.2) | collective-permute-done | bytes 786464 | tf_op jit(solution)/shard_map/ppermute | solution.py:296
  86.1 0.0 collective-permute-done.6.h1_ref
  86.1 10.1 %collective-permute-done.7.h2_ref = bf16[3,7,128,128]{3,2,1,0:T(8,128)(2,1)S(1)} collective-permute-done((bf16[3,7,128,128]{3,2,1,0:T(8,128)(2,1)S(1)}, bf16[3,7,128,128]{3,2,1,0:T(8,128)(2,1)S(1)}, u32[]{:S(2)}, u32[]{:S(2)}) %collective-permute-start.7) | collective-permute-done | bytes 688160 | tf_op jit(solution)/shard_map/ppermute | solution.py:295
  96.2 1.2 norm.4
  97.4 2.2 %collective-permute-start.8 = (bf16[3,4,128,128]{3,2,1,0:T(8,128)(2,1)S(1)}, bf16[3,4,128,128]{3,2,1,0:T(8,128)(2,1)S(1)}, u32[]{:S(2)}, u32[]{:S(2)}) collective-permute-start(bf16[3,4,128,128]{3,2,1,0:T(8,128)(2,1)S(1)} %get-tuple-element.62), channel_id=1, source_target_pairs={{0,32},{32,0},{64,96},{96,64},{1,33},{33,1},{65,97},{97,65},{2,34}... | collective-permute-start | bytes 1179656 | tf_op jit(solution)/shard_map/ppermute | solution.py:309
  99.5 0.1 collective-permute-start.9
  99.6 1.3 %collective-permute-done.8.refs_4_.refs_1_ = bf16[3,4,128,128]{3,2,1,0:T(8,128)(2,1)S(1)} collective-permute-done((bf16[3,4,128,128]{3,2,1,0:T(8,128)(2,1)S(1)}, bf16[3,4,128,128]{3,2,1,0:T(8,128)(2,1)S(1)}, u32[]{:S(2)}, u32[]{:S(2)}) %collective-permute-start.8) | collective-permute-done | bytes 393248 | tf_op jit(solution)/shard_map/ppermute | solution.py:309
  100.9 0.6 collective-permute-done.9.refs_5_.refs_2_
  101.5 9.1 %epi.4.refs_8_ = bf16[12,12,1,128,128]{4,3,2,1,0:T(8,128)(2,1)} custom-call(bf16[2,3,5,128,128]{4,3,2,1,0:T(8,128)(2,1)S(1)} %get-tuple-element.54.refs_0_, bf16[3,5,128,128]{3,2,1,0:T(8,128)(2,1)S(1)} %collective-permute-done.4.refs_1_, bf16[3,5,128,128]{3,2,1,0:T(8,128)(2,1)S(1)} %collective-permute-done.5.refs_2_, ...), custom_call_target="tpu_custom_call", output_to_operand_aliasing={{}: (9, {})} | custom-call | flops 1000 | bytes 1000 | tf_op jit(solution)/shard_map/epi/pallas_call | solution.py:250
  110.5 0.0 collective-permute-done.10.oth_ref
  110.6 0.9 norm.5
  111.5 0.5 collective-permute-start.11
  111.9 1.6 %collective-permute-done.11.refs_4_ = bf16[2,3,3,128,128]{4,3,2,1,0:T(8,128)(2,1)S(1)} collective-permute-done((bf16[2,3,3,128,128]{4,3,2,1,0:T(8,128)(2,1)S(1)}, bf16[2,3,3,128,128]{4,3,2,1,0:T(8,128)(2,1)S(1)}, u32[]{:S(2)}, u32[]{:S(2)}) %collective-permute-start.11) | collective-permute-done | bytes 589856 | tf_op jit(solution)/shard_map/ppermute | solution.py:309
  113.5 9.0 %epi.5 = bf16[12,12,1,128,128]{4,3,2,1,0:T(8,128)(2,1)} custom-call(bf16[2,3,4,128,128]{4,3,2,1,0:T(8,128)(2,1)S(1)} %get-tuple-element.61.refs_3_.refs_0_, bf16[3,4,128,128]{3,2,1,0:T(8,128)(2,1)S(1)} %collective-permute-done.8.refs_4_.refs_1_, bf16[3,4,128,128]{3,2,1,0:T(8,128)(2,1)S(1)} %collective-permute-done.9.refs_5_.refs_2_, ...), custom_call_target="tpu_custom_call", output_to_operand_aliasing={{}: (8, {})} | custom-call | flops 1000 | bytes 1000 | tf_op jit(solution)/shard_map/epi/pallas_call | solution.py:250
Async XLA Ops:
  0.0 1.1 copy-start
  11.1 43.6 %collective-permute-start.3 = (bf16[2,3,5,128,128]{4,3,2,1,0:T(8,128)(2,1)S(1)}, bf16[2,3,5,128,128]{4,3,2,1,0:T(8,128)(2,1)S(1)}, u32[]{:S(2)}, u32[]{:S(2)}) collective-permute-start(bf16[2,3,5,128,128]{4,3,2,1,0:T(8,128)(2,1)S(1)} %get-tuple-element.49), channel_id=1, source_target_pairs={{0,64},{1,65},{2,66},{3,67},{4,68},{5,69},{6,70},{7,71},{8,72},{9,... | collective-permute-start | bytes 2949128 | tf_op jit(solution)/shard_map/ppermute | solution.py:292
  13.9 32.5 %collective-permute-start = (bf16[3,5,128,128]{3,2,1,0:T(8,128)(2,1)S(1)}, bf16[3,5,128,128]{3,2,1,0:T(8,128)(2,1)S(1)}, u32[]{:S(2)}, u32[]{:S(2)}) collective-permute-start(bf16[3,5,128,128]{3,2,1,0:T(8,128)(2,1)S(1)} %get-tuple-element.44), channel_id=1, source_target_pairs={{0,1},{1,2},{2,3},{3,4},{4,5},{5,6},{6,7},{7,8},{8,9},{9,10},{10,1... | collective-permute-start | bytes 1474568 | tf_op jit(solution)/shard_map/ppermute | solution.py:291
  17.2 29.7 %collective-permute-start.1 = (bf16[3,5,128,128]{3,2,1,0:T(8,128)(2,1)S(1)}, bf16[3,5,128,128]{3,2,1,0:T(8,128)(2,1)S(1)}, u32[]{:S(2)}, u32[]{:S(2)}) collective-permute-start(bf16[3,5,128,128]{3,2,1,0:T(8,128)(2,1)S(1)} %get-tuple-element.45), channel_id=1, source_target_pairs={{1,64},{2,65},{3,66},{4,67},{5,68},{6,69},{7,70},{8,71},{9,72},{10... | collective-permute-start | bytes 1474568 | tf_op jit(solution)/shard_map/ppermute | solution.py:291
  19.1 35.6 %copy-start.1 = (f32[128,128]{1,0:T(8,128)S(1)}, f32[128,128]{1,0:T(8,128)}, u32[]{:S(2)}) copy-start(f32[128,128]{1,0:T(8,128)} %mix_ref.5) | copy-start | bytes 196612
  19.1 35.6 %copy-start.2 = (f32[128]{0:T(128)S(1)}, f32[128]{0:T(128)}, u32[]{:S(2)}) copy-start(f32[128]{0:T(128)} %param.8) | copy-start | bytes 1540
  32.6 25.6 %copy-start.4 = (bf16[3,3,3,128,128]{4,3,2,1,0:T(8,128)(2,1)S(1)}, bf16[3,3,3,128,128]{4,3,2,1,0:T(8,128)(2,1)}, u32[]{:S(2)}) copy-start(bf16[3,3,3,128,128]{4,3,2,1,0:T(8,128)(2,1)} %param.10) | copy-start | bytes 2654212
  46.9 39.2 %collective-permute-start.6 = (bf16[3,7,128,128]{3,2,1,0:T(8,128)(2,1)S(1)}, bf16[3,7,128,128]{3,2,1,0:T(8,128)(2,1)S(1)}, u32[]{:S(2)}, u32[]{:S(2)}) collective-permute-start(bf16[3,7,128,128]{3,2,1,0:T(8,128)(2,1)S(1)} %get-tuple-element.59), channel_id=1, source_target_pairs={{0,1},{1,2},{2,3},{3,4},{4,5},{5,6},{6,7},{7,8},{8,9},{9,10},{10,1... | collective-permute-start | bytes 2064392 | tf_op jit(solution)/shard_map/ppermute | solution.py:295
  48.9 47.3 %collective-permute-start.7 = (bf16[3,7,128,128]{3,2,1,0:T(8,128)(2,1)S(1)}, bf16[3,7,128,128]{3,2,1,0:T(8,128)(2,1)S(1)}, u32[]{:S(2)}, u32[]{:S(2)}) collective-permute-start(bf16[3,7,128,128]{3,2,1,0:T(8,128)(2,1)S(1)} %get-tuple-element.60), channel_id=1, source_target_pairs={{1,64},{2,65},{3,66},{4,67},{5,68},{6,69},{7,70},{8,71},{9,72},{10... | collective-permute-start | bytes 2064392 | tf_op jit(solution)/shard_map/ppermute | solution.py:295
  52.4 33.7 %collective-permute-start.2 = (bf16[2,3,4,128,128]{4,3,2,1,0:T(8,128)(2,1)S(1)}, bf16[2,3,4,128,128]{4,3,2,1,0:T(8,128)(2,1)S(1)}, u32[]{:S(2)}, u32[]{:S(2)}) collective-permute-start(bf16[2,3,4,128,128]{4,3,2,1,0:T(8,128)(2,1)S(1)} %get-tuple-element.46), channel_id=1, source_target_pairs={{0,64},{1,65},{2,66},{3,67},{4,68},{5,69},{6,70},{7,71},{8,72},{9,... | collective-permute-start | bytes 2359304 | tf_op jit(solution)/shard_map/ppermute | solution.py:296
  56.2 3.4 %collective-permute-start.4 = (bf16[3,5,128,128]{3,2,1,0:T(8,128)(2,1)S(1)}, bf16[3,5,128,128]{3,2,1,0:T(8,128)(2,1)S(1)}, u32[]{:S(2)}, u32[]{:S(2)}) collective-permute-start(bf16[3,5,128,128]{3,2,1,0:T(8,128)(2,1)S(1)} %get-tuple-element.55), channel_id=1, source_target_pairs={{0,32},{32,0},{64,96},{96,64},{1,33},{33,1},{65,97},{97,65},{2,34}... | collective-permute-start | bytes 1474568 | tf_op jit(solution)/shard_map/ppermute | solution.py:309
  58.1 2.2 %collective-permute-start.5 = (bf16[3,5,128,128]{3,2,1,0:T(8,128)(2,1)S(1)}, bf16[3,5,128,128]{3,2,1,0:T(8,128)(2,1)S(1)}, u32[]{:S(2)}, u32[]{:S(2)}) collective-permute-start(bf16[3,5,128,128]{3,2,1,0:T(8,128)(2,1)S(1)} %get-tuple-element.56), channel_id=1, source_target_pairs={{0,32},{32,0},{64,96},{96,64},{1,33},{33,1},{65,97},{97,65},{2,34}... | collective-permute-start | bytes 1474568 | tf_op jit(solution)/shard_map/ppermute | solution.py:309
  58.3 2.0 %copy-start.3 = (f32[128]{0:T(128)S(1)}, f32[128]{0:T(128)}, u32[]{:S(2)}) copy-start(f32[128]{0:T(128)} %param.11) | copy-start | bytes 1540
  69.3 41.3 %collective-permute-start.10 = (bf16[2,3,3,128,128]{4,3,2,1,0:T(8,128)(2,1)S(1)}, bf16[2,3,3,128,128]{4,3,2,1,0:T(8,128)(2,1)S(1)}, u32[]{:S(2)}, u32[]{:S(2)}) collective-permute-start(bf16[2,3,3,128,128]{4,3,2,1,0:T(8,128)(2,1)S(1)} %get-tuple-element.65), channel_id=1, source_target_pairs={{0,64},{1,65},{2,66},{3,67},{4,68},{5,69},{6,70},{7,71},{8,72},{9,... | collective-permute-start | bytes 1769480 | tf_op jit(solution)/shard_map/ppermute | solution.py:316
  97.4 3.5 %collective-permute-start.8 = (bf16[3,4,128,128]{3,2,1,0:T(8,128)(2,1)S(1)}, bf16[3,4,128,128]{3,2,1,0:T(8,128)(2,1)S(1)}, u32[]{:S(2)}, u32[]{:S(2)}) collective-permute-start(bf16[3,4,128,128]{3,2,1,0:T(8,128)(2,1)S(1)} %get-tuple-element.62), channel_id=1, source_target_pairs={{0,32},{32,0},{64,96},{96,64},{1,33},{33,1},{65,97},{97,65},{2,34}... | collective-permute-start | bytes 1179656 | tf_op jit(solution)/shard_map/ppermute | solution.py:309
  99.5 1.9 %collective-permute-start.9 = (bf16[3,4,128,128]{3,2,1,0:T(8,128)(2,1)S(1)}, bf16[3,4,128,128]{3,2,1,0:T(8,128)(2,1)S(1)}, u32[]{:S(2)}, u32[]{:S(2)}) collective-permute-start(bf16[3,4,128,128]{3,2,1,0:T(8,128)(2,1)S(1)} %get-tuple-element.63), channel_id=1, source_target_pairs={{0,32},{32,0},{64,96},{96,64},{1,33},{33,1},{65,97},{97,65},{2,34}... | collective-permute-start | bytes 1179656 | tf_op jit(solution)/shard_map/ppermute | solution.py:309
  111.5 2.1 %collective-permute-start.11 = (bf16[2,3,3,128,128]{4,3,2,1,0:T(8,128)(2,1)S(1)}, bf16[2,3,3,128,128]{4,3,2,1,0:T(8,128)(2,1)S(1)}, u32[]{:S(2)}, u32[]{:S(2)}) collective-permute-start(bf16[2,3,3,128,128]{4,3,2,1,0:T(8,128)(2,1)S(1)} %get-tuple-element.69), channel_id=1, source_target_pairs={{0,32},{32,0},{64,96},{96,64},{1,33},{33,1},{65,97},{97,65},{2,34}... | collective-permute-start | bytes 1769480 | tf_op jit(solution)/shard_map/ppermute | solution.py:309

commit v7 on v6

--- a/solution.py
+++ b/solution.py
@@ -291,8 +291,8 @@
     early = [lax.ppermute(h1, both, hop(0)), lax.ppermute(h2, both, hop(2))]
     oth0 = lax.ppermute(oth0, both, swap)
     own1, oth1, own2, oth2, h1, h2 = conv_chunks(features, analysis_kernel, CHUNKS[1:], 46)
-    h1, h2, oth1, *early = lax.optimization_barrier((h1, h2, oth1, *early))
     late = [lax.ppermute(h1, both, hop(0)), lax.ppermute(h2, both, hop(2))]
+    oth1, *early = lax.optimization_barrier((oth1, *early))
     oth1 = lax.ppermute(oth1, both, swap)
     rows, sent = [own0, own1, own2], [oth0, oth1, oth2]
     sources = []

time: 123 us -> 116 us (0.943)
  the two profiles are of different devices: /device:TPU:37 before, /device:TPU:25 now
where the time goes in v7:
time: 116 us
  Pallas kernels  53.9 us (46%)
  waiting for transfers between devices  32.3 us (28%)
  starting transfers between devices  27.8 us (24%)
  local copies, waits for them, and re-layouts  1.25 us (1%)
    pallas_call x3, Pallas kernels, epi_chunk(): pl.pallas_call(functools.partial(epi_kernel, tuple(pieces), v0, v1, int(p...  27 us
    pallas_call x2, Pallas kernels, conv_chunks(): pl.pallas_call(functools.partial(conv_kernel, base, starts), in_specs=[pl...  23.4 us
    ppermute x1, waiting for transfers between devices, shards(): oth0 = lax.ppermute(oth0, both, swap)  21.3 us
    ppermute x2, starting transfers between devices, shards(): late = [lax.ppermute(h1, both, hop(0)), lax.ppermute(h2, both, hop(2))]  7.67 us
    ppermute x2, starting transfers between devices, shards(): early = [lax.ppermute(h1, both, hop(0)), lax.ppermute(h2, both, hop(2))]  6.62 us
    ppermute x5, waiting for transfers between devices, shards(): flipped = [lax.ppermute(g, 'view', core) for g in give]  5.27 us
    ppermute x5, starting transfers between devices, shards(): flipped = [lax.ppermute(g, 'view', core) for g in give]  5.02 us
    ppermute x1, starting transfers between devices, shards(): oth1 = lax.ppermute(oth1, both, swap)  4.71 us
  transfers between devices with their start and end apart: 12, of which 9 were waited for; matrix products, arithmetic and copies ran while one was open for 0% of the time, Pallas kernels for 29%

profile of v7, /device:TPU:25, one launch (start us, length us, event | category | flops | bytes accessed | tf_op | source)
XLA Modules:
  0.0 115.6 jit_solution(15009970497661949998)
XLA Ops:
  0.0 0.0 copy-start
  0.0 1.1 copy-done
  1.1 10.0 %conv.2 = (bf16[2,3,5,128,128]{4,3,2,1,0:T(8,128)(2,1)S(1)}, bf16[2,3,5,128,128]{4,3,2,1,0:T(8,128)(2,1)S(1)}, bf16[3,5,128,128]{3,2,1,0:T(8,128)(2,1)S(1)}, bf16[3,5,128,128]{3,2,1,0:T(8,128)(2,1)S(1)}) custom-call(bf16[3,12,8,256,128]{4,3,2,1,0:T(8,128)(2,1)} %x_ref.2, bf16[5,5,128,128]{3,2,1,0:T(8,128)(2,1)S(1)} %copy-done), custom_call_target="tpu_custom_call" | custom-call | flops 1000 | bytes 1000 | tf_op jit(solution)/shard_map/conv/pallas_call | solution.py:118
  11.1 3.7 %collective-permute-start.3 = (bf16[2,3,5,128,128]{4,3,2,1,0:T(8,128)(2,1)S(1)}, bf16[2,3,5,128,128]{4,3,2,1,0:T(8,128)(2,1)S(1)}, u32[]{:S(2)}, u32[]{:S(2)}) collective-permute-start(bf16[2,3,5,128,128]{4,3,2,1,0:T(8,128)(2,1)S(1)} %get-tuple-element.45), channel_id=1, source_target_pairs={{0,64},{1,65},{2,66},{3,67},{4,68},{5,69},{6,70},{7,71},{8,72},{9,... | collective-permute-start | bytes 2949128 | tf_op jit(solution)/shard_map/ppermute | solution.py:292
  14.8 2.6 %collective-permute-start = (bf16[3,5,128,128]{3,2,1,0:T(8,128)(2,1)S(1)}, bf16[3,5,128,128]{3,2,1,0:T(8,128)(2,1)S(1)}, u32[]{:S(2)}, u32[]{:S(2)}) collective-permute-start(bf16[3,5,128,128]{3,2,1,0:T(8,128)(2,1)S(1)} %get-tuple-element.40), channel_id=1, source_target_pairs={{0,1},{1,2},{2,3},{3,4},{4,5},{5,6},{6,7},{7,8},{8,9},{9,10},{10,1... | collective-permute-start | bytes 1474568 | tf_op jit(solution)/shard_map/ppermute | solution.py:291
  17.5 4.0 %collective-permute-start.1 = (bf16[3,5,128,128]{3,2,1,0:T(8,128)(2,1)S(1)}, bf16[3,5,128,128]{3,2,1,0:T(8,128)(2,1)S(1)}, u32[]{:S(2)}, u32[]{:S(2)}) collective-permute-start(bf16[3,5,128,128]{3,2,1,0:T(8,128)(2,1)S(1)} %get-tuple-element.41), channel_id=1, source_target_pairs={{1,64},{2,65},{3,66},{4,67},{5,68},{6,69},{7,70},{8,71},{9,72},{10... | collective-permute-start | bytes 1474568 | tf_op jit(solution)/shard_map/ppermute | solution.py:291
  21.5 0.0 copy-start.1
  21.5 0.0 copy-start.2
  21.5 13.4 %conv.3 = (bf16[2,3,4,128,128]{4,3,2,1,0:T(8,128)(2,1)S(1)}, bf16[2,3,4,128,128]{4,3,2,1,0:T(8,128)(2,1)S(1)}, bf16[2,3,3,128,128]{4,3,2,1,0:T(8,128)(2,1)S(1)},...) custom-call(bf16[3,12,8,256,128]{4,3,2,1,0:T(8,128)(2,1)} %x_ref.2, ...), custom_call_target="tpu_custom_call" | custom-call | flops 1000 | bytes 1000 | tf_op jit(solution)/shard_map/conv/pallas_call | solution.py:118
  34.9 0.0 copy-start.4
  34.9 2.9 %collective-permute-start.6 = (bf16[3,7,128,128]{3,2,1,0:T(8,128)(2,1)S(1)}, bf16[3,7,128,128]{3,2,1,0:T(8,128)(2,1)S(1)}, u32[]{:S(2)}, u32[]{:S(2)}) collective-permute-start(bf16[3,7,128,128]{3,2,1,0:T(8,128)(2,1)S(1)} %get-tuple-element.55), channel_id=1, source_target_pairs={{0,1},{1,2},{2,3},{3,4},{4,5},{5,6},{6,7},{7,8},{8,9},{9,10},{10,1... | collective-permute-start | bytes 2064392 | tf_op jit(solution)/shard_map/ppermute | solution.py:294
  37.8 4.8 %collective-permute-start.7 = (bf16[3,7,128,128]{3,2,1,0:T(8,128)(2,1)S(1)}, bf16[3,7,128,128]{3,2,1,0:T(8,128)(2,1)S(1)}, u32[]{:S(2)}, u32[]{:S(2)}) collective-permute-start(bf16[3,7,128,128]{3,2,1,0:T(8,128)(2,1)S(1)} %get-tuple-element.56), channel_id=1, source_target_pairs={{1,64},{2,65},{3,66},{4,67},{5,68},{6,69},{7,70},{8,71},{9,72},{10... | collective-permute-start | bytes 2064392 | tf_op jit(solution)/shard_map/ppermute | solution.py:294
  42.6 3.2 %collective-permute-done.h1_ref = bf16[3,5,128,128]{3,2,1,0:T(8,128)(2,1)S(1)} collective-permute-done((bf16[3,5,128,128]{3,2,1,0:T(8,128)(2,1)S(1)}, bf16[3,5,128,128]{3,2,1,0:T(8,128)(2,1)S(1)}, u32[]{:S(2)}, u32[]{:S(2)}) %collective-permute-start) | collective-permute-done | bytes 491552 | tf_op jit(solution)/shard_map/ppermute | solution.py:291
  45.8 0.0 collective-permute-done.1.h2_ref
  45.8 4.7 %collective-permute-start.2 = (bf16[2,3,4,128,128]{4,3,2,1,0:T(8,128)(2,1)S(1)}, bf16[2,3,4,128,128]{4,3,2,1,0:T(8,128)(2,1)S(1)}, u32[]{:S(2)}, u32[]{:S(2)}) collective-permute-start(bf16[2,3,4,128,128]{4,3,2,1,0:T(8,128)(2,1)S(1)} %get-tuple-element.42), channel_id=1, source_target_pairs={{0,64},{1,65},{2,66},{3,67},{4,68},{5,69},{6,70},{7,71},{8,72},{9,... | collective-permute-start | bytes 2359304 | tf_op jit(solution)/shard_map/ppermute | solution.py:296
  50.5 21.3 %collective-permute-done.3.oth_ref = bf16[2,3,5,128,128]{4,3,2,1,0:T(8,128)(2,1)S(1)} collective-permute-done((bf16[2,3,5,128,128]{4,3,2,1,0:T(8,128)(2,1)S(1)}, bf16[2,3,5,128,128]{4,3,2,1,0:T(8,128)(2,1)S(1)}, u32[]{:S(2)}, u32[]{:S(2)}) %collective-permute-start.3) | collective-permute-done | bytes 983072 | tf_op jit(solution)/shard_map/ppermute | solution.py:292
  71.9 0.0 copy-done.1
  71.9 0.0 copy-done.2
  71.9 1.5 %norm.3 = (bf16[2,3,5,128,128]{4,3,2,1,0:T(8,128)(2,1)S(1)}, bf16[3,5,128,128]{3,2,1,0:T(8,128)(2,1)S(1)}, bf16[3,5,128,128]{3,2,1,0:T(8,128)(2,1)S(1)}) custom-call(bf16[2,3,5,128,128]{4,3,2,1,0:T(8,128)(2,1)S(1)} %get-tuple-element.44.own_ref, bf16[2,3,5,128,128]{4,3,2,1,0:T(8,128)(2,1)S(1)} %collective-permute-done.3.oth_ref, ...), custom_call_target="tpu_custom_call" | custom-call | flops 1000 | bytes 1000 | tf_op jit(solution)/shard_map/norm/pallas_call | solution.py:163
  73.3 2.2 %collective-permute-start.4 = (bf16[3,5,128,128]{3,2,1,0:T(8,128)(2,1)S(1)}, bf16[3,5,128,128]{3,2,1,0:T(8,128)(2,1)S(1)}, u32[]{:S(2)}, u32[]{:S(2)}) collective-permute-start(bf16[3,5,128,128]{3,2,1,0:T(8,128)(2,1)S(1)} %get-tuple-element.51), channel_id=1, source_target_pairs={{0,32},{32,0},{64,96},{96,64},{1,33},{33,1},{65,97},{97,65},{2,34}... | collective-permute-start | bytes 1474568 | tf_op jit(solution)/shard_map/ppermute | solution.py:309
  75.5 0.1 collective-permute-start.5
  75.6 0.0 copy-done.4
  75.6 0.1 slice_bitcast_fusion
  75.7 0.0 copy-start.3
  75.7 0.1 fusion.2
  75.8 0.1 pad_maximum_fusion.refs_3_.refs_6_.refs_5_
  75.9 1.1 collective-permute-done.4.refs_1_
  77.0 0.7 collective-permute-done.5.refs_2_
  77.7 0.0 copy-done.3
  77.7 8.9 %epi.3.refs_9_ = bf16[12,12,1,128,128]{4,3,2,1,0:T(8,128)(2,1)} custom-call(bf16[2,3,5,128,128]{4,3,2,1,0:T(8,128)(2,1)S(1)} %get-tuple-element.50.refs_0_, bf16[3,5,128,128]{3,2,1,0:T(8,128)(2,1)S(1)} %collective-permute-done.4.refs_1_, bf16[3,5,128,128]{3,2,1,0:T(8,128)(2,1)S(1)} %collective-permute-done.5.refs_2_, ...), custom_call_target="tpu_custom_call" | custom-call | flops 1000 | bytes 1000 | tf_op jit(solution)/shard_map/epi/pallas_call | solution.py:250
  86.6 0.1 collective-permute-start.10
  86.7 2.0 %collective-permute-done.2.oth_ref = bf16[2,3,4,128,128]{4,3,2,1,0:T(8,128)(2,1)S(1)} collective-permute-done((bf16[2,3,4,128,128]{4,3,2,1,0:T(8,128)(2,1)S(1)}, bf16[2,3,4,128,128]{4,3,2,1,0:T(8,128)(2,1)S(1)}, u32[]{:S(2)}, u32[]{:S(2)}) %collective-permute-start.2) | collective-permute-done | bytes 786464 | tf_op jit(solution)/shard_map/ppermute | solution.py:296
  88.7 0.0 collective-permute-done.6.h1_ref
  88.7 0.0 collective-permute-done.7.h2_ref
  88.7 1.2 %norm.4 = (bf16[2,3,4,128,128]{4,3,2,1,0:T(8,128)(2,1)S(1)}, bf16[3,4,128,128]{3,2,1,0:T(8,128)(2,1)S(1)}, bf16[3,4,128,128]{3,2,1,0:T(8,128)(2,1)S(1)}) custom-call(bf16[2,3,4,128,128]{4,3,2,1,0:T(8,128)(2,1)S(1)} %get-tuple-element.38.own_ref, bf16[2,3,4,128,128]{4,3,2,1,0:T(8,128)(2,1)S(1)} %collective-permute-done.2.oth_ref, ...), custom_call_target="tpu_custom_call" | custom-call | flops 1000 | bytes 1000 | tf_op jit(solution)/shard_map/norm/pallas_call | solution.py:163
  89.9 1.4 %collective-permute-start.8 = (bf16[3,4,128,128]{3,2,1,0:T(8,128)(2,1)S(1)}, bf16[3,4,128,128]{3,2,1,0:T(8,128)(2,1)S(1)}, u32[]{:S(2)}, u32[]{:S(2)}) collective-permute-start(bf16[3,4,128,128]{3,2,1,0:T(8,128)(2,1)S(1)} %get-tuple-element.58), channel_id=1, source_target_pairs={{0,32},{32,0},{64,96},{96,64},{1,33},{33,1},{65,97},{97,65},{2,34}... | collective-permute-start | bytes 1179656 | tf_op jit(solution)/shard_map/ppermute | solution.py:309
  91.3 0.1 collective-permute-start.9
  91.4 1.3 %collective-permute-done.8.refs_4_.refs_1_ = bf16[3,4,128,128]{3,2,1,0:T(8,128)(2,1)S(1)} collective-permute-done((bf16[3,4,128,128]{3,2,1,0:T(8,128)(2,1)S(1)}, bf16[3,4,128,128]{3,2,1,0:T(8,128)(2,1)S(1)}, u32[]{:S(2)}, u32[]{:S(2)}) %collective-permute-start.8) | collective-permute-done | bytes 393248 | tf_op jit(solution)/shard_map/ppermute | solution.py:309
  92.6 0.6 collective-permute-done.9.refs_5_.refs_2_
  93.2 9.1 %epi.4.refs_8_ = bf16[12,12,1,128,128]{4,3,2,1,0:T(8,128)(2,1)} custom-call(bf16[2,3,5,128,128]{4,3,2,1,0:T(8,128)(2,1)S(1)} %get-tuple-element.50.refs_0_, bf16[3,5,128,128]{3,2,1,0:T(8,128)(2,1)S(1)} %collective-permute-done.4.refs_1_, bf16[3,5,128,128]{3,2,1,0:T(8,128)(2,1)S(1)} %collective-permute-done.5.refs_2_, ...), custom_call_target="tpu_custom_call", output_to_operand_aliasing={{}: (9, {})} | custom-call | flops 1000 | bytes 1000 | tf_op jit(solution)/shard_map/epi/pallas_call | solution.py:250
  102.3 0.5 collective-permute-done.10.oth_ref
  102.8 0.9 norm.5
  103.7 1.3 %collective-permute-start.11 = (bf16[2,3,3,128,128]{4,3,2,1,0:T(8,128)(2,1)S(1)}, bf16[2,3,3,128,128]{4,3,2,1,0:T(8,128)(2,1)S(1)}, u32[]{:S(2)}, u32[]{:S(2)}) collective-permute-start(bf16[2,3,3,128,128]{4,3,2,1,0:T(8,128)(2,1)S(1)} %get-tuple-element.65), channel_id=1, source_target_pairs={{0,32},{32,0},{64,96},{96,64},{1,33},{33,1},{65,97},{97,65},{2,34}... | collective-permute-start | bytes 1769480 | tf_op jit(solution)/shard_map/ppermute | solution.py:309
  104.9 1.6 %collective-permute-done.11.refs_4_ = bf16[2,3,3,128,128]{4,3,2,1,0:T(8,128)(2,1)S(1)} collective-permute-done((bf16[2,3,3,128,128]{4,3,2,1,0:T(8,128)(2,1)S(1)}, bf16[2,3,3,128,128]{4,3,2,1,0:T(8,128)(2,1)S(1)}, u32[]{:S(2)}, u32[]{:S(2)}) %collective-permute-start.11) | collective-permute-done | bytes 589856 | tf_op jit(solution)/shard_map/ppermute | solution.py:309
  106.6 9.0 %epi.5 = bf16[12,12,1,128,128]{4,3,2,1,0:T(8,128)(2,1)} custom-call(bf16[2,3,4,128,128]{4,3,2,1,0:T(8,128)(2,1)S(1)} %get-tuple-element.57.refs_3_.refs_0_, bf16[3,4,128,128]{3,2,1,0:T(8,128)(2,1)S(1)} %collective-permute-done.8.refs_4_.refs_1_, bf16[3,4,128,128]{3,2,1,0:T(8,128)(2,1)S(1)} %collective-permute-done.9.refs_5_.refs_2_, ...), custom_call_target="tpu_custom_call", output_to_operand_aliasing={{}: (8, {})} | custom-call | flops 1000 | bytes 1000 | tf_op jit(solution)/shard_map/epi/pallas_call | solution.py:250
Async XLA Ops:
  0.0 1.1 copy-start
  11.1 60.7 %collective-permute-start.3 = (bf16[2,3,5,128,128]{4,3,2,1,0:T(8,128)(2,1)S(1)}, bf16[2,3,5,128,128]{4,3,2,1,0:T(8,128)(2,1)S(1)}, u32[]{:S(2)}, u32[]{:S(2)}) collective-permute-start(bf16[2,3,5,128,128]{4,3,2,1,0:T(8,128)(2,1)S(1)} %get-tuple-element.45), channel_id=1, source_target_pairs={{0,64},{1,65},{2,66},{3,67},{4,68},{5,69},{6,70},{7,71},{8,72},{9,... | collective-permute-start | bytes 2949128 | tf_op jit(solution)/shard_map/ppermute | solution.py:292
  14.8 31.0 %collective-permute-start = (bf16[3,5,128,128]{3,2,1,0:T(8,128)(2,1)S(1)}, bf16[3,5,128,128]{3,2,1,0:T(8,128)(2,1)S(1)}, u32[]{:S(2)}, u32[]{:S(2)}) collective-permute-start(bf16[3,5,128,128]{3,2,1,0:T(8,128)(2,1)S(1)} %get-tuple-element.40), channel_id=1, source_target_pairs={{0,1},{1,2},{2,3},{3,4},{4,5},{5,6},{6,7},{7,8},{8,9},{9,10},{10,1... | collective-permute-start | bytes 1474568 | tf_op jit(solution)/shard_map/ppermute | solution.py:291
  17.5 28.4 %collective-permute-start.1 = (bf16[3,5,128,128]{3,2,1,0:T(8,128)(2,1)S(1)}, bf16[3,5,128,128]{3,2,1,0:T(8,128)(2,1)S(1)}, u32[]{:S(2)}, u32[]{:S(2)}) collective-permute-start(bf16[3,5,128,128]{3,2,1,0:T(8,128)(2,1)S(1)} %get-tuple-element.41), channel_id=1, source_target_pairs={{1,64},{2,65},{3,66},{4,67},{5,68},{6,69},{7,70},{8,71},{9,72},{10... | collective-permute-start | bytes 1474568 | tf_op jit(solution)/shard_map/ppermute | solution.py:291
  21.5 50.4 %copy-start.1 = (f32[128,128]{1,0:T(8,128)S(1)}, f32[128,128]{1,0:T(8,128)}, u32[]{:S(2)}) copy-start(f32[128,128]{1,0:T(8,128)} %mix_ref.5) | copy-start | bytes 196612
  21.5 50.4 %copy-start.2 = (f32[128]{0:T(128)S(1)}, f32[128]{0:T(128)}, u32[]{:S(2)}) copy-start(f32[128]{0:T(128)} %param.8) | copy-start | bytes 1540
  34.9 40.7 %copy-start.4 = (bf16[3,3,3,128,128]{4,3,2,1,0:T(8,128)(2,1)S(1)}, bf16[3,3,3,128,128]{4,3,2,1,0:T(8,128)(2,1)}, u32[]{:S(2)}) copy-start(bf16[3,3,3,128,128]{4,3,2,1,0:T(8,128)(2,1)} %param.10) | copy-start | bytes 2654212
  34.9 53.8 %collective-permute-start.6 = (bf16[3,7,128,128]{3,2,1,0:T(8,128)(2,1)S(1)}, bf16[3,7,128,128]{3,2,1,0:T(8,128)(2,1)S(1)}, u32[]{:S(2)}, u32[]{:S(2)}) collective-permute-start(bf16[3,7,128,128]{3,2,1,0:T(8,128)(2,1)S(1)} %get-tuple-element.55), channel_id=1, source_target_pairs={{0,1},{1,2},{2,3},{3,4},{4,5},{5,6},{6,7},{7,8},{8,9},{9,10},{10,1... | collective-permute-start | bytes 2064392 | tf_op jit(solution)/shard_map/ppermute | solution.py:294
  37.8 50.9 %collective-permute-start.7 = (bf16[3,7,128,128]{3,2,1,0:T(8,128)(2,1)S(1)}, bf16[3,7,128,128]{3,2,1,0:T(8,128)(2,1)S(1)}, u32[]{:S(2)}, u32[]{:S(2)}) collective-permute-start(bf16[3,7,128,128]{3,2,1,0:T(8,128)(2,1)S(1)} %get-tuple-element.56), channel_id=1, source_target_pairs={{1,64},{2,65},{3,66},{4,67},{5,68},{6,69},{7,70},{8,71},{9,72},{10... | collective-permute-start | bytes 2064392 | tf_op jit(solution)/shard_map/ppermute | solution.py:294
  45.8 42.9 %collective-permute-start.2 = (bf16[2,3,4,128,128]{4,3,2,1,0:T(8,128)(2,1)S(1)}, bf16[2,3,4,128,128]{4,3,2,1,0:T(8,128)(2,1)S(1)}, u32[]{:S(2)}, u32[]{:S(2)}) collective-permute-start(bf16[2,3,4,128,128]{4,3,2,1,0:T(8,128)(2,1)S(1)} %get-tuple-element.42), channel_id=1, source_target_pairs={{0,64},{1,65},{2,66},{3,67},{4,68},{5,69},{6,70},{7,71},{8,72},{9,... | collective-permute-start | bytes 2359304 | tf_op jit(solution)/shard_map/ppermute | solution.py:296
  73.3 3.7 %collective-permute-start.4 = (bf16[3,5,128,128]{3,2,1,0:T(8,128)(2,1)S(1)}, bf16[3,5,128,128]{3,2,1,0:T(8,128)(2,1)S(1)}, u32[]{:S(2)}, u32[]{:S(2)}) collective-permute-start(bf16[3,5,128,128]{3,2,1,0:T(8,128)(2,1)S(1)} %get-tuple-element.51), channel_id=1, source_target_pairs={{0,32},{32,0},{64,96},{96,64},{1,33},{33,1},{65,97},{97,65},{2,34}... | collective-permute-start | bytes 1474568 | tf_op jit(solution)/shard_map/ppermute | solution.py:309
  75.5 2.2 %collective-permute-start.5 = (bf16[3,5,128,128]{3,2,1,0:T(8,128)(2,1)S(1)}, bf16[3,5,128,128]{3,2,1,0:T(8,128)(2,1)S(1)}, u32[]{:S(2)}, u32[]{:S(2)}) collective-permute-start(bf16[3,5,128,128]{3,2,1,0:T(8,128)(2,1)S(1)} %get-tuple-element.52), channel_id=1, source_target_pairs={{0,32},{32,0},{64,96},{96,64},{1,33},{33,1},{65,97},{97,65},{2,34}... | collective-permute-start | bytes 1474568 | tf_op jit(solution)/shard_map/ppermute | solution.py:309
  75.7 2.0 %copy-start.3 = (f32[128]{0:T(128)S(1)}, f32[128]{0:T(128)}, u32[]{:S(2)}) copy-start(f32[128]{0:T(128)} %param.11) | copy-start | bytes 1540
  86.6 16.1 %collective-permute-start.10 = (bf16[2,3,3,128,128]{4,3,2,1,0:T(8,128)(2,1)S(1)}, bf16[2,3,3,128,128]{4,3,2,1,0:T(8,128)(2,1)S(1)}, u32[]{:S(2)}, u32[]{:S(2)}) collective-permute-start(bf16[2,3,3,128,128]{4,3,2,1,0:T(8,128)(2,1)S(1)} %get-tuple-element.61), channel_id=1, source_target_pairs={{0,64},{1,65},{2,66},{3,67},{4,68},{5,69},{6,70},{7,71},{8,72},{9,... | collective-permute-start | bytes 1769480 | tf_op jit(solution)/shard_map/ppermute | solution.py:316
  89.9 2.7 %collective-permute-start.8 = (bf16[3,4,128,128]{3,2,1,0:T(8,128)(2,1)S(1)}, bf16[3,4,128,128]{3,2,1,0:T(8,128)(2,1)S(1)}, u32[]{:S(2)}, u32[]{:S(2)}) collective-permute-start(bf16[3,4,128,128]{3,2,1,0:T(8,128)(2,1)S(1)} %get-tuple-element.58), channel_id=1, source_target_pairs={{0,32},{32,0},{64,96},{96,64},{1,33},{33,1},{65,97},{97,65},{2,34}... | collective-permute-start | bytes 1179656 | tf_op jit(solution)/shard_map/ppermute | solution.py:309
  91.3 1.9 %collective-permute-start.9 = (bf16[3,4,128,128]{3,2,1,0:T(8,128)(2,1)S(1)}, bf16[3,4,128,128]{3,2,1,0:T(8,128)(2,1)S(1)}, u32[]{:S(2)}, u32[]{:S(2)}) collective-permute-start(bf16[3,4,128,128]{3,2,1,0:T(8,128)(2,1)S(1)} %get-tuple-element.59), channel_id=1, source_target_pairs={{0,32},{32,0},{64,96},{96,64},{1,33},{33,1},{65,97},{97,65},{2,34}... | collective-permute-start | bytes 1179656 | tf_op jit(solution)/shard_map/ppermute | solution.py:309
  103.7 2.9 %collective-permute-start.11 = (bf16[2,3,3,128,128]{4,3,2,1,0:T(8,128)(2,1)S(1)}, bf16[2,3,3,128,128]{4,3,2,1,0:T(8,128)(2,1)S(1)}, u32[]{:S(2)}, u32[]{:S(2)}) collective-permute-start(bf16[2,3,3,128,128]{4,3,2,1,0:T(8,128)(2,1)S(1)} %get-tuple-element.65), channel_id=1, source_target_pairs={{0,32},{32,0},{64,96},{96,64},{1,33},{33,1},{65,97},{97,65},{2,34}... | collective-permute-start | bytes 1769480 | tf_op jit(solution)/shard_map/ppermute | solution.py:309

commit v8 on v5

--- a/solution.py
+++ b/solution.py
@@ -17,11 +17,11 @@
     up = jnp.where(place == cols - 1, 0.0, pltpu.roll(after, rows - 1, 0))
     return down + here + up
 
-def split_columns(x_ref, v, i, wide, ev, od, at):
-    n = wide.shape[1] // 2
-    wide[at] = x_ref[v, i].astype(f32)
-    ev[v, at] = wide[at, pl.ds(0, n, 2), :].astype(bf16)
-    od[v, at] = wide[at, pl.ds(1, n, 2), :].astype(bf16)
+def split_columns(x_ref, v, i, wide, ev, od, at, to):
+    n = wide.shape[2] // 2
+    wide[to, at] = x_ref[v, i].astype(f32)
+    ev[to, at] = wide[to, at, pl.ds(0, n, 2), :].astype(bf16)
+    od[to, at] = wide[to, at, pl.ds(1, n, 2), :].astype(bf16)
 
 
 def main_weights(k_ref, wm_ref):
@@ -62,24 +62,30 @@
     first = lax.axis_index("view") < 2
     refs = (ev, od)
 
-    def step(b, carry):
-        for piece in pieces(b):
-            piece.wait()
-        for v in range(g):
-            split_columns(top.at[:, b], v, 0, wide, ev, od, 0)
-            split_columns(bottom.at[:, b], v, 0, wide, ev, od, 1)
-            split_columns(bottom.at[:, b], v, 1, wide, ev, od, 2)
+    m = HALO_STEP * m
+
+    def step(t, carry):
+        for q in range(HALO_STEP):
+            b = t * HALO_STEP + q
+            for piece in pieces(b):
+                piece.wait()
+            for v in range(g):
+                split_columns(top.at[:, b], v, 0, wide, ev, od, 0, q * g + v)
+                split_columns(bottom.at[:, b], v, 0, wide, ev, od, 1, q * g + v)
+                split_columns(bottom.at[:, b], v, 1, wide, ev, od, 2, q * g + v)
         up = jnp.dot(side_blocks(refs, [(0, 0), (1, 0)], m), wm_ref[8 * c:, :], preferred_element_type=f32)
         side = jnp.dot(side_blocks(refs, [(0, 0)], m), we_ref[4 * c:5 * c, :c], preferred_element_type=f32)
-        up = shifted_sum(up[:, :c], up[:, c:], side, n).astype(bf16).reshape(g, n, c)
+        up = shifted_sum(up[:, :c], up[:, c:], side, n).astype(bf16).reshape(HALO_STEP, g, n, c)
         dn = jnp.dot(side_blocks(refs, [(0, 1), (1, 1), (0, 2), (1, 2)], m), wm_ref[:4 * c, :], preferred_element_type=f32)
         side = jnp.dot(side_blocks(refs, [(0, 1), (0, 2)], m), we_ref[:2 * c, :c], preferred_element_type=f32)
-        dn = shifted_sum(dn[:, :c], dn[:, c:], side, n).astype(bf16).reshape(g, n, c)
-        h1_ref[:, b] = jnp.where(first, dn, up)
-        h2_ref[:, b] = jnp.where(first, up, dn)
+        dn = shifted_sum(dn[:, :c], dn[:, c:], side, n).astype(bf16).reshape(HALO_STEP, g, n, c)
+        for q in range(HALO_STEP):
+            b = t * HALO_STEP + q
+            h1_ref[:, b] = jnp.where(first, dn[q], up[q])
+            h2_ref[:, b] = jnp.where(first, up[q], dn[q])
         return carry
 
-    lax.fori_loop(0, views, step, 0)
+    lax.fori_loop(0, views // HALO_STEP, step, 0)
 
 
 def halo_sums(features, kernel):
@@ -92,7 +98,8 @@
         out_specs=[whole] * 4,
         scratch_shapes=[
             pltpu.VMEM((U, V, 1, W, C), bf16), pltpu.VMEM((U, V, 2, W, C), bf16), pltpu.VMEM(kernel.shape, bf16),
-            pltpu.VMEM((3, W, C), f32), pltpu.VMEM((U, 3, n, C), bf16), pltpu.VMEM((U, 3, n, C), bf16),
+            pltpu.VMEM((HALO_STEP * U, 3, W, C), f32),
+            pltpu.VMEM((HALO_STEP * U, 3, n, C), bf16), pltpu.VMEM((HALO_STEP * U, 3, n, C), bf16),
             pltpu.SemaphoreType.DMA((2 * V + 1,)),
         ],
         out_shape=[jax.ShapeDtypeStruct((U, V, n, C), bf16)] * 2
@@ -132,7 +139,7 @@
         fetch(b).wait()
         for v in range(g):
             for i in range(rows):
-                split_columns(xs.at[b], v, i, wide, ev, od, i)
+                split_columns(xs.at[b], v, i, wide, ev, od, i, v)
         at = b - start
         pair = side(0, 5, 2)
         r0 = row(main(0, 3, 2), pair[:, :c])
@@ -165,7 +172,7 @@
         out_specs=[whole] * (2 * len(spans)),
         scratch_shapes=[
             pltpu.VMEM((count, U, H, W, C), bf16),
-            pltpu.VMEM((H, W, C), f32), pltpu.VMEM((U, H, n, C), bf16), pltpu.VMEM((U, H, n, C), bf16),
+            pltpu.VMEM((U, H, W, C), f32), pltpu.VMEM((U, H, n, C), bf16), pltpu.VMEM((U, H, n, C), bf16),
             pltpu.SemaphoreType.DMA((count,)),
         ],
         out_shape=[jax.ShapeDtypeStruct((2, U, hi - lo, n, C), bf16) for lo, hi in spans for _ in range(2)],
@@ -308,8 +315,9 @@
     )(*args)
 
 
-CHUNKS = ((0, 4), (4, 9), (9, 12))
-PARTS = (1, 2, 1)
+CHUNKS = ((0, 5), (5, 9), (9, 12))
+PARTS = (2, 2, 1)
+HALO_STEP = 4
 
 
 def shards(features, analysis_kernel, norm_floor, norm_mixing, epipolar_kernel, epipolar_bias):
@@ -337,9 +345,7 @@
         rows += done[::2]
         sent += done[1::2]
         features, last = lax.optimization_barrier((features, done[0]))
-    sent[0] = lax.ppermute(sent[0], both, swap)
-    sent[1], h1, h2 = lax.optimization_barrier((sent[1], h1, h2))
-    sent[1] = lax.ppermute(sent[1], both, swap)
+    sent = [lax.ppermute(oth, both, swap) for oth in sent]
     sources = []
     out = None
     done = 0
@@ -355,9 +361,6 @@
         upto = V if hi == V else hi - 1
         out = epi_chunk(sources, CHUNKS[:i + 1], done, upto, out, em, ee, bias, total, V)
         done = upto
-        if i + 2 < len(CHUNKS):
-            sent[i + 2], out = lax.optimization_barrier((sent[i + 2], out))
-            sent[i + 2] = lax.ppermute(sent[i + 2], both, swap)
     return out
 
 

time: 114 us -> 111 us (0.974)
  waiting for transfers between devices: 36.4 us -> 34.7 us
    ppermute x3, waiting for transfers between devices: 31 us -> 29.4 us  [shards(): sent = [lax.ppermute(oth, both, swap) for oth in sent]]
    ppermute x4 -> x5, waiting for transfers between devices: 5.39 us -> 5.29 us  [shards(): flipped = [lax.ppermute(g, 'view', core) for g in give]]
  transfers between devices with their start and end apart: 9 -> 10, of which waited for: 6 -> 7; matrix products, arithmetic and copies ran while one was open for 0% -> 0% of each run, Pallas kernels for 37% -> 38%
where the time goes in v8:
time: 111 us
  Pallas kernels  59.7 us (54%)
  waiting for transfers between devices  34.7 us (31%)
  starting transfers between devices  13.7 us (12%)
  local copies, waits for them, and re-layouts  2.2 us (2%)
    ppermute x3, waiting for transfers between devices, shards(): sent = [lax.ppermute(oth, both, swap) for oth in sent]  29.4 us
    pallas_call x3, Pallas kernels, epi_chunk(): pl.pallas_call(functools.partial(epi_kernel, tuple(pieces), v0, v1, int(p...  27 us
    pallas_call x2, Pallas kernels, conv_chunks(): pl.pallas_call(functools.partial(conv_kernel, base, starts), in_specs=[pl...  21 us
    pallas_call x1, Pallas kernels, halo_sums(): pl.pallas_call(halo_kernel, in_specs=[pl.BlockSpec(memory_space=pl.ANY)]...  8.17 us
    ppermute x3, starting transfers between devices, shards(): sent = [lax.ppermute(oth, both, swap) for oth in sent]  7.75 us
    ppermute x5, waiting for transfers between devices, shards(): flipped = [lax.ppermute(g, 'view', core) for g in give]  5.29 us
    pallas_call x3, Pallas kernels, norm_chunk(): pl.pallas_call(functools.partial(norm_kernel, lo), in_specs=[whole] * 6,...  3.52 us
  transfers between devices with their start and end apart: 10, of which 7 were waited for; matrix products, arithmetic and copies ran while one was open for 0% of the time, Pallas kernels for 38%

profile of v8, /device:TPU:121, one launch (start us, length us, event | category | flops | bytes accessed | tf_op | source)
XLA Modules:
  0.0 110.6 jit_solution(10616014167627581999)
XLA Ops:
  0.0 8.2 %halo.1 = (bf16[3,12,128,128]{3,2,1,0:T(8,128)(2,1)}, bf16[3,12,128,128]{3,2,1,0:T(8,128)(2,1)}, bf16[1280,256]{1,0:T(8,128)(2,1)}, bf16[896,256]{1,0:T(8,128)(2,1)}) custom-call(bf16[3,12,8,256,128]{4,3,2,1,0:T(8,128)(2,1)} %x_ref.3, bf16[5,5,128,128]{3,2,1,0:T(8,128)(2,1)} %k_ref.1), custom_call_target="tpu_custom_call" | custom-call | flops 1000 | bytes 1000 | tf_op jit(solution)/shard_map/halo/pallas_call | solution.py:95
  8.2 1.9 %collective-permute-start.3 = (bf16[3,12,128,128]{3,2,1,0:T(8,128)(2,1)}, bf16[3,12,128,128]{3,2,1,0:T(8,128)(2,1)S(1)}, u32[]{:S(2)}, u32[]{:S(2)}) collective-permute-start(bf16[3,12,128,128]{3,2,1,0:T(8,128)(2,1)} %get-tuple-element.42), channel_id=1, source_target_pairs={{1,64},{2,65},{3,66},{4,67},{5,68},{6,69},{7,70},{8,71},{9,72},{10... | collective-permute-start | bytes 3538952 | tf_op jit(solution)/shard_map/ppermute | solution.py:340
  10.1 2.0 %collective-permute-start.2 = (bf16[3,12,128,128]{3,2,1,0:T(8,128)(2,1)}, bf16[3,12,128,128]{3,2,1,0:T(8,128)(2,1)S(1)}, u32[]{:S(2)}, u32[]{:S(2)}) collective-permute-start(bf16[3,12,128,128]{3,2,1,0:T(8,128)(2,1)} %get-tuple-element.31), channel_id=1, source_target_pairs={{0,1},{1,2},{2,3},{3,4},{4,5},{5,6},{6,7},{7,8},{8,9},{9,10},{10,1... | collective-permute-start | bytes 3538952 | tf_op jit(solution)/shard_map/ppermute | solution.py:339
  12.1 0.0 copy-start
  12.2 1.1 copy-done
  13.2 0.0 copy-start.1
  13.2 1.0 copy-done.1
  14.3 9.0 %conv.2 = (bf16[2,3,5,128,128]{4,3,2,1,0:T(8,128)(2,1)S(1)}, bf16[2,3,5,128,128]{4,3,2,1,0:T(8,128)(2,1)S(1)}) custom-call(bf16[3,12,8,256,128]{4,3,2,1,0:T(8,128)(2,1)} %x_ref.3, bf16[1280,256]{1,0:T(8,128)(2,1)S(1)} %copy-done, bf16[896,256]{1,0:T(8,128)(2,1)S(1)} %copy-done.1), custom_call_target="tpu_custom_call" | custom-call | flops 1000 | bytes 1000 | tf_op jit(solution)/shard_map/conv/pallas_call | solution.py:169
  23.2 4.7 %collective-permute-start.1 = (bf16[2,3,5,128,128]{4,3,2,1,0:T(8,128)(2,1)S(1)}, bf16[2,3,5,128,128]{4,3,2,1,0:T(8,128)(2,1)S(1)}, u32[]{:S(2)}, u32[]{:S(2)}) collective-permute-start(bf16[2,3,5,128,128]{4,3,2,1,0:T(8,128)(2,1)S(1)} %get-tuple-element.39), channel_id=1, source_target_pairs={{0,64},{1,65},{2,66},{3,67},{4,68},{5,69},{6,70},{7,71},{8,72},{9,... | collective-permute-start | bytes 2949128 | tf_op jit(solution)/shard_map/ppermute | solution.py:348
  27.9 0.0 copy-start.2
  27.9 0.0 copy-start.3
  28.0 12.0 %conv.3 = (bf16[2,3,4,128,128]{4,3,2,1,0:T(8,128)(2,1)S(1)}, bf16[2,3,4,128,128]{4,3,2,1,0:T(8,128)(2,1)S(1)}, bf16[2,3,3,128,128]{4,3,2,1,0:T(8,128)(2,1)S(1)}, bf16[2,3,3,128,128]{4,3,2,1,0:T(8,128)(2,1)S(1)}) custom-call(bf16[3,12,8,256,128]{4,3,2,1,0:T(8,128)(2,1)} %x_ref.3, bf16[1280,256]{1,0:T(8,128)(2,1)S(1)} %copy-done, bf16[896,256]{1,0:T(8,128)(2,1)S(1)} %copy-done.1), custom_call_target="tpu_custom_call" | custom-call | flops 1000 | bytes 1000 | tf_op jit(solution)/shard_map/conv/pallas_call | solution.py:169
  40.0 0.1 collective-permute-start
  40.1 2.9 %collective-permute-start.8 = (bf16[2,3,3,128,128]{4,3,2,1,0:T(8,128)(2,1)S(1)}, bf16[2,3,3,128,128]{4,3,2,1,0:T(8,128)(2,1)S(1)}, u32[]{:S(2)}, u32[]{:S(2)}) collective-permute-start(bf16[2,3,3,128,128]{4,3,2,1,0:T(8,128)(2,1)S(1)} %get-tuple-element.51), channel_id=1, source_target_pairs={{0,64},{1,65},{2,66},{3,67},{4,68},{5,69},{6,70},{7,71},{8,72},{9,... | collective-permute-start | bytes 1769480 | tf_op jit(solution)/shard_map/ppermute | solution.py:348
  43.1 25.9 %collective-permute-done.1.oth_ref = bf16[2,3,5,128,128]{4,3,2,1,0:T(8,128)(2,1)S(1)} collective-permute-done((bf16[2,3,5,128,128]{4,3,2,1,0:T(8,128)(2,1)S(1)}, bf16[2,3,5,128,128]{4,3,2,1,0:T(8,128)(2,1)S(1)}, u32[]{:S(2)}, u32[]{:S(2)}) %collective-permute-start.1) | collective-permute-done | bytes 983072 | tf_op jit(solution)/shard_map/ppermute | solution.py:348
  68.9 0.0 collective-permute-done.3.h2_ref
  68.9 0.0 collective-permute-done.2.h1_ref
  68.9 0.0 copy-done.2
  68.9 0.0 copy-done.3
  68.9 0.0 copy-start.5
  69.0 1.5 %norm.3 = (bf16[2,3,5,128,128]{4,3,2,1,0:T(8,128)(2,1)S(1)}, bf16[3,5,128,128]{3,2,1,0:T(8,128)(2,1)S(1)}, bf16[3,5,128,128]{3,2,1,0:T(8,128)(2,1)S(1)}) custom-call(bf16[2,3,5,128,128]{4,3,2,1,0:T(8,128)(2,1)S(1)} %get-tuple-element.35.own_ref, bf16[2,3,5,128,128]{4,3,2,1,0:T(8,128)(2,1)S(1)} %collective-permute-done.1.oth_ref, ...), custom_call_target="tpu_custom_call" | custom-call | flops 1000 | bytes 1000 | tf_op jit(solution)/shard_map/norm/pallas_call | solution.py:212
  70.4 0.7 collective-permute-start.4
  71.1 0.1 collective-permute-start.5
  71.2 0.0 copy-done.5
  71.2 0.1 slice_bitcast_fusion
  71.3 0.0 copy-start.4
  71.3 0.1 fusion.2
  71.4 0.1 pad_maximum_fusion.refs_3_.refs_6_.refs_5_
  71.4 1.1 %collective-permute-done.4.refs_1_ = bf16[3,5,128,128]{3,2,1,0:T(8,128)(2,1)S(1)} collective-permute-done((bf16[3,5,128,128]{3,2,1,0:T(8,128)(2,1)S(1)}, bf16[3,5,128,128]{3,2,1,0:T(8,128)(2,1)S(1)}, u32[]{:S(2)}, u32[]{:S(2)}) %collective-permute-start.4) | collective-permute-done | bytes 491552 | tf_op jit(solution)/shard_map/ppermute | solution.py:359
  72.6 0.7 collective-permute-done.5.refs_2_
  73.3 0.0 copy-done.4
  73.3 8.9 %epi.3.refs_9_ = bf16[12,12,1,128,128]{4,3,2,1,0:T(8,128)(2,1)} custom-call(bf16[2,3,5,128,128]{4,3,2,1,0:T(8,128)(2,1)S(1)} %get-tuple-element.43.refs_0_, bf16[3,5,128,128]{3,2,1,0:T(8,128)(2,1)S(1)} %collective-permute-done.4.refs_1_, bf16[3,5,128,128]{3,2,1,0:T(8,128)(2,1)S(1)} %collective-permute-done.5.refs_2_, ...), custom_call_target="tpu_custom_call" | custom-call | flops 1000 | bytes 1000 | tf_op jit(solution)/shard_map/epi/pallas_call | solution.py:299
  82.2 3.6 %collective-permute-done.oth_ref = bf16[2,3,4,128,128]{4,3,2,1,0:T(8,128)(2,1)S(1)} collective-permute-done((bf16[2,3,4,128,128]{4,3,2,1,0:T(8,128)(2,1)S(1)}, bf16[2,3,4,128,128]{4,3,2,1,0:T(8,128)(2,1)S(1)}, u32[]{:S(2)}, u32[]{:S(2)}) %collective-permute-start) | collective-permute-done | bytes 786464 | tf_op jit(solution)/shard_map/ppermute | solution.py:348
  85.8 1.2 %norm.4 = (bf16[2,3,4,128,128]{4,3,2,1,0:T(8,128)(2,1)S(1)}, bf16[3,4,128,128]{3,2,1,0:T(8,128)(2,1)S(1)}, bf16[3,4,128,128]{3,2,1,0:T(8,128)(2,1)S(1)}) custom-call(bf16[2,3,4,128,128]{4,3,2,1,0:T(8,128)(2,1)S(1)} %get-tuple-element.37.own_ref, bf16[2,3,4,128,128]{4,3,2,1,0:T(8,128)(2,1)S(1)} %collective-permute-done.oth_ref, ...), custom_call_target="tpu_custom_call" | custom-call | flops 1000 | bytes 1000 | tf_op jit(solution)/shard_map/norm/pallas_call | solution.py:212
  87.0 0.7 collective-permute-start.6
  87.6 0.1 collective-permute-start.7
  87.7 1.3 %collective-permute-done.6.refs_4_.refs_1_ = bf16[3,4,128,128]{3,2,1,0:T(8,128)(2,1)S(1)} collective-permute-done((bf16[3,4,128,128]{3,2,1,0:T(8,128)(2,1)S(1)}, bf16[3,4,128,128]{3,2,1,0:T(8,128)(2,1)S(1)}, u32[]{:S(2)}, u32[]{:S(2)}) %collective-permute-start.6) | collective-permute-done | bytes 393248 | tf_op jit(solution)/shard_map/ppermute | solution.py:359
  89.0 0.6 collective-permute-done.7.refs_5_.refs_2_
  89.5 9.1 %epi.4.refs_8_ = bf16[12,12,1,128,128]{4,3,2,1,0:T(8,128)(2,1)} custom-call(bf16[2,3,5,128,128]{4,3,2,1,0:T(8,128)(2,1)S(1)} %get-tuple-element.43.refs_0_, bf16[3,5,128,128]{3,2,1,0:T(8,128)(2,1)S(1)} %collective-permute-done.4.refs_1_, bf16[3,5,128,128]{3,2,1,0:T(8,128)(2,1)S(1)} %collective-permute-done.5.refs_2_, ...), custom_call_target="tpu_custom_call", output_to_operand_aliasing={{}: (9, {})} | custom-call | flops 1000 | bytes 1000 | tf_op jit(solution)/shard_map/epi/pallas_call | solution.py:299
  98.6 0.0 collective-permute-done.8.oth_ref
  98.6 0.9 norm.5
  99.5 0.5 collective-permute-start.9
  100.0 1.6 %collective-permute-done.9.refs_4_ = bf16[2,3,3,128,128]{4,3,2,1,0:T(8,128)(2,1)S(1)} collective-permute-done((bf16[2,3,3,128,128]{4,3,2,1,0:T(8,128)(2,1)S(1)}, bf16[2,3,3,128,128]{4,3,2,1,0:T(8,128)(2,1)S(1)}, u32[]{:S(2)}, u32[]{:S(2)}) %collective-permute-start.9) | collective-permute-done | bytes 589856 | tf_op jit(solution)/shard_map/ppermute | solution.py:359
  101.6 9.0 %epi.5 = bf16[12,12,1,128,128]{4,3,2,1,0:T(8,128)(2,1)} custom-call(bf16[2,3,4,128,128]{4,3,2,1,0:T(8,128)(2,1)S(1)} %get-tuple-element.47.refs_3_.refs_0_, bf16[3,4,128,128]{3,2,1,0:T(8,128)(2,1)S(1)} %collective-permute-done.6.refs_4_.refs_1_, bf16[3,4,128,128]{3,2,1,0:T(8,128)(2,1)S(1)} %collective-permute-done.7.refs_5_.refs_2_, ...), custom_call_target="tpu_custom_call", output_to_operand_aliasing={{}: (8, {})} | custom-call | flops 1000 | bytes 1000 | tf_op jit(solution)/shard_map/epi/pallas_call | solution.py:299
Async XLA Ops:
  8.2 60.8 %collective-permute-start.3 = (bf16[3,12,128,128]{3,2,1,0:T(8,128)(2,1)}, bf16[3,12,128,128]{3,2,1,0:T(8,128)(2,1)S(1)}, u32[]{:S(2)}, u32[]{:S(2)}) collective-permute-start(bf16[3,12,128,128]{3,2,1,0:T(8,128)(2,1)} %get-tuple-element.42), channel_id=1, source_target_pairs={{1,64},{2,65},{3,66},{4,67},{5,68},{6,69},{7,70},{8,71},{9,72},{10... | collective-permute-start | bytes 3538952 | tf_op jit(solution)/shard_map/ppermute | solution.py:340
  10.1 58.8 %collective-permute-start.2 = (bf16[3,12,128,128]{3,2,1,0:T(8,128)(2,1)}, bf16[3,12,128,128]{3,2,1,0:T(8,128)(2,1)S(1)}, u32[]{:S(2)}, u32[]{:S(2)}) collective-permute-start(bf16[3,12,128,128]{3,2,1,0:T(8,128)(2,1)} %get-tuple-element.31), channel_id=1, source_target_pairs={{0,1},{1,2},{2,3},{3,4},{4,5},{5,6},{6,7},{7,8},{8,9},{9,10},{10,1... | collective-permute-start | bytes 3538952 | tf_op jit(solution)/shard_map/ppermute | solution.py:339
  12.1 1.1 copy-start
  13.2 1.0 copy-start.1
  23.2 45.7 %collective-permute-start.1 = (bf16[2,3,5,128,128]{4,3,2,1,0:T(8,128)(2,1)S(1)}, bf16[2,3,5,128,128]{4,3,2,1,0:T(8,128)(2,1)S(1)}, u32[]{:S(2)}, u32[]{:S(2)}) collective-permute-start(bf16[2,3,5,128,128]{4,3,2,1,0:T(8,128)(2,1)S(1)} %get-tuple-element.39), channel_id=1, source_target_pairs={{0,64},{1,65},{2,66},{3,67},{4,68},{5,69},{6,70},{7,71},{8,72},{9,... | collective-permute-start | bytes 2949128 | tf_op jit(solution)/shard_map/ppermute | solution.py:348
  27.9 41.0 %copy-start.2 = (f32[128,128]{1,0:T(8,128)S(1)}, f32[128,128]{1,0:T(8,128)}, u32[]{:S(2)}) copy-start(f32[128,128]{1,0:T(8,128)} %mix_ref.5) | copy-start | bytes 196612
  27.9 41.0 %copy-start.3 = (f32[128]{0:T(128)S(1)}, f32[128]{0:T(128)}, u32[]{:S(2)}) copy-start(f32[128]{0:T(128)} %param.8) | copy-start | bytes 1540
  40.0 45.8 %collective-permute-start = (bf16[2,3,4,128,128]{4,3,2,1,0:T(8,128)(2,1)S(1)}, bf16[2,3,4,128,128]{4,3,2,1,0:T(8,128)(2,1)S(1)}, u32[]{:S(2)}, u32[]{:S(2)}) collective-permute-start(bf16[2,3,4,128,128]{4,3,2,1,0:T(8,128)(2,1)S(1)} %get-tuple-element.38), channel_id=1, source_target_pairs={{0,64},{1,65},{2,66},{3,67},{4,68},{5,69},{6,70},{7,71},{8,72},{9,... | collective-permute-start | bytes 2359304 | tf_op jit(solution)/shard_map/ppermute | solution.py:348
  40.1 58.5 %collective-permute-start.8 = (bf16[2,3,3,128,128]{4,3,2,1,0:T(8,128)(2,1)S(1)}, bf16[2,3,3,128,128]{4,3,2,1,0:T(8,128)(2,1)S(1)}, u32[]{:S(2)}, u32[]{:S(2)}) collective-permute-start(bf16[2,3,3,128,128]{4,3,2,1,0:T(8,128)(2,1)S(1)} %get-tuple-element.51), channel_id=1, source_target_pairs={{0,64},{1,65},{2,66},{3,67},{4,68},{5,69},{6,70},{7,71},{8,72},{9,... | collective-permute-start | bytes 1769480 | tf_op jit(solution)/shard_map/ppermute | solution.py:348
  68.9 2.2 %copy-start.5 = (bf16[3,3,3,128,128]{4,3,2,1,0:T(8,128)(2,1)S(1)}, bf16[3,3,3,128,128]{4,3,2,1,0:T(8,128)(2,1)}, u32[]{:S(2)}) copy-start(bf16[3,3,3,128,128]{4,3,2,1,0:T(8,128)(2,1)} %param.10) | copy-start | bytes 2654212
  70.4 2.2 %collective-permute-start.4 = (bf16[3,5,128,128]{3,2,1,0:T(8,128)(2,1)S(1)}, bf16[3,5,128,128]{3,2,1,0:T(8,128)(2,1)S(1)}, u32[]{:S(2)}, u32[]{:S(2)}) collective-permute-start(bf16[3,5,128,128]{3,2,1,0:T(8,128)(2,1)S(1)} %get-tuple-element.44), channel_id=1, source_target_pairs={{0,32},{32,0},{64,96},{96,64},{1,33},{33,1},{65,97},{97,65},{2,34}... | collective-permute-start | bytes 1474568 | tf_op jit(solution)/shard_map/ppermute | solution.py:359
  71.1 2.2 %collective-permute-start.5 = (bf16[3,5,128,128]{3,2,1,0:T(8,128)(2,1)S(1)}, bf16[3,5,128,128]{3,2,1,0:T(8,128)(2,1)S(1)}, u32[]{:S(2)}, u32[]{:S(2)}) collective-permute-start(bf16[3,5,128,128]{3,2,1,0:T(8,128)(2,1)S(1)} %get-tuple-element.45), channel_id=1, source_target_pairs={{0,32},{32,0},{64,96},{96,64},{1,33},{33,1},{65,97},{97,65},{2,34}... | collective-permute-start | bytes 1474568 | tf_op jit(solution)/shard_map/ppermute | solution.py:359
  71.3 2.0 %copy-start.4 = (f32[128]{0:T(128)S(1)}, f32[128]{0:T(128)}, u32[]{:S(2)}) copy-start(f32[128]{0:T(128)} %param.11) | copy-start | bytes 1540
  87.0 2.0 %collective-permute-start.6 = (bf16[3,4,128,128]{3,2,1,0:T(8,128)(2,1)S(1)}, bf16[3,4,128,128]{3,2,1,0:T(8,128)(2,1)S(1)}, u32[]{:S(2)}, u32[]{:S(2)}) collective-permute-start(bf16[3,4,128,128]{3,2,1,0:T(8,128)(2,1)S(1)} %get-tuple-element.48), channel_id=1, source_target_pairs={{0,32},{32,0},{64,96},{96,64},{1,33},{33,1},{65,97},{97,65},{2,34}... | collective-permute-start | bytes 1179656 | tf_op jit(solution)/shard_map/ppermute | solution.py:359
  87.6 1.9 %collective-permute-start.7 = (bf16[3,4,128,128]{3,2,1,0:T(8,128)(2,1)S(1)}, bf16[3,4,128,128]{3,2,1,0:T(8,128)(2,1)S(1)}, u32[]{:S(2)}, u32[]{:S(2)}) collective-permute-start(bf16[3,4,128,128]{3,2,1,0:T(8,128)(2,1)S(1)} %get-tuple-element.49), channel_id=1, source_target_pairs={{0,32},{32,0},{64,96},{96,64},{1,33},{33,1},{65,97},{97,65},{2,34}... | collective-permute-start | bytes 1179656 | tf_op jit(solution)/shard_map/ppermute | solution.py:359
  99.5 2.1 %collective-permute-start.9 = (bf16[2,3,3,128,128]{4,3,2,1,0:T(8,128)(2,1)S(1)}, bf16[2,3,3,128,128]{4,3,2,1,0:T(8,128)(2,1)S(1)}, u32[]{:S(2)}, u32[]{:S(2)}) collective-permute-start(bf16[2,3,3,128,128]{4,3,2,1,0:T(8,128)(2,1)S(1)} %get-tuple-element.55), channel_id=1, source_target_pairs={{0,32},{32,0},{64,96},{96,64},{1,33},{33,1},{65,97},{97,65},{2,34}... | collective-permute-start | bytes 1769480 | tf_op jit(solution)/shard_map/ppermute | solution.py:359

commit v9 on v8

--- a/solution.py
+++ b/solution.py
@@ -253,8 +253,8 @@
             ).wait()
     m = nv * n
     steps = total // 2
-    def out_copy(t, slot):
-        return pltpu.make_async_copy(obuf.at[slot], out_ref.at[pl.ds(2 * t, 2), v0:v1, 0], sem_out.at[slot])
+    def out_copy(t, slot, h):
+        return pltpu.make_async_copy(obuf.at[slot, h], out_ref.at[2 * t + h, v0:v1, 0], sem_out.at[slot, h])
     def step(t, carry):
         slot = lax.rem(t, 2)
         for b in range(total // U):
@@ -262,7 +262,8 @@
 
         @pl.when(t >= 2)
         def _():
-            out_copy(t - 2, slot).wait()
+            for h in range(2):
+                out_copy(t - 2, slot, h).wait()
         def block(i, j):
             return cod[2 * t + i, j:j + nv].reshape(m, c)
         blocks = [[block(i, j) for j in range(3)] for i in range(4)]
@@ -271,11 +272,12 @@
             mn = jnp.dot(jnp.concatenate(sum(blocks[h:h + 3], []), axis=1), wm_ref[...], preferred_element_type=f32)
             res = shifted_sum(mn[:, :c], mn[:, c:], ex[:, h * c:(h + 1) * c], n) + bias_ref[...]
             obuf[slot, h] = res.astype(bf16).reshape(nv, n, c)
-        out_copy(t, slot).start()
+            out_copy(t, slot, h).start()
         return carry
     lax.fori_loop(0, steps, step, 0)
     for t in (steps - 2, steps - 1):
-        out_copy(t, t % 2).wait()
+        for h in range(2):
+            out_copy(t, t % 2, h).wait()
 
 def epi_weights(k):
     c = k.shape[3]
@@ -305,7 +307,7 @@
             pltpu.VMEM((total + 2, nv + 2, n, C), bf16),
             pltpu.VMEM((2, 2, nv, n, C), bf16),
             pltpu.SemaphoreType.DMA((4 * len(pieces),)),
-            pltpu.SemaphoreType.DMA((2,)),
+            pltpu.SemaphoreType.DMA((2, 2)),
         ],
         out_shape=jax.ShapeDtypeStruct((total, V, 1, n, C), bf16),
         input_output_aliases={len(args) - 1: 0} if prev is not None else {},

time: 111 us -> 111 us (level)
  no operation moved by 1% of the time
where the time goes in v9:
time: 111 us
  Pallas kernels  59.9 us (54%)
  waiting for transfers between devices  34.7 us (31%)
  starting transfers between devices  13.7 us (12%)
  local copies, waits for them, and re-layouts  2.2 us (2%)
    ppermute x3, waiting for transfers between devices, shards(): sent = [lax.ppermute(oth, both, swap) for oth in sent]  29.4 us
    pallas_call x3, Pallas kernels, epi_chunk(): pl.pallas_call(functools.partial(epi_kernel, tuple(pieces), v0, v1, int(p...  27.2 us
    pallas_call x2, Pallas kernels, conv_chunks(): pl.pallas_call(functools.partial(conv_kernel, base, starts), in_specs=[pl...  21 us
    pallas_call x1, Pallas kernels, halo_sums(): pl.pallas_call(halo_kernel, in_specs=[pl.BlockSpec(memory_space=pl.ANY)]...  8.17 us
    ppermute x3, starting transfers between devices, shards(): sent = [lax.ppermute(oth, both, swap) for oth in sent]  7.75 us
    ppermute x5, waiting for transfers between devices, shards(): flipped = [lax.ppermute(g, 'view', core) for g in give]  5.29 us
    pallas_call x3, Pallas kernels, norm_chunk(): pl.pallas_call(functools.partial(norm_kernel, lo), in_specs=[whole] * 6,...  3.52 us
  transfers between devices with their start and end apart: 10, of which 7 were waited for; matrix products, arithmetic and copies ran while one was open for 0% of the time, Pallas kernels for 38%

profile of v9, /device:TPU:121, one launch (start us, length us, event | category | flops | bytes accessed | tf_op | source)
XLA Modules:
  0.0 110.8 jit_solution(5742820896890057424)
XLA Ops:
  0.0 8.2 %halo.1 = (bf16[3,12,128,128]{3,2,1,0:T(8,128)(2,1)}, bf16[3,12,128,128]{3,2,1,0:T(8,128)(2,1)}, bf16[1280,256]{1,0:T(8,128)(2,1)}, bf16[896,256]{1,0:T(8,128)(2,1)}) custom-call(bf16[3,12,8,256,128]{4,3,2,1,0:T(8,128)(2,1)} %x_ref.3, bf16[5,5,128,128]{3,2,1,0:T(8,128)(2,1)} %k_ref.1), custom_call_target="tpu_custom_call" | custom-call | flops 1000 | bytes 1000 | tf_op jit(solution)/shard_map/halo/pallas_call | solution.py:95
  8.2 1.9 %collective-permute-start.3 = (bf16[3,12,128,128]{3,2,1,0:T(8,128)(2,1)}, bf16[3,12,128,128]{3,2,1,0:T(8,128)(2,1)S(1)}, u32[]{:S(2)}, u32[]{:S(2)}) collective-permute-start(bf16[3,12,128,128]{3,2,1,0:T(8,128)(2,1)} %get-tuple-element.42), channel_id=1, source_target_pairs={{1,64},{2,65},{3,66},{4,67},{5,68},{6,69},{7,70},{8,71},{9,72},{10... | collective-permute-start | bytes 3538952 | tf_op jit(solution)/shard_map/ppermute | solution.py:342
  10.1 2.0 %collective-permute-start.2 = (bf16[3,12,128,128]{3,2,1,0:T(8,128)(2,1)}, bf16[3,12,128,128]{3,2,1,0:T(8,128)(2,1)S(1)}, u32[]{:S(2)}, u32[]{:S(2)}) collective-permute-start(bf16[3,12,128,128]{3,2,1,0:T(8,128)(2,1)} %get-tuple-element.31), channel_id=1, source_target_pairs={{0,1},{1,2},{2,3},{3,4},{4,5},{5,6},{6,7},{7,8},{8,9},{9,10},{10,1... | collective-permute-start | bytes 3538952 | tf_op jit(solution)/shard_map/ppermute | solution.py:341
  12.1 0.0 copy-start
  12.2 1.1 copy-done
  13.2 0.0 copy-start.1
  13.2 1.0 copy-done.1
  14.3 9.0 %conv.2 = (bf16[2,3,5,128,128]{4,3,2,1,0:T(8,128)(2,1)S(1)}, bf16[2,3,5,128,128]{4,3,2,1,0:T(8,128)(2,1)S(1)}) custom-call(bf16[3,12,8,256,128]{4,3,2,1,0:T(8,128)(2,1)} %x_ref.3, bf16[1280,256]{1,0:T(8,128)(2,1)S(1)} %copy-done, bf16[896,256]{1,0:T(8,128)(2,1)S(1)} %copy-done.1), custom_call_target="tpu_custom_call" | custom-call | flops 1000 | bytes 1000 | tf_op jit(solution)/shard_map/conv/pallas_call | solution.py:169
  23.2 4.7 %collective-permute-start.1 = (bf16[2,3,5,128,128]{4,3,2,1,0:T(8,128)(2,1)S(1)}, bf16[2,3,5,128,128]{4,3,2,1,0:T(8,128)(2,1)S(1)}, u32[]{:S(2)}, u32[]{:S(2)}) collective-permute-start(bf16[2,3,5,128,128]{4,3,2,1,0:T(8,128)(2,1)S(1)} %get-tuple-element.39), channel_id=1, source_target_pairs={{0,64},{1,65},{2,66},{3,67},{4,68},{5,69},{6,70},{7,71},{8,72},{9,... | collective-permute-start | bytes 2949128 | tf_op jit(solution)/shard_map/ppermute | solution.py:350
  27.9 0.0 copy-start.2
  27.9 0.0 copy-start.3
  28.0 12.0 %conv.3 = (bf16[2,3,4,128,128]{4,3,2,1,0:T(8,128)(2,1)S(1)}, bf16[2,3,4,128,128]{4,3,2,1,0:T(8,128)(2,1)S(1)}, bf16[2,3,3,128,128]{4,3,2,1,0:T(8,128)(2,1)S(1)}, bf16[2,3,3,128,128]{4,3,2,1,0:T(8,128)(2,1)S(1)}) custom-call(bf16[3,12,8,256,128]{4,3,2,1,0:T(8,128)(2,1)} %x_ref.3, bf16[1280,256]{1,0:T(8,128)(2,1)S(1)} %copy-done, bf16[896,256]{1,0:T(8,128)(2,1)S(1)} %copy-done.1), custom_call_target="tpu_custom_call" | custom-call | flops 1000 | bytes 1000 | tf_op jit(solution)/shard_map/conv/pallas_call | solution.py:169
  40.0 0.1 collective-permute-start
  40.1 2.9 %collective-permute-start.8 = (bf16[2,3,3,128,128]{4,3,2,1,0:T(8,128)(2,1)S(1)}, bf16[2,3,3,128,128]{4,3,2,1,0:T(8,128)(2,1)S(1)}, u32[]{:S(2)}, u32[]{:S(2)}) collective-permute-start(bf16[2,3,3,128,128]{4,3,2,1,0:T(8,128)(2,1)S(1)} %get-tuple-element.51), channel_id=1, source_target_pairs={{0,64},{1,65},{2,66},{3,67},{4,68},{5,69},{6,70},{7,71},{8,72},{9,... | collective-permute-start | bytes 1769480 | tf_op jit(solution)/shard_map/ppermute | solution.py:350
  43.1 25.9 %collective-permute-done.1.oth_ref = bf16[2,3,5,128,128]{4,3,2,1,0:T(8,128)(2,1)S(1)} collective-permute-done((bf16[2,3,5,128,128]{4,3,2,1,0:T(8,128)(2,1)S(1)}, bf16[2,3,5,128,128]{4,3,2,1,0:T(8,128)(2,1)S(1)}, u32[]{:S(2)}, u32[]{:S(2)}) %collective-permute-start.1) | collective-permute-done | bytes 983072 | tf_op jit(solution)/shard_map/ppermute | solution.py:350
  68.9 0.0 collective-permute-done.3.h2_ref
  68.9 0.0 collective-permute-done.2.h1_ref
  68.9 0.0 copy-done.2
  68.9 0.0 copy-done.3
  68.9 0.0 copy-start.5
  69.0 1.5 %norm.3 = (bf16[2,3,5,128,128]{4,3,2,1,0:T(8,128)(2,1)S(1)}, bf16[3,5,128,128]{3,2,1,0:T(8,128)(2,1)S(1)}, bf16[3,5,128,128]{3,2,1,0:T(8,128)(2,1)S(1)}) custom-call(bf16[2,3,5,128,128]{4,3,2,1,0:T(8,128)(2,1)S(1)} %get-tuple-element.35.own_ref, bf16[2,3,5,128,128]{4,3,2,1,0:T(8,128)(2,1)S(1)} %collective-permute-done.1.oth_ref, ...), custom_call_target="tpu_custom_call" | custom-call | flops 1000 | bytes 1000 | tf_op jit(solution)/shard_map/norm/pallas_call | solution.py:212
  70.4 0.7 collective-permute-start.4
  71.1 0.1 collective-permute-start.5
  71.2 0.0 copy-done.5
  71.2 0.1 slice_bitcast_fusion
  71.3 0.0 copy-start.4
  71.3 0.1 fusion.2
  71.4 0.1 pad_maximum_fusion.refs_3_.refs_6_.refs_5_
  71.4 1.1 %collective-permute-done.4.refs_1_ = bf16[3,5,128,128]{3,2,1,0:T(8,128)(2,1)S(1)} collective-permute-done((bf16[3,5,128,128]{3,2,1,0:T(8,128)(2,1)S(1)}, bf16[3,5,128,128]{3,2,1,0:T(8,128)(2,1)S(1)}, u32[]{:S(2)}, u32[]{:S(2)}) %collective-permute-start.4) | collective-permute-done | bytes 491552 | tf_op jit(solution)/shard_map/ppermute | solution.py:361
  72.6 0.7 collective-permute-done.5.refs_2_
  73.3 0.0 copy-done.4
  73.3 9.0 %epi.3.refs_9_ = bf16[12,12,1,128,128]{4,3,2,1,0:T(8,128)(2,1)} custom-call(bf16[2,3,5,128,128]{4,3,2,1,0:T(8,128)(2,1)S(1)} %get-tuple-element.43.refs_0_, bf16[3,5,128,128]{3,2,1,0:T(8,128)(2,1)S(1)} %collective-permute-done.4.refs_1_, bf16[3,5,128,128]{3,2,1,0:T(8,128)(2,1)S(1)} %collective-permute-done.5.refs_2_, ...), custom_call_target="tpu_custom_call" | custom-call | flops 1000 | bytes 1000 | tf_op jit(solution)/shard_map/epi/pallas_call | solution.py:301
  82.3 3.5 %collective-permute-done.oth_ref = bf16[2,3,4,128,128]{4,3,2,1,0:T(8,128)(2,1)S(1)} collective-permute-done((bf16[2,3,4,128,128]{4,3,2,1,0:T(8,128)(2,1)S(1)}, bf16[2,3,4,128,128]{4,3,2,1,0:T(8,128)(2,1)S(1)}, u32[]{:S(2)}, u32[]{:S(2)}) %collective-permute-start) | collective-permute-done | bytes 786464 | tf_op jit(solution)/shard_map/ppermute | solution.py:350
  85.8 1.2 %norm.4 = (bf16[2,3,4,128,128]{4,3,2,1,0:T(8,128)(2,1)S(1)}, bf16[3,4,128,128]{3,2,1,0:T(8,128)(2,1)S(1)}, bf16[3,4,128,128]{3,2,1,0:T(8,128)(2,1)S(1)}) custom-call(bf16[2,3,4,128,128]{4,3,2,1,0:T(8,128)(2,1)S(1)} %get-tuple-element.37.own_ref, bf16[2,3,4,128,128]{4,3,2,1,0:T(8,128)(2,1)S(1)} %collective-permute-done.oth_ref, ...), custom_call_target="tpu_custom_call" | custom-call | flops 1000 | bytes 1000 | tf_op jit(solution)/shard_map/norm/pallas_call | solution.py:212
  87.0 0.7 collective-permute-start.6
  87.6 0.1 collective-permute-start.7
  87.7 1.3 %collective-permute-done.6.refs_4_.refs_1_ = bf16[3,4,128,128]{3,2,1,0:T(8,128)(2,1)S(1)} collective-permute-done((bf16[3,4,128,128]{3,2,1,0:T(8,128)(2,1)S(1)}, bf16[3,4,128,128]{3,2,1,0:T(8,128)(2,1)S(1)}, u32[]{:S(2)}, u32[]{:S(2)}) %collective-permute-start.6) | collective-permute-done | bytes 393248 | tf_op jit(solution)/shard_map/ppermute | solution.py:361
  89.0 0.6 collective-permute-done.7.refs_5_.refs_2_
  89.5 9.2 %epi.4.refs_8_ = bf16[12,12,1,128,128]{4,3,2,1,0:T(8,128)(2,1)} custom-call(bf16[2,3,5,128,128]{4,3,2,1,0:T(8,128)(2,1)S(1)} %get-tuple-element.43.refs_0_, bf16[3,5,128,128]{3,2,1,0:T(8,128)(2,1)S(1)} %collective-permute-done.4.refs_1_, bf16[3,5,128,128]{3,2,1,0:T(8,128)(2,1)S(1)} %collective-permute-done.5.refs_2_, ...), custom_call_target="tpu_custom_call", output_to_operand_aliasing={{}: (9, {})} | custom-call | flops 1000 | bytes 1000 | tf_op jit(solution)/shard_map/epi/pallas_call | solution.py:301
  98.7 0.0 collective-permute-done.8.oth_ref
  98.7 0.9 norm.5
  99.6 0.5 collective-permute-start.9
  100.1 1.6 %collective-permute-done.9.refs_4_ = bf16[2,3,3,128,128]{4,3,2,1,0:T(8,128)(2,1)S(1)} collective-permute-done((bf16[2,3,3,128,128]{4,3,2,1,0:T(8,128)(2,1)S(1)}, bf16[2,3,3,128,128]{4,3,2,1,0:T(8,128)(2,1)S(1)}, u32[]{:S(2)}, u32[]{:S(2)}) %collective-permute-start.9) | collective-permute-done | bytes 589856 | tf_op jit(solution)/shard_map/ppermute | solution.py:361
  101.7 9.1 %epi.5 = bf16[12,12,1,128,128]{4,3,2,1,0:T(8,128)(2,1)} custom-call(bf16[2,3,4,128,128]{4,3,2,1,0:T(8,128)(2,1)S(1)} %get-tuple-element.47.refs_3_.refs_0_, bf16[3,4,128,128]{3,2,1,0:T(8,128)(2,1)S(1)} %collective-permute-done.6.refs_4_.refs_1_, bf16[3,4,128,128]{3,2,1,0:T(8,128)(2,1)S(1)} %collective-permute-done.7.refs_5_.refs_2_, ...), custom_call_target="tpu_custom_call", output_to_operand_aliasing={{}: (8, {})} | custom-call | flops 1000 | bytes 1000 | tf_op jit(solution)/shard_map/epi/pallas_call | solution.py:301
Async XLA Ops:
  8.2 60.8 %collective-permute-start.3 = (bf16[3,12,128,128]{3,2,1,0:T(8,128)(2,1)}, bf16[3,12,128,128]{3,2,1,0:T(8,128)(2,1)S(1)}, u32[]{:S(2)}, u32[]{:S(2)}) collective-permute-start(bf16[3,12,128,128]{3,2,1,0:T(8,128)(2,1)} %get-tuple-element.42), channel_id=1, source_target_pairs={{1,64},{2,65},{3,66},{4,67},{5,68},{6,69},{7,70},{8,71},{9,72},{10... | collective-permute-start | bytes 3538952 | tf_op jit(solution)/shard_map/ppermute | solution.py:342
  10.1 58.8 %collective-permute-start.2 = (bf16[3,12,128,128]{3,2,1,0:T(8,128)(2,1)}, bf16[3,12,128,128]{3,2,1,0:T(8,128)(2,1)S(1)}, u32[]{:S(2)}, u32[]{:S(2)}) collective-permute-start(bf16[3,12,128,128]{3,2,1,0:T(8,128)(2,1)} %get-tuple-element.31), channel_id=1, source_target_pairs={{0,1},{1,2},{2,3},{3,4},{4,5},{5,6},{6,7},{7,8},{8,9},{9,10},{10,1... | collective-permute-start | bytes 3538952 | tf_op jit(solution)/shard_map/ppermute | solution.py:341
  12.1 1.1 copy-start
  13.2 1.0 copy-start.1
  23.2 45.7 %collective-permute-start.1 = (bf16[2,3,5,128,128]{4,3,2,1,0:T(8,128)(2,1)S(1)}, bf16[2,3,5,128,128]{4,3,2,1,0:T(8,128)(2,1)S(1)}, u32[]{:S(2)}, u32[]{:S(2)}) collective-permute-start(bf16[2,3,5,128,128]{4,3,2,1,0:T(8,128)(2,1)S(1)} %get-tuple-element.39), channel_id=1, source_target_pairs={{0,64},{1,65},{2,66},{3,67},{4,68},{5,69},{6,70},{7,71},{8,72},{9,... | collective-permute-start | bytes 2949128 | tf_op jit(solution)/shard_map/ppermute | solution.py:350
  27.9 41.0 %copy-start.2 = (f32[128,128]{1,0:T(8,128)S(1)}, f32[128,128]{1,0:T(8,128)}, u32[]{:S(2)}) copy-start(f32[128,128]{1,0:T(8,128)} %mix_ref.5) | copy-start | bytes 196612
  27.9 41.0 %copy-start.3 = (f32[128]{0:T(128)S(1)}, f32[128]{0:T(128)}, u32[]{:S(2)}) copy-start(f32[128]{0:T(128)} %param.8) | copy-start | bytes 1540
  40.0 45.8 %collective-permute-start = (bf16[2,3,4,128,128]{4,3,2,1,0:T(8,128)(2,1)S(1)}, bf16[2,3,4,128,128]{4,3,2,1,0:T(8,128)(2,1)S(1)}, u32[]{:S(2)}, u32[]{:S(2)}) collective-permute-start(bf16[2,3,4,128,128]{4,3,2,1,0:T(8,128)(2,1)S(1)} %get-tuple-element.38), channel_id=1, source_target_pairs={{0,64},{1,65},{2,66},{3,67},{4,68},{5,69},{6,70},{7,71},{8,72},{9,... | collective-permute-start | bytes 2359304 | tf_op jit(solution)/shard_map/ppermute | solution.py:350
  40.1 58.6 %collective-permute-start.8 = (bf16[2,3,3,128,128]{4,3,2,1,0:T(8,128)(2,1)S(1)}, bf16[2,3,3,128,128]{4,3,2,1,0:T(8,128)(2,1)S(1)}, u32[]{:S(2)}, u32[]{:S(2)}) collective-permute-start(bf16[2,3,3,128,128]{4,3,2,1,0:T(8,128)(2,1)S(1)} %get-tuple-element.51), channel_id=1, source_target_pairs={{0,64},{1,65},{2,66},{3,67},{4,68},{5,69},{6,70},{7,71},{8,72},{9,... | collective-permute-start | bytes 1769480 | tf_op jit(solution)/shard_map/ppermute | solution.py:350
  68.9 2.2 %copy-start.5 = (bf16[3,3,3,128,128]{4,3,2,1,0:T(8,128)(2,1)S(1)}, bf16[3,3,3,128,128]{4,3,2,1,0:T(8,128)(2,1)}, u32[]{:S(2)}) copy-start(bf16[3,3,3,128,128]{4,3,2,1,0:T(8,128)(2,1)} %param.10) | copy-start | bytes 2654212
  70.4 2.2 %collective-permute-start.4 = (bf16[3,5,128,128]{3,2,1,0:T(8,128)(2,1)S(1)}, bf16[3,5,128,128]{3,2,1,0:T(8,128)(2,1)S(1)}, u32[]{:S(2)}, u32[]{:S(2)}) collective-permute-start(bf16[3,5,128,128]{3,2,1,0:T(8,128)(2,1)S(1)} %get-tuple-element.44), channel_id=1, source_target_pairs={{0,32},{32,0},{64,96},{96,64},{1,33},{33,1},{65,97},{97,65},{2,34}... | collective-permute-start | bytes 1474568 | tf_op jit(solution)/shard_map/ppermute | solution.py:361
  71.1 2.2 %collective-permute-start.5 = (bf16[3,5,128,128]{3,2,1,0:T(8,128)(2,1)S(1)}, bf16[3,5,128,128]{3,2,1,0:T(8,128)(2,1)S(1)}, u32[]{:S(2)}, u32[]{:S(2)}) collective-permute-start(bf16[3,5,128,128]{3,2,1,0:T(8,128)(2,1)S(1)} %get-tuple-element.45), channel_id=1, source_target_pairs={{0,32},{32,0},{64,96},{96,64},{1,33},{33,1},{65,97},{97,65},{2,34}... | collective-permute-start | bytes 1474568 | tf_op jit(solution)/shard_map/ppermute | solution.py:361
  71.3 2.0 %copy-start.4 = (f32[128]{0:T(128)S(1)}, f32[128]{0:T(128)}, u32[]{:S(2)}) copy-start(f32[128]{0:T(128)} %param.11) | copy-start | bytes 1540
  87.0 2.0 %collective-permute-start.6 = (bf16[3,4,128,128]{3,2,1,0:T(8,128)(2,1)S(1)}, bf16[3,4,128,128]{3,2,1,0:T(8,128)(2,1)S(1)}, u32[]{:S(2)}, u32[]{:S(2)}) collective-permute-start(bf16[3,4,128,128]{3,2,1,0:T(8,128)(2,1)S(1)} %get-tuple-element.48), channel_id=1, source_target_pairs={{0,32},{32,0},{64,96},{96,64},{1,33},{33,1},{65,97},{97,65},{2,34}... | collective-permute-start | bytes 1179656 | tf_op jit(solution)/shard_map/ppermute | solution.py:361
  87.6 1.9 %collective-permute-start.7 = (bf16[3,4,128,128]{3,2,1,0:T(8,128)(2,1)S(1)}, bf16[3,4,128,128]{3,2,1,0:T(8,128)(2,1)S(1)}, u32[]{:S(2)}, u32[]{:S(2)}) collective-permute-start(bf16[3,4,128,128]{3,2,1,0:T(8,128)(2,1)S(1)} %get-tuple-element.49), channel_id=1, source_target_pairs={{0,32},{32,0},{64,96},{96,64},{1,33},{33,1},{65,97},{97,65},{2,34}... | collective-permute-start | bytes 1179656 | tf_op jit(solution)/shard_map/ppermute | solution.py:361
  99.6 2.1 %collective-permute-start.9 = (bf16[2,3,3,128,128]{4,3,2,1,0:T(8,128)(2,1)S(1)}, bf16[2,3,3,128,128]{4,3,2,1,0:T(8,128)(2,1)S(1)}, u32[]{:S(2)}, u32[]{:S(2)}) collective-permute-start(bf16[2,3,3,128,128]{4,3,2,1,0:T(8,128)(2,1)S(1)} %get-tuple-element.55), channel_id=1, source_target_pairs={{0,32},{32,0},{64,96},{96,64},{1,33},{33,1},{65,97},{97,65},{2,34}... | collective-permute-start | bytes 1769480 | tf_op jit(solution)/shard_map/ppermute | solution.py:361
